TPU v7x, 32 devices: a whole 2x2x4 slice. The times are simulated.
32 devices in a mesh: groups: 2 (over x), dp: 16 (over z, y, core).
Axes of the slice: x: 2, y: 2, z: 4, core: 2. Of those that a mesh axis runs over, the one named last changes fastest.
Arguments:
- embeddings: bfloat16 [262144, 1024], P(('groups', 'dp')), parts along dimension 0
- cluster_ids: int32 [262144], P(('groups', 'dp')), parts along dimension 0, may hold values from 0 to 15, as said below
- owner_table: int32 [32], P('groups'), parts along dimension 0, may hold values from 0 to 15, each once
- start_basis: float32 [8, 1024], replicated, may hold values from -6 to 6
Outputs:
- directions: float32 [32, 8, 1024], P(('groups', 'dp')), parts along dimension 0
- projections: float32 [8, 262144], P(None, ('groups', 'dp')), parts along dimension 1
There are 2 independent parts, one for each index of `groups`. A program takes and returns all parts, laid end to end along the dimension named above; an argument that names none is the same for every part. Nothing has to cross between parts.
Inputs may be any that keep to these rules, and one draw needn't show every extreme that they name: `cluster_ids`: Sorted. Each cluster's rows form a run whose length is a multiple of 2048, from 2048 to 32768; every cluster has rows and one has exactly 32768. The rows of one device belong to at most 4 clusters, and some device's rows belong to exactly 4. A permutation: index k of dp owns cluster owner_table[k].
All inputs are finite; a program needn't handle non-finite values.
Results may differ from a plain program's by a relative error of at most 0.0075.
Values sent between devices are 32-bit elements; how exact they have to be, the bound alone decides.
No kernel may reach another device: no remote copies, remote signals or barrier semaphores. Data moves between devices by JAX's collectives and lax.ppermute only.
A program may use at most 128 MiB of HBM per device.

v0:
```python
import jax
import jax.numpy as jnp
from jax import lax
from jax.sharding import PartitionSpec as P

DIRS = 8
SEGS = 4
ITERS = 6


def chol_rows(images):
    gram_matrix = jnp.einsum("bid,bjd->bij", images, images, precision=lax.Precision.HIGHEST)
    lower_factor = jnp.linalg.cholesky(gram_matrix)
    return jax.scipy.linalg.solve_triangular(lower_factor, images, lower=True)


def per_device(embeddings, cluster_ids, owner_table, start_basis):
    row_count, feature_count = embeddings.shape
    cluster_count = owner_table.shape[0]
    slot_index = jnp.arange(SEGS, dtype=jnp.int32)
    first_label = cluster_ids[0]
    labels = first_label + slot_index
    member_mask = cluster_ids[None, :] == labels[:, None]
    member = member_mask.astype(jnp.float32)
    counts_local = jnp.sum(member, axis=1)
    all_labels = jnp.arange(cluster_count, dtype=jnp.int32)
    select = (all_labels[None, :] == labels[:, None]).astype(jnp.float32)
    owner_select = (owner_table[None, :] == labels[:, None]).astype(jnp.float32)
    partial_sums = jnp.dot(
        member_mask.astype(jnp.bfloat16), embeddings, preferred_element_type=jnp.float32
    )
    spread_sums = jnp.dot(select.T, partial_sums, precision=lax.Precision.HIGHEST)
    spread_counts = jnp.dot(counts_local, select, precision=lax.Precision.HIGHEST)
    total_sums, total_counts = lax.psum((spread_sums, spread_counts), "dp")
    cluster_means = total_sums / total_counts[:, None]
    seg_means = jnp.dot(select, cluster_means, precision=lax.Precision.HIGHEST)
    row_means = jnp.einsum("jr,jd->rd", member, seg_means, precision=lax.Precision.HIGHEST)
    centered = (embeddings.astype(jnp.float32) - row_means).astype(jnp.bfloat16)

    def masked_scores(basis_seg):
        narrow = basis_seg.astype(jnp.bfloat16).reshape(SEGS * DIRS, feature_count)
        scores = lax.dot_general(
            narrow, centered, (((1,), (1,)), ((), ())), preferred_element_type=jnp.float32
        )
        return scores.reshape(SEGS, DIRS, row_count) * member[:, None, :]

    basis_seg = jnp.broadcast_to(start_basis, (SEGS, DIRS, feature_count))
    for iteration in range(ITERS):
        image_scores = masked_scores(basis_seg).astype(jnp.bfloat16).reshape(SEGS * DIRS, row_count)
        images = jnp.dot(image_scores, centered, preferred_element_type=jnp.float32)
        images = images.reshape(SEGS, DIRS, feature_count)
        spread_out = jnp.einsum(
            "jk,jid->kid", owner_select, images, precision=lax.Precision.HIGHEST
        )
        owned_image = lax.psum_scatter(spread_out, "dp", scatter_dimension=0, tiled=True)
        owned_basis = chol_rows(owned_image)
        gathered = lax.all_gather(owned_basis, "dp", axis=0, tiled=True)
        basis_seg = jnp.einsum(
            "jk,kid->jid", owner_select, gathered, precision=lax.Precision.HIGHEST
        )
    projections = jnp.sum(masked_scores(basis_seg), axis=0)
    return (owned_basis, projections)


def solution(mesh):
    in_specs = (P(("groups", "dp"), None), P(("groups", "dp")), P("groups"), P())
    out_specs = (P(("groups", "dp"), None, None), P(None, ("groups", "dp")))
    return jax.shard_map(
        per_device, mesh=mesh, in_specs=in_specs, out_specs=out_specs, check_vma=False
    )
```

profile of v0, /device:TPU:0, one launch (start us, length us, event | category | flops | bytes accessed | tf_op | source)
XLA Modules:
  0.0 743.2 jit_solution(12154255851934739533)
XLA Ops:
  7.2 1.2 slice.11
  9.1 8.1 %fusion.93 = f32[4,1024]{1,0:T(4,128)S(1)} fusion(bf16[8192,1024]{1,0:T(8,128)(2,1)} %param.7, s32[8192]{0:T(1024)} %param.8, s32[4]{0:T(128)S(1)} %iota_add_fusion), kind=kOutput, calls=%fused_computation.75 | convolution fusion | flops 67141632 | bytes 16826384 | tf_op jit(solution)/shard_map/dot_general | solution.py:29
  18.7 34.9 %psum.15 = f32[16]{0:T(128)S(1)} all-reduce(f32[16]{0:T(128)S(1)} %convolution_bitcast_fusion.13), channel_id=1, replica_groups=mesh['groups'=2,'dp'=16] {'dp'}, use_global_device_ids=true, to_apply=%region_2.0 | all-reduce | flops 16 | bytes 128 | tf_op jit(solution)/shard_map/psum | solution.py:34
  53.7 51.8 %all-reduce.2.cloned.1.call-done = f32[16,1024]{1,0:T(8,128)} async-done(((f32[16,1024]{1,0:T(8,128)}), f32[16,1024]{1,0:T(8,128)}) %all-reduce.2.cloned.1.call-update) | async-done | bytes 65552 | tf_op jit(solution)/shard_map/psum | solution.py:34
  105.4 1.0 fusion.111
  106.5 19.0 %subtract_convert_fusion = bf16[8192,1024]{1,0:T(8,128)(2,1)} fusion(bf16[8192,1024]{1,0:T(8,128)(2,1)} %param.7, f32[4,1024]{1,0:T(4,128)S(1)} %fusion.111, s32[8192]{0:T(1024)S(1)} %copy-done, s32[4]{0:T(128)S(1)} %iota_add_fusion), kind=kOutput, calls=%fused_computation | convolution fusion | flops 427851776 | bytes 33603600 | tf_op jit(solution)/shard_map/jr,jd->rd/dot_general | solution.py:37
  125.5 18.0 %fusion.22 = f32[4,8,1024]{2,1,0:T(8,128)S(1)} fusion(bf16[8192,1024]{1,0:T(8,128)(2,1)} %subtract_convert_fusion, f32[4,8192]{1,0:T(4,128)S(1)} %compare_convert_fusion, bf16[8,1024]{1,0:T(8,128)(2,1)S(1)} %convert_element_type.60), kind=kOutput, calls=%fused_computation.23 | convolution fusion | flops 1074266112 | bytes 17055744 | tf_op jit(solution)/shard_map/dot_general | solution.py:50
  144.1 1.1 copy.18
  145.3 57.5 %reduce-scatter.7.cloned.1.call-done = f32[1,8,1024]{2,1,0:T(8,128)} async-done(((f32[16,8,1024]{2,1,0:T(8,128)}), f32[1,8,1024]{2,1,0:T(8,128)}) %reduce-scatter.7.cloned.1.call-update) | async-done | bytes 32784 | tf_op jit(solution)/shard_map/reduce_scatter | solution.py:55
  207.5 21.0 %all_gather.18 = f32[16,8,1024]{2,1,0:T(8,128)S(1)} all-gather(f32[1,8,1024]{2,1,0:T(8,128)S(1)} %convolution_bitcast_fusion.6), channel_id=1, replica_groups=mesh['groups'=2,'dp'=16] {'dp'}, dimensions={0}, use_global_device_ids=true | all-gather | bytes 557056 | tf_op jit(solution)/shard_map/all_gather | solution.py:57
  229.1 17.9 %fusion.18 = f32[4,8,1024]{2,1,0:T(8,128)S(1)} fusion(bf16[8192,1024]{1,0:T(8,128)(2,1)} %subtract_convert_fusion, f32[4,8192]{1,0:T(4,128)S(1)} %compare_convert_fusion, bf16[4,8,1024]{2,0,1:T(4,128)(2,1)S(1)} %fusion.84), kind=kOutput, calls=%fused_computation.19 | convolution fusion | flops 1074266112 | bytes 17104896 | tf_op jit(solution)/shard_map/dot_general | solution.py:50
  247.6 1.1 copy.21
  248.7 53.1 %reduce-scatter.9.cloned.1.call-done = f32[1,8,1024]{2,1,0:T(8,128)} async-done(((f32[16,8,1024]{2,1,0:T(8,128)}), f32[1,8,1024]{2,1,0:T(8,128)}) %reduce-scatter.9.cloned.1.call-update) | async-done | bytes 32784 | tf_op jit(solution)/shard_map/reduce_scatter | solution.py:55
  305.7 1.0 convolution_bitcast_fusion.5
  306.6 20.8 %all_gather.19 = f32[16,8,1024]{2,1,0:T(8,128)S(1)} all-gather(f32[1,8,1024]{2,1,0:T(8,128)S(1)} %convolution_bitcast_fusion.5), channel_id=1, replica_groups=mesh['groups'=2,'dp'=16] {'dp'}, dimensions={0}, use_global_device_ids=true | all-gather | bytes 557056 | tf_op jit(solution)/shard_map/all_gather | solution.py:57
  328.1 17.9 %fusion.14 = f32[4,8,1024]{2,1,0:T(8,128)S(1)} fusion(bf16[8192,1024]{1,0:T(8,128)(2,1)} %subtract_convert_fusion, f32[4,8192]{1,0:T(4,128)S(1)} %compare_convert_fusion, bf16[4,8,1024]{2,0,1:T(4,128)(2,1)S(1)} %fusion.82), kind=kOutput, calls=%fused_computation.15 | convolution fusion | flops 1074266112 | bytes 17104896 | tf_op jit(solution)/shard_map/dot_general | solution.py:50
  346.5 1.1 copy.24
  347.7 53.2 %reduce-scatter.11.cloned.1.call-done = f32[1,8,1024]{2,1,0:T(8,128)} async-done(((f32[16,8,1024]{2,1,0:T(8,128)}), f32[1,8,1024]{2,1,0:T(8,128)}) %reduce-scatter.11.cloned.1.call-update) | async-done | bytes 32784 | tf_op jit(solution)/shard_map/reduce_scatter | solution.py:55
  405.6 21.1 %all_gather.20 = f32[16,8,1024]{2,1,0:T(8,128)S(1)} all-gather(f32[1,8,1024]{2,1,0:T(8,128)S(1)} %convolution_bitcast_fusion.4), channel_id=1, replica_groups=mesh['groups'=2,'dp'=16] {'dp'}, dimensions={0}, use_global_device_ids=true | all-gather | bytes 557056 | tf_op jit(solution)/shard_map/all_gather | solution.py:57
  427.3 17.9 %fusion.10 = f32[4,8,1024]{2,1,0:T(8,128)S(1)} fusion(bf16[8192,1024]{1,0:T(8,128)(2,1)} %subtract_convert_fusion, f32[4,8192]{1,0:T(4,128)S(1)} %compare_convert_fusion, bf16[4,8,1024]{2,0,1:T(4,128)(2,1)S(1)} %fusion.80), kind=kOutput, calls=%fused_computation.11 | convolution fusion | flops 1074266112 | bytes 17104896 | tf_op jit(solution)/shard_map/dot_general | solution.py:50
  445.7 1.1 copy.27
  446.9 53.1 %reduce-scatter.13.cloned.1.call-done = f32[1,8,1024]{2,1,0:T(8,128)} async-done(((f32[16,8,1024]{2,1,0:T(8,128)}), f32[1,8,1024]{2,1,0:T(8,128)}) %reduce-scatter.13.cloned.1.call-update) | async-done | bytes 32784 | tf_op jit(solution)/shard_map/reduce_scatter | solution.py:55
  504.8 20.9 %all_gather.21 = f32[16,8,1024]{2,1,0:T(8,128)S(1)} all-gather(f32[1,8,1024]{2,1,0:T(8,128)S(1)} %convolution_bitcast_fusion.3), channel_id=1, replica_groups=mesh['groups'=2,'dp'=16] {'dp'}, dimensions={0}, use_global_device_ids=true | all-gather | bytes 557056 | tf_op jit(solution)/shard_map/all_gather | solution.py:57
  526.2 17.9 %fusion.6 = f32[4,8,1024]{2,1,0:T(8,128)S(1)} fusion(bf16[8192,1024]{1,0:T(8,128)(2,1)} %subtract_convert_fusion, f32[4,8192]{1,0:T(4,128)S(1)} %compare_convert_fusion, bf16[4,8,1024]{2,0,1:T(4,128)(2,1)S(1)} %fusion.78), kind=kOutput, calls=%fused_computation.7 | convolution fusion | flops 1074266112 | bytes 17104896 | tf_op jit(solution)/shard_map/dot_general | solution.py:50
  544.7 1.1 copy.30
  545.9 53.2 %reduce-scatter.15.cloned.1.call-done = f32[1,8,1024]{2,1,0:T(8,128)} async-done(((f32[16,8,1024]{2,1,0:T(8,128)}), f32[1,8,1024]{2,1,0:T(8,128)}) %reduce-scatter.15.cloned.1.call-update) | async-done | bytes 32784 | tf_op jit(solution)/shard_map/reduce_scatter | solution.py:55
  603.8 21.1 %all_gather.22 = f32[16,8,1024]{2,1,0:T(8,128)S(1)} all-gather(f32[1,8,1024]{2,1,0:T(8,128)S(1)} %convolution_bitcast_fusion.2), channel_id=1, replica_groups=mesh['groups'=2,'dp'=16] {'dp'}, dimensions={0}, use_global_device_ids=true | all-gather | bytes 557056 | tf_op jit(solution)/shard_map/all_gather | solution.py:57
  625.5 17.9 %fusion.2 = f32[4,8,1024]{2,1,0:T(8,128)S(1)} fusion(bf16[8192,1024]{1,0:T(8,128)(2,1)} %subtract_convert_fusion, f32[4,8192]{1,0:T(4,128)S(1)} %compare_convert_fusion, bf16[4,8,1024]{2,0,1:T(4,128)(2,1)S(1)} %fusion.76), kind=kOutput, calls=%fused_computation.3 | convolution fusion | flops 1074266112 | bytes 17104896 | tf_op jit(solution)/shard_map/dot_general | solution.py:50
  643.9 1.1 copy.33
  645.1 53.2 %reduce-scatter.17.cloned.1.call-done = f32[1,8,1024]{2,1,0:T(8,128)} async-done(((f32[16,8,1024]{2,1,0:T(8,128)}), f32[1,8,1024]{2,1,0:T(8,128)}) %reduce-scatter.17.cloned.1.call-update) | async-done | bytes 32784 | tf_op jit(solution)/shard_map/reduce_scatter | solution.py:55
  703.0 20.9 %all_gather.23 = f32[16,8,1024]{2,1,0:T(8,128)S(1)} all-gather(f32[1,8,1024]{2,1,0:T(8,128)S(1)} %convolution_bitcast_fusion.1), channel_id=1, replica_groups=mesh['groups'=2,'dp'=16] {'dp'}, dimensions={0}, use_global_device_ids=true | all-gather | bytes 557056 | tf_op jit(solution)/shard_map/all_gather | solution.py:57
  724.5 11.4 %fusion.70 = f32[8,8192]{1,0:T(8,128)} fusion(bf16[8192,1024]{1,0:T(8,128)(2,1)} %subtract_convert_fusion, f32[4,8192]{1,0:T(4,128)S(1)} %compare_convert_fusion, bf16[4,8,1024]{2,0,1:T(4,128)(2,1)S(1)} %fusion.74), kind=kOutput, calls=%fused_computation.40 | convolution fusion | flops 537329664 | bytes 17235968 | tf_op jit(solution)/shard_map/dot_general | solution.py:42
  (93 shorter events, 36.7 us)
Async XLA Ops:
  7.2 11.0 %copy-start = (s32[8192]{0:T(1024)S(1)}, s32[8192]{0:T(1024)}, u32[]{:S(2)}) copy-start(s32[8192]{0:T(1024)} %param.8) | copy-start | bytes 98308
  7.2 46.5 %copy-start.3 = (f32[8,1024]{1,0:T(8,128)S(1)}, f32[8,1024]{1,0:T(8,128)}, u32[]{:S(2)}) copy-start(f32[8,1024]{1,0:T(8,128)} %param.10) | copy-start | bytes 98308
  7.2 98.3 %all-reduce.2.cloned.1.call-start = ((), (), s32[]{:S(2)}) async-start(), calls=%async_computation.6 | async-start | bytes 131072 | tf_op jit(solution)/shard_map/psum | solution.py:34
  18.1 184.6 %reduce-scatter.7.cloned.1.call-start = ((), (), s32[]{:S(2)}) async-start(), calls=%async_computation.7 | async-start | bytes 557056 | tf_op jit(solution)/shard_map/reduce_scatter | solution.py:55
  125.5 18.0 %copy-start.2 = (s32[16]{0:T(128)S(1)}, s32[16]{0:T(128)}, u32[]{:S(2)}) copy-start(s32[16]{0:T(128)} %param.9) | copy-start | bytes 196
  145.2 156.7 %reduce-scatter.9.cloned.1.call-start = ((), (), s32[]{:S(2)}) async-start(), calls=%async_computation.8 | async-start | bytes 557056 | tf_op jit(solution)/shard_map/reduce_scatter | solution.py:55
  248.7 152.2 %reduce-scatter.11.cloned.1.call-start = ((), (), s32[]{:S(2)}) async-start(), calls=%async_computation.9 | async-start | bytes 557056 | tf_op jit(solution)/shard_map/reduce_scatter | solution.py:55
  347.6 152.4 %reduce-scatter.13.cloned.1.call-start = ((), (), s32[]{:S(2)}) async-start(), calls=%async_computation.10 | async-start | bytes 557056 | tf_op jit(solution)/shard_map/reduce_scatter | solution.py:55
  446.8 152.2 %reduce-scatter.15.cloned.1.call-start = ((), (), s32[]{:S(2)}) async-start(), calls=%async_computation.11 | async-start | bytes 557056 | tf_op jit(solution)/shard_map/reduce_scatter | solution.py:55
  545.8 152.4 %reduce-scatter.17.cloned.1.call-start = ((), (), s32[]{:S(2)}) async-start(), calls=%async_computation.12 | async-start | bytes 557056 | tf_op jit(solution)/shard_map/reduce_scatter | solution.py:55
  703.0 32.9 %copy-start.1 = (f32[1,8,1024]{2,1,0:T(8,128)}, f32[1,8,1024]{2,1,0:T(8,128)S(1)}, u32[]{:S(2)}) copy-start(f32[1,8,1024]{2,1,0:T(8,128)S(1)} %convolution_bitcast_fusion.1) | copy-start | bytes 98308
Sparse Core Ops, SparseCore 0:
  18.3 87.1 all-reduce.1
  145.3 57.3 reduce-scatter.6
  248.8 53.0 reduce-scatter.8
  347.8 53.0 reduce-scatter.10
  447.0 53.0 reduce-scatter.12
  545.9 53.0 reduce-scatter.14
  645.2 53.0 reduce-scatter.16
where the time goes:
time: 752 us; the launch traced here: 743 us
  waiting for transfers between devices  375 us (50%)
  matrix products  167 us (22%)
  blocking collectives  161 us (21%)
  other arithmetic  17.2 us (2%)
  between operations  14.9 us (2%)
  local copies, waits for them, and re-layouts  8.25 us (1%)
    reduce_scatter x6, waiting for transfers between devices, per_device(): lax.psum_scatter(spread_out, 'dp', scatter_dimension=0, tiled=True)  323 us
    all_gather x6, blocking collectives, per_device(): gathered = lax.all_gather(owned_basis, 'dp', axis=0, tiled=True)  126 us
    dot_general x6, matrix products, per_device(): images = jnp.dot(image_scores, centered, preferred_element_type=jnp.float32)  108 us
    psum x1, waiting for transfers between devices, per_device(): total_sums, total_counts = lax.psum((spread_sums, spread_counts), 'dp')  51.8 us
    psum x1, blocking collectives, per_device(): total_sums, total_counts = lax.psum((spread_sums, spread_counts), 'dp')  34.9 us
    dot_general x1, matrix products, per_device(): jnp.einsum('jr,jd->rd', member, seg_means, precision=lax.Precision.HIGHEST)  19 us
  transfers between devices with their start and end apart: 7, of which 7 were waited for; matrix products, arithmetic and copies ran while one was open for 0% of the time, Pallas kernels for 0%

commit v1 on v0

v1 whole, which is shorter than its diff:
```python
import functools

import jax
import jax.numpy as jnp
from jax import lax
from jax.experimental import pallas as pl
from jax.experimental.pallas import tpu as pltpu
from jax.sharding import PartitionSpec as P

DIRS = 8
ITERS = 6
UNIT = 2048
HIGHEST = lax.Precision.HIGHEST
VMEM_LIMIT = 56 * 1024 * 1024


def dot(a, b, contract=((1,), (0,)), precision=None):
    return lax.dot_general(
        a, b, (contract, ((), ())), precision=precision, preferred_element_type=jnp.float32
    )


def means_kernel(x_ref, out_ref):
    out_ref[0] = jnp.sum(x_ref[...].astype(jnp.float32), axis=0, keepdims=True) / UNIT


def unit_means(x):
    rows, width = x.shape
    return pl.pallas_call(
        means_kernel,
        grid=(rows // UNIT,),
        in_specs=[pl.BlockSpec((UNIT, width), lambda u: (u, 0))],
        out_specs=pl.BlockSpec((1, 1, width), lambda u: (u, 0, 0)),
        out_shape=jax.ShapeDtypeStruct((rows // UNIT, 1, width), jnp.float32),
        compiler_params=pltpu.CompilerParams(vmem_limit_bytes=VMEM_LIMIT),
        name="unit_means",
    )(x)


def apply_unit(narrow, high, low):
    return dot(narrow, high) + dot(narrow, low)


def spread_kernel(x_ref, mean_ref, start_ref, high_ref, low_ref, image_ref):
    centered = (x_ref[...].astype(jnp.float32) - mean_ref[0]).astype(jnp.bfloat16)
    spread = dot(centered, centered, ((0,), (0,)))
    high = spread.astype(jnp.bfloat16)
    high_ref[0] = high
    low = (spread - high.astype(jnp.float32)).astype(jnp.bfloat16)
    low_ref[0] = low
    image_ref[0] = apply_unit(start_ref[...].astype(jnp.bfloat16), high, low)


def unit_spread(x, means, start):
    rows, width = x.shape
    units = rows // UNIT
    half = jax.ShapeDtypeStruct((units, width, width), jnp.bfloat16)
    square = pl.BlockSpec((1, width, width), lambda u: (u, 0, 0))
    return pl.pallas_call(
        spread_kernel,
        grid=(units,),
        in_specs=[
            pl.BlockSpec((UNIT, width), lambda u: (u, 0)),
            pl.BlockSpec((1, 1, width), lambda u: (u, 0, 0)),
            pl.BlockSpec((DIRS, width), lambda u: (0, 0)),
        ],
        out_specs=[square, square, pl.BlockSpec((1, DIRS, width), lambda u: (u, 0, 0))],
        out_shape=[half, half, jax.ShapeDtypeStruct((units, DIRS, width), jnp.float32)],
        compiler_params=pltpu.CompilerParams(vmem_limit_bytes=VMEM_LIMIT),
        name="unit_spread",
    )(x, means, start)


def merge_units(images, narrow, shift, same_ref, out_ref):
    units = len(images)
    full = []
    for u in range(units):
        along = jnp.sum(narrow[u].astype(jnp.float32) * shift[u], axis=1, keepdims=True)
        full.append(images[u] + (UNIT * along) * shift[u])
    for u in range(units):
        total = full[u]
        for v in range(units):
            if v != u:
                total = total + full[v] * same_ref[u, v]
        out_ref[u] = total


def first_kernel(same_ref, weight_ref, all_means_ref, means_ref, start_ref, image_ref, out_ref, shift_ref):
    units = means_ref.shape[0]
    cluster_means = dot(weight_ref[...], all_means_ref[...], precision=HIGHEST)
    narrow = start_ref[...].astype(jnp.bfloat16)
    shift = [means_ref[u] - cluster_means[u : u + 1] for u in range(units)]
    for u in range(units):
        shift_ref[u] = shift[u]
    merge_units([image_ref[u] for u in range(units)], [narrow] * units, shift, same_ref, out_ref)


def vmem(count):
    return [pl.BlockSpec(memory_space=pltpu.VMEM)] * count


def smem(count):
    return [pl.BlockSpec(memory_space=pltpu.SMEM)] * count


def first_images(same, weight, all_means, means, start, images):
    units, _, width = means.shape
    return pl.pallas_call(
        first_kernel,
        in_specs=smem(1) + vmem(5),
        out_specs=vmem(2),
        out_shape=[
            jax.ShapeDtypeStruct((units, DIRS, width), jnp.float32),
            jax.ShapeDtypeStruct((units, 1, width), jnp.float32),
        ],
        compiler_params=pltpu.CompilerParams(vmem_limit_bytes=VMEM_LIMIT),
        name="first_images",
    )(same, weight, all_means, means, start, images)


def orthonormal(side_ref, image_ref, first_ref, last_ref):
    units = image_ref.shape[0]
    size = units * DIRS
    first, last = first_ref[...], last_ref[...]
    images = jnp.concatenate(
        [image_ref[u] + first * side_ref[0, u] + last * side_ref[1, u] for u in range(units)], axis=0
    )
    gram = dot(images, images, ((1,), (1,)), HIGHEST)
    row = lax.broadcasted_iota(jnp.int32, (DIRS, size), 0)
    lane = lax.broadcasted_iota(jnp.int32, (DIRS, size), 1)
    inverse = []
    for u in range(units):
        left = gram[u * DIRS : (u + 1) * DIRS]
        right = (lane == row + u * DIRS).astype(jnp.float32)
        for k in range(DIRS - 1):
            c = u * DIRS + k
            factor = jnp.where(row[:, :1] > k, left[:, c : c + 1] / left[k : k + 1, c : c + 1], 0.0)
            right = right - factor * right[k : k + 1]
            left = left - factor * left[k : k + 1]
        diagonal = jnp.sum(jnp.where(lane == row + u * DIRS, left, 0.0), axis=1, keepdims=True)
        inverse.append(right / jnp.sqrt(diagonal))
    return dot(jnp.concatenate(inverse, axis=0), images, precision=HIGHEST)


def step_kernel(same_ref, side_ref, image_ref, first_ref, last_ref, shift_ref, high_ref, low_ref, out_ref):
    units = image_ref.shape[0]
    basis = orthonormal(side_ref, image_ref, first_ref, last_ref).astype(jnp.bfloat16)
    narrow = [basis[u * DIRS : (u + 1) * DIRS] for u in range(units)]
    images = [apply_unit(narrow[u], high_ref[u], low_ref[u]) for u in range(units)]
    merge_units(images, narrow, [shift_ref[u] for u in range(units)], same_ref, out_ref)


def step(same, side, images, first, last, shift, high, low):
    return pl.pallas_call(
        step_kernel,
        in_specs=smem(2) + vmem(6),
        out_specs=vmem(1)[0],
        out_shape=jax.ShapeDtypeStruct(images.shape, jnp.float32),
        compiler_params=pltpu.CompilerParams(vmem_limit_bytes=VMEM_LIMIT),
        name="step",
    )(same, side, images, first, last, shift, high, low)


def last_kernel(side_ref, image_ref, first_ref, last_ref, mean_ref, shift_ref, x_ref, basis_ref, out_ref, narrow):
    units = image_ref.shape[0]
    u = pl.program_id(0)

    @pl.when(u == 0)
    def _():
        basis = orthonormal(side_ref, image_ref, first_ref, last_ref)
        for v in range(units):
            basis_ref[v] = basis[v * DIRS : (v + 1) * DIRS]
            narrow[v] = basis[v * DIRS : (v + 1) * DIRS].astype(jnp.bfloat16)

    chosen = narrow[u]
    cluster_mean = mean_ref[u] - shift_ref[u]
    offset = jnp.sum(chosen.astype(jnp.float32) * cluster_mean, axis=1, keepdims=True)
    out_ref[...] = dot(chosen, x_ref[...], ((1,), (1,))) - offset


def last(side, images, first, last_image, means, shift, x):
    rows, width = x.shape
    units = rows // UNIT
    whole = pl.BlockSpec((units, DIRS, width), lambda u: (0, 0, 0))
    one = pl.BlockSpec((DIRS, width), lambda u: (0, 0))
    line = pl.BlockSpec((units, 1, width), lambda u: (0, 0, 0))
    return pl.pallas_call(
        last_kernel,
        grid=(units,),
        in_specs=smem(1) + [whole, one, one, line, line, pl.BlockSpec((UNIT, width), lambda u: (u, 0))],
        out_specs=[whole, pl.BlockSpec((DIRS, UNIT), lambda u: (0, u))],
        out_shape=[
            jax.ShapeDtypeStruct((units, DIRS, width), jnp.float32),
            jax.ShapeDtypeStruct((DIRS, rows), jnp.float32),
        ],
        scratch_shapes=[pltpu.VMEM((units, DIRS, width), jnp.bfloat16)],
        compiler_params=pltpu.CompilerParams(vmem_limit_bytes=VMEM_LIMIT),
        name="last",
    )(side, images, first, last_image, means, shift, x)


def per_device(n_dp, embeddings, cluster_ids, owner_table, start_basis):
    rows, width = embeddings.shape
    units = rows // UNIT
    chips = n_dp // 2
    me = lax.axis_index("dp")
    chip, core = me // 2, me % 2
    labels = cluster_ids.reshape(units, UNIT)[:, 0]

    means = unit_means(embeddings)
    stats = jnp.concatenate(
        [
            means.reshape(units, width),
            jnp.broadcast_to(labels.astype(jnp.float32)[:, None], (units, width)),
        ]
    )
    high, low, raw = unit_spread(embeddings, means, start_basis)
    stats = lax.all_gather(stats, "dp").reshape(n_dp, 2, units, width)
    all_means = stats[:, 0].reshape(n_dp * units, width)
    all_labels = stats[:, 1, :, 0].astype(jnp.int32)

    match = (labels[:, None] == all_labels.reshape(1, -1)).astype(jnp.float32)
    weight = match / jnp.sum(match, axis=1, keepdims=True)
    same = (labels[:, None] == labels[None, :]).astype(jnp.float32)
    side = jnp.stack([labels == labels[0], labels == labels[-1]]).astype(jnp.float32)

    heads, tails = all_labels[:, 0], all_labels[:, -1]
    head, tail = heads[me], tails[me]
    chip_head, chip_tail = heads[2 * chip], tails[2 * chip + 1]
    mate = me ^ 1

    def flag(value):
        return value.astype(jnp.float32)

    even = core == 0
    join_head = flag(heads[2 * chip + 1] == chip_head)
    join_tail = flag(tails[2 * chip] == chip_tail)
    mate_left = flag((core == 1) & (tails[mate] == head))
    mate_right = flag((core == 0) & (heads[mate] == tail))
    chip_own_head = flag(head == chip_head)
    chip_own_tail = flag(tail == chip_tail)

    near = (lambda p: p ^ 1, lambda p: (p + 1) % chips if p % 2 else (p - 1) % chips)
    far = (lambda p: p ^ 2, lambda p: (p + 2) % chips if p % 4 >= 2 else (p - 2) % chips)
    links = []
    for pairing in (near, far):
        targets = [2 * pairing[c](p) + c for p in range(chips) for c in range(2)]
        other = jnp.asarray([t // 2 for t in targets], jnp.int32)[me]
        up = other > chip
        from_left = flag(~up & (tails[2 * other + 1] == chip_head))
        from_right = flag(up & (heads[2 * other] == chip_tail))
        links.append((list(enumerate(targets)), up, from_left, from_right))
    mates = [(i, i ^ 1) for i in range(n_dp)]

    def swap(a, b):
        both = lax.ppermute(jnp.concatenate([a, b]), "dp", mates)
        return both[:DIRS], both[DIRS:]

    def exchange(images):
        own_head, own_tail = images[0], images[-1]
        mate_head, mate_tail = swap(own_head, own_tail)
        total_head = jnp.where(even, own_head + join_head * mate_head, mate_head + join_head * own_head)
        total_tail = jnp.where(even, mate_tail + join_tail * own_tail, own_tail + join_tail * mate_tail)
        left = right = jnp.zeros_like(own_head)
        for permutation, up, from_left, from_right in links:
            got = lax.ppermute(jnp.where(up, total_tail, total_head), "dp", permutation)
            left = left + from_left * got
            right = right + from_right * got
        mate_side = swap(left, right)
        first = chip_own_head * (left + mate_side[0]) + mate_left * mate_tail
        last_image = chip_own_tail * (right + mate_side[1]) + mate_right * mate_head
        return first, last_image

    images, shift = first_images(same, weight, all_means, means, start_basis, raw)
    for _ in range(ITERS - 1):
        images = step(same, side, images, *exchange(images), shift, high, low)
    basis, projections = last(side, images, *exchange(images), means, shift, embeddings)

    flat = all_labels.reshape(-1)
    starts = jnp.concatenate([jnp.ones((1,), bool), flat[1:] != flat[:-1]]).reshape(n_dp, units)[me]
    pick = (owner_table[:, None] == labels[None, :]) & starts[None, :]
    outgoing = jnp.einsum("ku,uid->kid", pick.astype(jnp.float32), basis, precision=HIGHEST)
    arrived = lax.all_to_all(outgoing, "dp", 0, 0, tiled=True)
    return jnp.sum(arrived, axis=0, keepdims=True), projections


def solution(mesh):
    in_specs = (P(("groups", "dp"), None), P(("groups", "dp")), P("groups"), P())
    out_specs = (P(("groups", "dp"), None, None), P(None, ("groups", "dp")))
    body = functools.partial(per_device, mesh.shape["dp"])
    return jax.shard_map(body, mesh=mesh, in_specs=in_specs, out_specs=out_specs, check_vma=False)
```

time: 752 us -> 229 us (0.30)
  waiting for transfers between devices: 375 us -> 26.2 us
  matrix products: 167 us -> 1.42 us
  blocking collectives: 161 us -> 42 us
  Pallas kernels: 0 us -> 95.6 us
  starting transfers between devices: 0.29 us -> 21.6 us
    reduce_scatter x6 -> x0, waiting for transfers between devices: 323 us -> none  [per_device(): lax.psum_scatter(spread_out, 'dp', scatter_dimension=0, tiled=True)]
    dot_general x30 -> x1, matrix products: 161 us -> 1.42 us  [per_device(): jnp.einsum('ku,uid->kid', pick.astype(jnp.float32), basis, precision=HIGH...]
    all_gather x6 -> x1, blocking collectives: 126 us -> 24.6 us  [per_device(): stats = lax.all_gather(stats, 'dp').reshape(n_dp, 2, units, width)]
    pallas_call x0 -> x9, Pallas kernels: none -> 95.6 us  [the longest x5 50.6 us: step(): pl.pallas_call(step_kernel, in_specs=smem(2) + vmem(6), out_specs=vmem(1)...]
    psum x1 -> x0, waiting for transfers between devices: 51.8 us -> none  [per_device(): total_sums, total_counts = lax.psum((spread_sums, spread_counts), 'dp')]
    psum x1 -> x0, blocking collectives: 34.9 us -> none  [per_device(): total_sums, total_counts = lax.psum((spread_sums, spread_counts), 'dp')]
    ppermute x0 -> x24, waiting for transfers between devices: none -> 26.2 us  [the longest x12 16.9 us: exchange(): got = lax.ppermute(jnp.where(up, total_tail, total_head), 'dp', permutation)]
    ppermute x0 -> x24, starting transfers between devices: none -> 21.6 us  [the longest x12 16.3 us: swap(): both = lax.ppermute(jnp.concatenate([a, b]), 'dp', mates)]
  transfers between devices with their start and end apart: 7 -> 24, of which waited for: 7 -> 21; matrix products, arithmetic and copies ran while one was open for 0% -> 2% of each run, Pallas kernels for 0% -> 0%
where the time goes in v1:
time: 229 us; the launch traced here: 227 us
  Pallas kernels  95.6 us (42%)
  blocking collectives  42 us (18%)
  waiting for transfers between devices  26.2 us (11%)
  starting transfers between devices  21.6 us (9%)
  between operations  16.6 us (7%)
  other arithmetic  13.2 us (6%)
  local copies, waits for them, and re-layouts  10.4 us (5%)
    pallas_call x5, Pallas kernels, step(): pl.pallas_call(step_kernel, in_specs=smem(2) + vmem(6), out_specs=vmem(1)...  50.6 us
    all_gather x1, blocking collectives, per_device(): stats = lax.all_gather(stats, 'dp').reshape(n_dp, 2, units, width)  24.6 us
    pallas_call x1, Pallas kernels, unit_spread(): pl.pallas_call(spread_kernel, grid=(units,), in_specs=[pl.BlockSpec((UNIT...  24.5 us
    all_to_all x1, blocking collectives, per_device(): arrived = lax.all_to_all(outgoing, 'dp', 0, 0, tiled=True)  17.5 us
    ppermute x12, waiting for transfers between devices, exchange(): got = lax.ppermute(jnp.where(up, total_tail, total_head), 'dp', permutation)  16.9 us
    ppermute x12, starting transfers between devices, swap(): both = lax.ppermute(jnp.concatenate([a, b]), 'dp', mates)  16.3 us
    pallas_call x1, Pallas kernels, last(): pl.pallas_call(last_kernel, grid=(units,), in_specs=smem(1) + [whole, one...  10.3 us
    ppermute x12, waiting for transfers between devices, swap(): both = lax.ppermute(jnp.concatenate([a, b]), 'dp', mates)  9.24 us
  transfers between devices with their start and end apart: 24, of which 21 were waited for; matrix products, arithmetic and copies ran while one was open for 2% of the time, Pallas kernels for 0%

profile of v1, /device:TPU:0, one launch (start us, length us, event | category | flops | bytes accessed | tf_op | source)
XLA Modules:
  0.0 227.1 jit_solution(8469092423052024255)
XLA Ops:
  1.6 8.1 %unit_means.1.mean_ref.means_ref = f32[4,1,1024]{2,1,0:T(1,128)} custom-call(bf16[8192,1024]{1,0:T(8,128)(2,1)} %x_ref.5), custom_call_target="tpu_custom_call" | custom-call | tf_op jit(solution)/shard_map/unit_means/pallas_call | solution.py:29
  10.6 24.6 %all-gather = f32[128,1024]{1,0:T(8,128)S(1)} all-gather(f32[8,1024]{1,0:T(8,128)S(1)} %pad_maximum_fusion.12), channel_id=2, replica_groups=mesh['groups'=2,'dp'=16] {'dp'}, dimensions={0}, use_global_device_ids=true | all-gather | bytes 557056 | tf_op jit(solution)/shard_map/all_gather | solution.py:218
  38.0 24.5 %unit_spread.1 = (bf16[4,1024,1024]{2,1,0:T(8,128)(2,1)}, bf16[4,1024,1024]{2,1,0:T(8,128)(2,1)}, f32[4,8,1024]{2,1,0:T(8,128)}) custom-call(bf16[8192,1024]{1,0:T(8,128)(2,1)} %x_ref.5, f32[4,1,1024]{2,1,0:T(1,128)} %unit_means.1.mean_ref.means_ref, f32[8,1024]{1,0:T(8,128)} %start_ref.3), custom_call_target="tpu_custom_call" | custom-call | tf_op jit(solution)/shard_map/unit_spread/pallas_call | solution.py:59
  62.5 2.1 first_images.1
  74.5 1.4 compare_reduce_fusion.1
  88.5 10.1 %step.5.image_ref = f32[4,8,1024]{2,1,0:T(8,128)} custom-call(f32[4,4]{1,0:T(4,128)} %compare_convert_fusion.same_ref, f32[2,4]{1,0:T(2,128)} %add_convert_fusion.side_ref, f32[4,8,1024]{2,1,0:T(8,128)} %get-tuple-element.10.image_ref, f32[8,1024]{1,0:T(8,128)} %get-tuple-element.51.first_ref, f32[8,1024]{1,0:T(8,128)} %get-tuple-element.50.last_ref, ...), custom_call_target="tpu_custom_call" | custom-call | tf_op jit(solution)/shard_map/step/pallas_call | solution.py:154
  99.8 0.9 collective-permute-done.4
  101.5 1.8 collective-permute-start.6
  103.3 2.0 collective-permute-start.5
  105.5 1.8 collective-permute-done.5
  107.3 3.0 %collective-permute-start.7 = (f32[16,1024]{1,0:T(8,128)S(1)}, f32[16,1024]{1,0:T(8,128)S(1)}, u32[]{:S(2)}, u32[]{:S(2)}) collective-permute-start(f32[16,1024]{1,0:T(8,128)S(1)} %pad_maximum_fusion.3), channel_id=1, source_target_pairs={{0,1},{1,0},{2,3},{3,2},{4,5},{5,4},{6,7},{7,6},{8,9},{9,8},{10,11... | collective-permute-start | bytes 196616 | tf_op jit(solution)/shard_map/ppermute | solution.py:256
  110.3 0.9 collective-permute-done.7
  111.8 10.1 %step.6.image_ref = f32[4,8,1024]{2,1,0:T(8,128)} custom-call(f32[4,4]{1,0:T(4,128)} %compare_convert_fusion.same_ref, f32[2,4]{1,0:T(2,128)} %add_convert_fusion.side_ref, f32[4,8,1024]{2,1,0:T(8,128)} %step.5.image_ref, f32[8,1024]{1,0:T(8,128)} %get-tuple-element.47.first_ref, f32[8,1024]{1,0:T(8,128)} %get-tuple-element.46.last_ref, ...), custom_call_target="tpu_custom_call" | custom-call | tf_op jit(solution)/shard_map/step/pallas_call | solution.py:154
  123.1 0.9 collective-permute-done.8
  125.4 3.4 %collective-permute-done.10 = f32[8,1024]{1,0:T(8,128)S(1)} collective-permute-done((f32[8,1024]{1,0:T(8,128)S(1)}, f32[8,1024]{1,0:T(8,128)S(1)}, u32[]{:S(2)}, u32[]{:S(2)}) %collective-permute-start.10) | collective-permute-done | bytes 32800 | tf_op jit(solution)/shard_map/ppermute | solution.py:266
  128.9 2.0 collective-permute-start.11
  130.8 0.9 collective-permute-done.11
  132.4 10.1 %step.7.image_ref = f32[4,8,1024]{2,1,0:T(8,128)} custom-call(f32[4,4]{1,0:T(4,128)} %compare_convert_fusion.same_ref, f32[2,4]{1,0:T(2,128)} %add_convert_fusion.side_ref, f32[4,8,1024]{2,1,0:T(8,128)} %step.6.image_ref, f32[8,1024]{1,0:T(8,128)} %get-tuple-element.43.first_ref, f32[8,1024]{1,0:T(8,128)} %get-tuple-element.42.last_ref, ...), custom_call_target="tpu_custom_call" | custom-call | tf_op jit(solution)/shard_map/step/pallas_call | solution.py:154
  143.7 0.9 collective-permute-done.12
  145.8 3.5 %collective-permute-done.14 = f32[8,1024]{1,0:T(8,128)S(1)} collective-permute-done((f32[8,1024]{1,0:T(8,128)S(1)}, f32[8,1024]{1,0:T(8,128)S(1)}, u32[]{:S(2)}, u32[]{:S(2)}) %collective-permute-start.14) | collective-permute-done | bytes 32800 | tf_op jit(solution)/shard_map/ppermute | solution.py:266
  149.8 3.0 %collective-permute-start.15 = (f32[16,1024]{1,0:T(8,128)S(1)}, f32[16,1024]{1,0:T(8,128)S(1)}, u32[]{:S(2)}, u32[]{:S(2)}) collective-permute-start(f32[16,1024]{1,0:T(8,128)S(1)} %pad_maximum_fusion.7), channel_id=1, source_target_pairs={{0,1},{1,0},{2,3},{3,2},{4,5},{5,4},{6,7},{7,6},{8,9},{9,8},{10,11... | collective-permute-start | bytes 196616 | tf_op jit(solution)/shard_map/ppermute | solution.py:256
  152.7 0.9 collective-permute-done.15
  154.2 10.3 %step.8.image_ref = f32[4,8,1024]{2,1,0:T(8,128)} custom-call(f32[4,4]{1,0:T(4,128)} %compare_convert_fusion.same_ref, f32[2,4]{1,0:T(2,128)} %add_convert_fusion.side_ref, f32[4,8,1024]{2,1,0:T(8,128)} %step.7.image_ref, f32[8,1024]{1,0:T(8,128)} %get-tuple-element.39.first_ref, f32[8,1024]{1,0:T(8,128)} %get-tuple-element.38.last_ref, ...), custom_call_target="tpu_custom_call" | custom-call | tf_op jit(solution)/shard_map/step/pallas_call | solution.py:154
  165.7 0.9 collective-permute-done.16
  167.6 3.8 %collective-permute-done.18 = f32[8,1024]{1,0:T(8,128)S(1)} collective-permute-done((f32[8,1024]{1,0:T(8,128)S(1)}, f32[8,1024]{1,0:T(8,128)S(1)}, u32[]{:S(2)}, u32[]{:S(2)}) %collective-permute-start.18) | collective-permute-done | bytes 32800 | tf_op jit(solution)/shard_map/ppermute | solution.py:266
  171.5 2.3 %collective-permute-start.19 = (f32[16,1024]{1,0:T(8,128)S(1)}, f32[16,1024]{1,0:T(8,128)S(1)}, u32[]{:S(2)}, u32[]{:S(2)}) collective-permute-start(f32[16,1024]{1,0:T(8,128)S(1)} %pad_maximum_fusion.9), channel_id=1, source_target_pairs={{0,1},{1,0},{2,3},{3,2},{4,5},{5,4},{6,7},{7,6},{8,9},{9,8},{10,11... | collective-permute-start | bytes 196616 | tf_op jit(solution)/shard_map/ppermute | solution.py:256
  175.4 10.1 %step.9.image_ref = f32[4,8,1024]{2,1,0:T(8,128)} custom-call(f32[4,4]{1,0:T(4,128)} %compare_convert_fusion.same_ref, f32[2,4]{1,0:T(2,128)} %add_convert_fusion.side_ref, f32[4,8,1024]{2,1,0:T(8,128)} %step.8.image_ref, f32[8,1024]{1,0:T(8,128)} %get-tuple-element.35.first_ref, f32[8,1024]{1,0:T(8,128)} %get-tuple-element.34.last_ref, ...), custom_call_target="tpu_custom_call" | custom-call | tf_op jit(solution)/shard_map/step/pallas_call | solution.py:154
  188.7 3.6 %collective-permute-done.22 = f32[8,1024]{1,0:T(8,128)S(1)} collective-permute-done((f32[8,1024]{1,0:T(8,128)S(1)}, f32[8,1024]{1,0:T(8,128)S(1)}, u32[]{:S(2)}, u32[]{:S(2)}) %collective-permute-start.22) | collective-permute-done | bytes 32800 | tf_op jit(solution)/shard_map/ppermute | solution.py:266
  192.5 2.9 %collective-permute-start.23 = (f32[16,1024]{1,0:T(8,128)S(1)}, f32[16,1024]{1,0:T(8,128)S(1)}, u32[]{:S(2)}, u32[]{:S(2)}) collective-permute-start(f32[16,1024]{1,0:T(8,128)S(1)} %pad_maximum_fusion.11), channel_id=1, source_target_pairs={{0,1},{1,0},{2,3},{3,2},{4,5},{5,4},{6,7},{7,6},{8,9},{9,8},{10,11... | collective-permute-start | bytes 196616 | tf_op jit(solution)/shard_map/ppermute | solution.py:256
  196.9 10.3 %last.1 = (f32[4,8,1024]{2,1,0:T(8,128)}, f32[8,8192]{1,0:T(8,128)}) custom-call(f32[2,4]{1,0:T(2,128)} %add_convert_fusion.side_ref, f32[4,8,1024]{2,1,0:T(8,128)} %step.9.image_ref, f32[8,1024]{1,0:T(8,128)} %get-tuple-element.31.first_ref, f32[8,1024]{1,0:T(8,128)} %get-tuple-element.30.last_ref, f32[4,1,1024]{2,1,0:T(1,128)} %unit_means.1.mean_ref.means_ref, ...), custom_call_target="tpu_custom_call" | custom-call | tf_op jit(solution)/shard_map/last/pallas_call | solution.py:187
  207.2 1.4 fusion
  209.0 17.5 %all_to_all.5 = f32[16,8,1024]{2,1,0:T(8,128)S(1)} all-to-all(f32[16,8,1024]{2,1,0:T(8,128)S(1)} %copy.24), channel_id=1, replica_groups=mesh['groups'=2,'dp'=16] {'dp'}, dimensions={0} | all-to-all | bytes 1048576 | tf_op jit(solution)/shard_map/all_to_all | solution.py:283
  (100 shorter events, 30.5 us)
Async XLA Ops:
  38.0 27.8 %copy-start.2 = (s32[16]{0:T(128)S(1)}, s32[16]{0:T(128)}, u32[]{:S(2)}) copy-start(s32[16]{0:T(128)} %constant.57.clone) | copy-start | bytes 196
  38.0 29.0 %copy-start.1 = (s32[16]{0:T(128)S(1)}, s32[16]{0:T(128)}, u32[]{:S(2)}) copy-start(s32[16]{0:T(128)} %constant.56.clone) | copy-start | bytes 196
  65.4 8.2 %collective-permute-start = (f32[16,1024]{1,0:T(8,128)S(1)}, f32[16,1024]{1,0:T(8,128)S(1)}, u32[]{:S(2)}, u32[]{:S(2)}) collective-permute-start(f32[16,1024]{1,0:T(8,128)S(1)} %pad_maximum_fusion), channel_id=1, source_target_pairs={{0,1},{1,0},{2,3},{3,2},{4,5},{5,4},{6,7},{7,6},{8,9},{9,8},{10,11... | collective-permute-start | bytes 196616 | tf_op jit(solution)/shard_map/ppermute | solution.py:256
  74.4 11.9 %collective-permute-start.2 = (f32[8,1024]{1,0:T(8,128)S(1)}, f32[8,1024]{1,0:T(8,128)S(1)}, u32[]{:S(2)}, u32[]{:S(2)}) collective-permute-start(f32[8,1024]{1,0:T(8,128)S(1)} %get-tuple-element.29), channel_id=1, source_target_pairs={{0,4},{1,13},{2,6},{3,15},{4,0},{5,9},{6,2},{7,11},{8,12},{9,5},{1... | collective-permute-start | bytes 98312 | tf_op jit(solution)/shard_map/ppermute | solution.py:266
  74.5 11.9 %collective-permute-start.1 = (f32[8,1024]{1,0:T(8,128)S(1)}, f32[8,1024]{1,0:T(8,128)S(1)}, u32[]{:S(2)}, u32[]{:S(2)}) collective-permute-start(f32[8,1024]{1,0:T(8,128)S(1)} %get-tuple-element.28), channel_id=1, source_target_pairs={{0,2},{1,15},{2,0},{3,5},{4,6},{5,3},{6,4},{7,9},{8,10},{9,7},{10,... | collective-permute-start | bytes 98312 | tf_op jit(solution)/shard_map/ppermute | solution.py:266
  86.4 1.5 collective-permute-start.3
  99.4 1.3 collective-permute-start.4
  101.5 4.0 %collective-permute-start.6 = (f32[8,1024]{1,0:T(8,128)S(1)}, f32[8,1024]{1,0:T(8,128)S(1)}, u32[]{:S(2)}, u32[]{:S(2)}) collective-permute-start(f32[8,1024]{1,0:T(8,128)S(1)} %get-tuple-element.27), channel_id=1, source_target_pairs={{0,4},{1,13},{2,6},{3,15},{4,0},{5,9},{6,2},{7,11},{8,12},{9,5},{1... | collective-permute-start | bytes 98312 | tf_op jit(solution)/shard_map/ppermute | solution.py:266
  103.3 3.9 %collective-permute-start.5 = (f32[8,1024]{1,0:T(8,128)S(1)}, f32[8,1024]{1,0:T(8,128)S(1)}, u32[]{:S(2)}, u32[]{:S(2)}) collective-permute-start(f32[8,1024]{1,0:T(8,128)S(1)} %get-tuple-element.26), channel_id=1, source_target_pairs={{0,2},{1,15},{2,0},{3,5},{4,6},{5,3},{6,4},{7,9},{8,10},{9,7},{10,... | collective-permute-start | bytes 98312 | tf_op jit(solution)/shard_map/ppermute | solution.py:266
  107.3 3.9 %collective-permute-start.7 = (f32[16,1024]{1,0:T(8,128)S(1)}, f32[16,1024]{1,0:T(8,128)S(1)}, u32[]{:S(2)}, u32[]{:S(2)}) collective-permute-start(f32[16,1024]{1,0:T(8,128)S(1)} %pad_maximum_fusion.3), channel_id=1, source_target_pairs={{0,1},{1,0},{2,3},{3,2},{4,5},{5,4},{6,7},{7,6},{8,9},{9,8},{10,11... | collective-permute-start | bytes 196616 | tf_op jit(solution)/shard_map/ppermute | solution.py:256
  122.7 1.3 collective-permute-start.8
  124.8 4.0 %collective-permute-start.10 = (f32[8,1024]{1,0:T(8,128)S(1)}, f32[8,1024]{1,0:T(8,128)S(1)}, u32[]{:S(2)}, u32[]{:S(2)}) collective-permute-start(f32[8,1024]{1,0:T(8,128)S(1)} %get-tuple-element.25), channel_id=1, source_target_pairs={{0,4},{1,13},{2,6},{3,15},{4,0},{5,9},{6,2},{7,11},{8,12},{9,5},{1... | collective-permute-start | bytes 98312 | tf_op jit(solution)/shard_map/ppermute | solution.py:266
  124.9 4.0 %collective-permute-start.9 = (f32[8,1024]{1,0:T(8,128)S(1)}, f32[8,1024]{1,0:T(8,128)S(1)}, u32[]{:S(2)}, u32[]{:S(2)}) collective-permute-start(f32[8,1024]{1,0:T(8,128)S(1)} %get-tuple-element.24), channel_id=1, source_target_pairs={{0,2},{1,15},{2,0},{3,5},{4,6},{5,3},{6,4},{7,9},{8,10},{9,7},{10,... | collective-permute-start | bytes 98312 | tf_op jit(solution)/shard_map/ppermute | solution.py:266
  128.9 2.9 %collective-permute-start.11 = (f32[16,1024]{1,0:T(8,128)S(1)}, f32[16,1024]{1,0:T(8,128)S(1)}, u32[]{:S(2)}, u32[]{:S(2)}) collective-permute-start(f32[16,1024]{1,0:T(8,128)S(1)} %pad_maximum_fusion.5), channel_id=1, source_target_pairs={{0,1},{1,0},{2,3},{3,2},{4,5},{5,4},{6,7},{7,6},{8,9},{9,8},{10,11... | collective-permute-start | bytes 196616 | tf_op jit(solution)/shard_map/ppermute | solution.py:256
  143.2 1.3 collective-permute-start.12
  145.4 4.0 %collective-permute-start.14 = (f32[8,1024]{1,0:T(8,128)S(1)}, f32[8,1024]{1,0:T(8,128)S(1)}, u32[]{:S(2)}, u32[]{:S(2)}) collective-permute-start(f32[8,1024]{1,0:T(8,128)S(1)} %get-tuple-element.23), channel_id=1, source_target_pairs={{0,4},{1,13},{2,6},{3,15},{4,0},{5,9},{6,2},{7,11},{8,12},{9,5},{1... | collective-permute-start | bytes 98312 | tf_op jit(solution)/shard_map/ppermute | solution.py:266
  145.8 3.9 %collective-permute-start.13 = (f32[8,1024]{1,0:T(8,128)S(1)}, f32[8,1024]{1,0:T(8,128)S(1)}, u32[]{:S(2)}, u32[]{:S(2)}) collective-permute-start(f32[8,1024]{1,0:T(8,128)S(1)} %get-tuple-element.22), channel_id=1, source_target_pairs={{0,2},{1,15},{2,0},{3,5},{4,6},{5,3},{6,4},{7,9},{8,10},{9,7},{10,... | collective-permute-start | bytes 98312 | tf_op jit(solution)/shard_map/ppermute | solution.py:266
  149.8 3.9 %collective-permute-start.15 = (f32[16,1024]{1,0:T(8,128)S(1)}, f32[16,1024]{1,0:T(8,128)S(1)}, u32[]{:S(2)}, u32[]{:S(2)}) collective-permute-start(f32[16,1024]{1,0:T(8,128)S(1)} %pad_maximum_fusion.7), channel_id=1, source_target_pairs={{0,1},{1,0},{2,3},{3,2},{4,5},{5,4},{6,7},{7,6},{8,9},{9,8},{10,11... | collective-permute-start | bytes 196616 | tf_op jit(solution)/shard_map/ppermute | solution.py:256
  165.3 1.3 collective-permute-start.16
  167.4 4.0 %collective-permute-start.18 = (f32[8,1024]{1,0:T(8,128)S(1)}, f32[8,1024]{1,0:T(8,128)S(1)}, u32[]{:S(2)}, u32[]{:S(2)}) collective-permute-start(f32[8,1024]{1,0:T(8,128)S(1)} %get-tuple-element.21), channel_id=1, source_target_pairs={{0,4},{1,13},{2,6},{3,15},{4,0},{5,9},{6,2},{7,11},{8,12},{9,5},{1... | collective-permute-start | bytes 98312 | tf_op jit(solution)/shard_map/ppermute | solution.py:266
  167.5 4.0 %collective-permute-start.17 = (f32[8,1024]{1,0:T(8,128)S(1)}, f32[8,1024]{1,0:T(8,128)S(1)}, u32[]{:S(2)}, u32[]{:S(2)}) collective-permute-start(f32[8,1024]{1,0:T(8,128)S(1)} %get-tuple-element.20), channel_id=1, source_target_pairs={{0,2},{1,15},{2,0},{3,5},{4,6},{5,3},{6,4},{7,9},{8,10},{9,7},{10,... | collective-permute-start | bytes 98312 | tf_op jit(solution)/shard_map/ppermute | solution.py:266
  171.5 3.2 %collective-permute-start.19 = (f32[16,1024]{1,0:T(8,128)S(1)}, f32[16,1024]{1,0:T(8,128)S(1)}, u32[]{:S(2)}, u32[]{:S(2)}) collective-permute-start(f32[16,1024]{1,0:T(8,128)S(1)} %pad_maximum_fusion.9), channel_id=1, source_target_pairs={{0,1},{1,0},{2,3},{3,2},{4,5},{5,4},{6,7},{7,6},{8,9},{9,8},{10,11... | collective-permute-start | bytes 196616 | tf_op jit(solution)/shard_map/ppermute | solution.py:256
  186.3 1.3 collective-permute-start.20
  188.4 4.0 %collective-permute-start.22 = (f32[8,1024]{1,0:T(8,128)S(1)}, f32[8,1024]{1,0:T(8,128)S(1)}, u32[]{:S(2)}, u32[]{:S(2)}) collective-permute-start(f32[8,1024]{1,0:T(8,128)S(1)} %get-tuple-element.19), channel_id=1, source_target_pairs={{0,4},{1,13},{2,6},{3,15},{4,0},{5,9},{6,2},{7,11},{8,12},{9,5},{1... | collective-permute-start | bytes 98312 | tf_op jit(solution)/shard_map/ppermute | solution.py:266
  188.5 3.9 %collective-permute-start.21 = (f32[8,1024]{1,0:T(8,128)S(1)}, f32[8,1024]{1,0:T(8,128)S(1)}, u32[]{:S(2)}, u32[]{:S(2)}) collective-permute-start(f32[8,1024]{1,0:T(8,128)S(1)} %get-tuple-element.18), channel_id=1, source_target_pairs={{0,2},{1,15},{2,0},{3,5},{4,6},{5,3},{6,4},{7,9},{8,10},{9,7},{10,... | collective-permute-start | bytes 98312 | tf_op jit(solution)/shard_map/ppermute | solution.py:266
  192.5 3.8 %collective-permute-start.23 = (f32[16,1024]{1,0:T(8,128)S(1)}, f32[16,1024]{1,0:T(8,128)S(1)}, u32[]{:S(2)}, u32[]{:S(2)}) collective-permute-start(f32[16,1024]{1,0:T(8,128)S(1)} %pad_maximum_fusion.11), channel_id=1, source_target_pairs={{0,1},{1,0},{2,3},{3,2},{4,5},{5,4},{6,7},{7,6},{8,9},{9,8},{10,11... | collective-permute-start | bytes 196616 | tf_op jit(solution)/shard_map/ppermute | solution.py:256
  196.9 10.3 %copy-start = (s32[16]{0:T(128)S(1)}, s32[16]{0:T(128)}, u32[]{:S(2)}) copy-start(s32[16]{0:T(128)} %param.8) | copy-start | bytes 196

commit v2 on v1

v2 whole, which is shorter than its diff:
```python
import functools

import jax
import jax.numpy as jnp
from jax import lax
from jax.experimental import pallas as pl
from jax.experimental.pallas import tpu as pltpu
from jax.sharding import PartitionSpec as P

DIRS = 8
ITERS = 6
UNIT = 2048
HIGHEST = lax.Precision.HIGHEST
MIB = 1024 * 1024


def dot(a, b, contract=((1,), (0,)), precision=None):
    return lax.dot_general(
        a, b, (contract, ((), ())), precision=precision, preferred_element_type=jnp.float32
    )


def means_kernel(parts, x_ref, out_ref):
    part = jnp.sum(x_ref[...].astype(jnp.float32), axis=0, keepdims=True) * (1 / UNIT)

    @pl.when(pl.program_id(1) == 0)
    def _():
        out_ref[0] = part

    @pl.when(pl.program_id(1) > 0)
    def _():
        out_ref[0] += part


def unit_means(x, parts=4):
    rows, width = x.shape
    return pl.pallas_call(
        functools.partial(means_kernel, parts),
        grid=(rows // UNIT, parts),
        in_specs=[pl.BlockSpec((UNIT // parts, width), lambda u, p: (u * parts + p, 0))],
        out_specs=pl.BlockSpec((1, 1, width), lambda u, p: (u, 0, 0)),
        out_shape=jax.ShapeDtypeStruct((rows // UNIT, 1, width), jnp.float32),
        compiler_params=pltpu.CompilerParams(vmem_limit_bytes=8 * MIB),
        name="unit_means",
    )(x)


def apply_unit(narrow, high, low):
    return dot(narrow, high) + dot(narrow, low)


def spread_kernel(x_ref, mean_ref, start_ref, high_ref, low_ref, image_ref):
    u = pl.program_id(0)
    centered = (x_ref[...].astype(jnp.float32) - mean_ref[0]).astype(jnp.bfloat16)
    spread = dot(centered, centered, ((0,), (0,)))
    high = spread.astype(jnp.bfloat16)
    high_ref[u] = high
    low = (spread - high.astype(jnp.float32)).astype(jnp.bfloat16)
    low_ref[u] = low
    image_ref[u] = apply_unit(start_ref[...].astype(jnp.bfloat16), high, low)


def unit_spread(x, means, start):
    rows, width = x.shape
    units = rows // UNIT
    half = pltpu.VMEM((units, width, width), jnp.bfloat16)
    return pl.pallas_call(
        spread_kernel,
        grid=(units,),
        in_specs=[
            pl.BlockSpec((UNIT, width), lambda u: (u, 0)),
            pl.BlockSpec((1, 1, width), lambda u: (u, 0, 0)),
            pl.BlockSpec((DIRS, width), lambda u: (0, 0)),
        ],
        out_specs=vmem(3),
        out_shape=[half, half, pltpu.VMEM((units, DIRS, width), jnp.float32)],
        compiler_params=pltpu.CompilerParams(vmem_limit_bytes=28 * MIB),
        name="unit_spread",
    )(x, means, start)


def flags(label_ref):
    units = label_ref.shape[0]
    same = [
        [jnp.where(label_ref[u] == label_ref[v], 1.0, 0.0) for v in range(units)] for u in range(units)
    ]
    return same, [same[u][0] for u in range(units)], [same[u][units - 1] for u in range(units)]


def merge_units(images, narrow, shift, same, out_ref, ends_ref):
    units = len(images)
    full = []
    for u in range(units):
        along = jnp.sum(narrow[u].astype(jnp.float32) * shift[u], axis=1, keepdims=True)
        full.append(images[u] + (UNIT * along) * shift[u])
    for u in range(units):
        total = full[u]
        for v in range(units):
            if v != u:
                total = total + full[v] * same[u][v]
        out_ref[u] = total
        if u == 0:
            ends_ref[:DIRS] = total
        if u == units - 1:
            ends_ref[DIRS:] = total


def first_kernel(label_ref, first_ref, last_ref, means_ref, start_ref, image_ref, out_ref, ends_ref, shift_ref):
    units = means_ref.shape[0]
    same, at_first, at_last = flags(label_ref)
    narrow = start_ref[...].astype(jnp.bfloat16)
    shift = []
    for u in range(units):
        total = first_ref[0:1] * at_first[u] + last_ref[0:1] * at_last[u]
        count = first_ref[1:2] * at_first[u] + last_ref[1:2] * at_last[u]
        for v in range(units):
            total = total + means_ref[v] * same[u][v]
            count = count + same[u][v]
        shift.append(means_ref[u] - total / count)
        shift_ref[u] = shift[u]
    merge_units([image_ref[u] for u in range(units)], [narrow] * units, shift, same, out_ref, ends_ref)


def vmem(count):
    return [pl.BlockSpec(memory_space=pltpu.VMEM)] * count


def smem(count):
    return [pl.BlockSpec(memory_space=pltpu.SMEM)] * count


def image_shapes(units, width):
    return [
        jax.ShapeDtypeStruct((units, DIRS, width), jnp.float32),
        jax.ShapeDtypeStruct((2 * DIRS, width), jnp.float32),
    ]


def first_images(labels, first, last_stats, means, start, images):
    units, _, width = means.shape
    return pl.pallas_call(
        first_kernel,
        in_specs=smem(1) + vmem(5),
        out_specs=vmem(3),
        out_shape=image_shapes(units, width) + [jax.ShapeDtypeStruct((units, 1, width), jnp.float32)],
        compiler_params=pltpu.CompilerParams(vmem_limit_bytes=4 * MIB),
        name="first_images",
    )(labels, first, last_stats, means, start, images)


def orthonormal(at_first, at_last, image_ref, first_ref, last_ref):
    units = image_ref.shape[0]
    size = units * DIRS
    first, last = first_ref[...], last_ref[...]
    images = jnp.concatenate(
        [image_ref[u] + first * at_first[u] + last * at_last[u] for u in range(units)], axis=0
    )
    gram = dot(images, images, ((1,), (1,)), HIGHEST)
    row = lax.broadcasted_iota(jnp.int32, (DIRS, size), 0)
    lane = lax.broadcasted_iota(jnp.int32, (DIRS, size), 1)
    inverse = []
    for u in range(units):
        left = gram[u * DIRS : (u + 1) * DIRS]
        right = (lane == row + u * DIRS).astype(jnp.float32)
        for k in range(DIRS - 1):
            c = u * DIRS + k
            factor = jnp.where(row[:, :1] > k, left[:, c : c + 1] / left[k : k + 1, c : c + 1], 0.0)
            right = right - factor * right[k : k + 1]
            left = left - factor * left[k : k + 1]
        diagonal = jnp.sum(jnp.where(lane == row + u * DIRS, left, 0.0), axis=1, keepdims=True)
        inverse.append(right / jnp.sqrt(diagonal))
    return dot(jnp.concatenate(inverse, axis=0), images, precision=HIGHEST)


def step_kernel(label_ref, image_ref, first_ref, last_ref, shift_ref, high_ref, low_ref, out_ref, ends_ref):
    units = image_ref.shape[0]
    same, at_first, at_last = flags(label_ref)
    basis = orthonormal(at_first, at_last, image_ref, first_ref, last_ref).astype(jnp.bfloat16)
    narrow = [basis[u * DIRS : (u + 1) * DIRS] for u in range(units)]
    images = [apply_unit(narrow[u], high_ref[u], low_ref[u]) for u in range(units)]
    merge_units(images, narrow, [shift_ref[u] for u in range(units)], same, out_ref, ends_ref)


def step(labels, images, first, last_image, shift, high, low):
    units, _, width = images.shape
    return pl.pallas_call(
        step_kernel,
        in_specs=smem(1) + vmem(6),
        out_specs=vmem(2),
        out_shape=image_shapes(units, width),
        compiler_params=pltpu.CompilerParams(vmem_limit_bytes=8 * MIB),
        name="step",
    )(labels, images, first, last_image, shift, high, low)


def last_kernel(label_ref, image_ref, first_ref, last_ref, mean_ref, shift_ref, x_ref, basis_ref, out_ref, narrow):
    units = image_ref.shape[0]
    u = pl.program_id(0)

    @pl.when(u == 0)
    def _():
        _, at_first, at_last = flags(label_ref)
        basis = orthonormal(at_first, at_last, image_ref, first_ref, last_ref)
        for v in range(units):
            basis_ref[v] = basis[v * DIRS : (v + 1) * DIRS]
            narrow[v] = basis[v * DIRS : (v + 1) * DIRS].astype(jnp.bfloat16)

    chosen = narrow[u]
    cluster_mean = mean_ref[u] - shift_ref[u]
    offset = jnp.sum(chosen.astype(jnp.float32) * cluster_mean, axis=1, keepdims=True)
    out_ref[...] = dot(chosen, x_ref[...], ((1,), (1,))) - offset


def last(labels, images, first, last_image, means, shift, x):
    rows, width = x.shape
    units = rows // UNIT
    whole = pl.BlockSpec((units, DIRS, width), lambda u: (0, 0, 0))
    one = pl.BlockSpec((DIRS, width), lambda u: (0, 0))
    line = pl.BlockSpec((units, 1, width), lambda u: (0, 0, 0))
    return pl.pallas_call(
        last_kernel,
        grid=(units,),
        in_specs=smem(1) + [whole, one, one, line, line, pl.BlockSpec((UNIT, width), lambda u: (u, 0))],
        out_specs=[whole, pl.BlockSpec((DIRS, UNIT), lambda u: (0, u))],
        out_shape=[
            jax.ShapeDtypeStruct((units, DIRS, width), jnp.float32),
            jax.ShapeDtypeStruct((DIRS, rows), jnp.float32),
        ],
        scratch_shapes=[pltpu.VMEM((units, DIRS, width), jnp.bfloat16)],
        compiler_params=pltpu.CompilerParams(vmem_limit_bytes=14 * MIB),
        name="last",
    )(labels, images, first, last_image, means, shift, x)


def per_device(n_dp, embeddings, cluster_ids, owner_table, start_basis):
    rows, width = embeddings.shape
    units = rows // UNIT
    chips = n_dp // 2
    me = lax.axis_index("dp")
    chip, core = me >> 1, me & 1
    even = core == 0
    labels = cluster_ids[::UNIT]

    near = (lambda p: p ^ 1, lambda p: (p + 1) % chips if p % 2 else (p - 1) % chips)
    far = (lambda p: p ^ 2, lambda p: (p + 2) % chips if p % 4 >= 2 else (p - 2) % chips)
    links = [
        [(2 * p + c, 2 * pairing[c](p) + c) for p in range(chips) for c in range(2)]
        for pairing in (near, far)
    ]
    upward = [(chip & 1) == core, ((chip >> 1) & 1) == core]
    mates = [(i, i ^ 1) for i in range(n_dp)]

    def halves(both):
        return both[:DIRS], both[DIRS:]

    def swap(both):
        return halves(lax.ppermute(both, "dp", mates))

    def chip_totals(own, mate, joins):
        head = jnp.where(even, own[0] + joins[0] * mate[0], mate[0] + joins[0] * own[0])
        tail = jnp.where(even, mate[1] + joins[1] * own[1], own[1] + joins[1] * mate[1])
        return head, tail

    def collect(left, right, own_side, mate, masks):
        mate_left, mate_right, at_head, at_tail = masks
        mate_side = swap(jnp.concatenate([left, right]))
        first = at_head * (left + mate_side[0]) + mate_left * mate[1]
        last_image = at_tail * (right + mate_side[1]) + mate_right * mate[0]
        return first, last_image

    means = unit_means(embeddings)
    row = lax.broadcasted_iota(jnp.int32, (DIRS, width), 0)

    def ends_stats(label):
        match = (labels == label).astype(jnp.float32)
        total = jnp.sum(match[:, None] * means.reshape(units, width), axis=0, keepdims=True)
        count = jnp.sum(match)
        return jnp.where(row == 0, total, jnp.where(row == 1, count, label.astype(jnp.float32)))

    own = jnp.concatenate([ends_stats(labels[0]), ends_stats(labels[-1])])
    mate = swap(own)
    own = halves(own)
    head, tail = own[0][2:3], own[1][2:3]
    mate_head, mate_tail = mate[0][2:3], mate[1][2:3]
    chip_head = jnp.where(even, head, mate_head)
    chip_tail = jnp.where(even, mate_tail, tail)

    def flag(value):
        return value.astype(jnp.float32)

    joins = flag(head == mate_head), flag(tail == mate_tail)
    masks = (
        flag(~even & (mate_tail == head)),
        flag(even & (mate_head == tail)),
        flag(head == chip_head),
        flag(tail == chip_tail),
    )
    totals = chip_totals(own, mate, joins)
    totals = jnp.where(row < 2, totals[0], chip_head), jnp.where(row < 2, totals[1], chip_tail)
    arrived = [
        lax.ppermute(jnp.where(up, totals[1], totals[0]), "dp", link) for link, up in zip(links, upward)
    ]
    high, low, raw = unit_spread(embeddings, means, start_basis)
    left = right = jnp.zeros((DIRS, width), jnp.float32)
    sides = []
    for got, up in zip(arrived, upward):
        from_left = flag(~up & (got[2:3] == chip_head))
        from_right = flag(up & (got[2:3] == chip_tail))
        sides.append((from_left, from_right))
        left = left + from_left * got
        right = right + from_right * got
    first_stats, last_stats = collect(left, right, own, mate, masks)

    def exchange(ends):
        mate, own = swap(ends), halves(ends)
        totals = chip_totals(own, mate, joins)
        left = right = jnp.zeros_like(own[0])
        for link, up, (from_left, from_right) in zip(links, upward, sides):
            got = lax.ppermute(jnp.where(up, totals[1], totals[0]), "dp", link)
            left = left + from_left * got
            right = right + from_right * got
        return collect(left, right, own, mate, masks)

    images, ends, shift = first_images(labels, first_stats, last_stats, means, start_basis, raw)
    for _ in range(ITERS - 1):
        images, ends = step(labels, images, *exchange(ends), shift, high, low)
    basis, projections = last(labels, images, *exchange(ends), means, shift, embeddings)

    starts = jnp.concatenate([first_stats[1, :1] == 0, labels[1:] != labels[:-1]])
    pick = (owner_table[:, None] == labels[None, :]) & starts[None, :]
    outgoing = jnp.einsum("ku,uid->kid", pick.astype(jnp.float32), basis, precision=HIGHEST)
    arrived = lax.all_to_all(outgoing, "dp", 0, 0, tiled=True)
    return jnp.sum(arrived, axis=0, keepdims=True), projections


def solution(mesh):
    in_specs = (P(("groups", "dp"), None), P(("groups", "dp")), P("groups"), P())
    out_specs = (P(("groups", "dp"), None, None), P(None, ("groups", "dp")))
    body = functools.partial(per_device, mesh.shape["dp"])
    return jax.shard_map(body, mesh=mesh, in_specs=in_specs, out_specs=out_specs, check_vma=False)
```

time: 229 us -> 155 us (0.68)
  Pallas kernels: 95.6 us -> 55.1 us
  blocking collectives: 42 us -> 17.1 us
  between operations: 16.6 us -> 2.91 us
  waiting for transfers between devices: 26.2 us -> 36.5 us
  other arithmetic: 13.2 us -> 4.59 us
  starting transfers between devices: 21.6 us -> 29.9 us
  local copies, waits for them, and re-layouts: 10.4 us -> 8.05 us
    pallas_call x7, Pallas kernels: 60.8 us -> 24.7 us  [the longest x5 20.4 us: step(): pl.pallas_call(step_kernel, in_specs=smem(1) + vmem(6), out_specs=vmem(2)...]
    all_gather x1 -> x0, blocking collectives: 24.6 us -> none  [per_device(): stats = lax.all_gather(stats, 'dp').reshape(n_dp, 2, units, width)]
    ppermute x24 -> x28, waiting for transfers between devices: 26.2 us -> 36.5 us  [the longest x12 22.2 us: exchange(): got = lax.ppermute(jnp.where(up, totals[1], totals[0]), 'dp', link)]
    ppermute x24 -> x28, starting transfers between devices: 21.6 us -> 29.9 us  [the longest x14 22.1 us: swap(): return halves(lax.ppermute(both, 'dp', mates))]
    unnamed x9 -> x14, local copies, waits for them, and re-layouts: 0.85 us -> 5.8 us
    squeeze x6 -> x0, local copies, waits for them, and re-layouts: 4.68 us -> none  [exchange(): own_head, own_tail = (images[0], images[-1])]
    add x6 -> x8, other arithmetic: 3.78 us -> 0.19 us  [the longest x7 0.17 us: collect(): last_image = at_tail * (right + mate_side[1]) + mate_right * mate[0]]
    select_n x6 -> x9, other arithmetic: 4.76 us -> 1.4 us  [the longest x1 1.11 us: ends_stats(): jnp.where(row == 1, count, label.astype(jnp.float32))]
  transfers between devices with their start and end apart: 24 -> 28, of which waited for: 21 -> 27; matrix products, arithmetic and copies ran while one was open for 2% -> 0% of each run, Pallas kernels for 0% -> 15%
where the time goes in v2:
time: 155 us
  Pallas kernels  55.1 us (36%)
  waiting for transfers between devices  36.5 us (24%)
  starting transfers between devices  29.9 us (19%)
  blocking collectives  17.1 us (11%)
  local copies, waits for them, and re-layouts  8.05 us (5%)
  other arithmetic  4.59 us (3%)
  between operations  2.91 us (2%)
    pallas_call x1, Pallas kernels, unit_spread(): pl.pallas_call(spread_kernel, grid=(units,), in_specs=[pl.BlockSpec((UNIT...  23.1 us
    ppermute x12, waiting for transfers between devices, exchange(): got = lax.ppermute(jnp.where(up, totals[1], totals[0]), 'dp', link)  22.2 us
    ppermute x14, starting transfers between devices, swap(): return halves(lax.ppermute(both, 'dp', mates))  22.1 us
    pallas_call x5, Pallas kernels, step(): pl.pallas_call(step_kernel, in_specs=smem(1) + vmem(6), out_specs=vmem(2)...  20.4 us
    all_to_all x1, blocking collectives, per_device(): arrived = lax.all_to_all(outgoing, 'dp', 0, 0, tiled=True)  17.1 us
    ppermute x14, waiting for transfers between devices, swap(): return halves(lax.ppermute(both, 'dp', mates))  12 us
    pallas_call x1, Pallas kernels, last(): pl.pallas_call(last_kernel, grid=(units,), in_specs=smem(1) + [whole, one...  7.34 us
    unnamed x14, local copies, waits for them, and re-layouts  5.8 us
  transfers between devices with their start and end apart: 28, of which 27 were waited for; matrix products, arithmetic and copies ran while one was open for 0% of the time, Pallas kernels for 15%

profile of v2, /device:TPU:0, one launch (start us, length us, event | category | flops | bytes accessed | tf_op | source)
XLA Modules:
  0.0 154.7 jit_solution(14364378635455303620)
XLA Ops:
  3.4 1.9 %fusion.38 = (f32[]{:T(128)}, f32[4]{0:T(128)S(1)}, f32[]{:T(128)}, f32[4]{0:T(128)S(1)}) fusion(s32[4]{0:T(128)S(1)} %slice.160.label_ref, s32[]{:T(128)} %bitcast, s32[]{:T(128)} %bitcast.1), kind=kLoop, calls=%fused_computation.126 | loop fusion | flops 22 | bytes 64 | tf_op jit(solution)/shard_map/reduce_sum | solution.py:277
  5.3 5.8 %copy-done = bf16[8192,1024]{1,0:T(8,128)(2,1)S(1)} copy-done((bf16[8192,1024]{1,0:T(8,128)(2,1)S(1)}, bf16[8192,1024]{1,0:T(8,128)(2,1)}, u32[]{:S(2)}) %copy-start) | copy-done | bytes 16777240
  11.0 3.6 %unit_means.1.mean_ref.means_ref = f32[4,1,1024]{2,1,0:T(1,128)S(1)} custom-call(bf16[8192,1024]{1,0:T(8,128)(2,1)S(1)} %copy-done), custom_call_target="tpu_custom_call" | custom-call | tf_op jit(solution)/shard_map/unit_means/pallas_call | solution.py:37
  14.7 1.1 compare_select_fusion
  17.5 2.9 %collective-permute-start.1 = (f32[8,1024]{1,0:T(8,128)S(1)}, f32[8,1024]{1,0:T(8,128)S(1)}, u32[]{:S(2)}, u32[]{:S(2)}) collective-permute-start(f32[8,1024]{1,0:T(8,128)S(1)} %get-tuple-element.82), channel_id=1, source_target_pairs={{0,2},{1,15},{2,0},{3,5},{4,6},{5,3},{6,4},{7,9},{8,10},{9,7},{10,... | collective-permute-start | bytes 98312 | tf_op jit(solution)/shard_map/ppermute | solution.py:301
  20.4 1.6 %collective-permute-start.2 = (f32[8,1024]{1,0:T(8,128)S(1)}, f32[8,1024]{1,0:T(8,128)S(1)}, u32[]{:S(2)}, u32[]{:S(2)}) collective-permute-start(f32[8,1024]{1,0:T(8,128)S(1)} %get-tuple-element.83), channel_id=1, source_target_pairs={{0,4},{1,13},{2,6},{3,15},{4,0},{5,9},{6,2},{7,11},{8,12},{9,5},{1... | collective-permute-start | bytes 98312 | tf_op jit(solution)/shard_map/ppermute | solution.py:301
  22.3 2.0 %collective-permute-done.2 = f32[8,1024]{1,0:T(8,128)S(1)} collective-permute-done((f32[8,1024]{1,0:T(8,128)S(1)}, f32[8,1024]{1,0:T(8,128)S(1)}, u32[]{:S(2)}, u32[]{:S(2)}) %collective-permute-start.2) | collective-permute-done | bytes 32800 | tf_op jit(solution)/shard_map/ppermute | solution.py:301
  24.4 3.6 %collective-permute-start.3 = (f32[16,1024]{1,0:T(8,128)S(1)}, f32[16,1024]{1,0:T(8,128)S(1)}, u32[]{:S(2)}, u32[]{:S(2)}) collective-permute-start(f32[16,1024]{1,0:T(8,128)S(1)} %pad_maximum_fusion.1), channel_id=1, source_target_pairs={{0,1},{1,0},{2,3},{3,2},{4,5},{5,4},{6,7},{7,6},{8,9},{9,8},{10,11... | collective-permute-start | bytes 196616 | tf_op jit(solution)/shard_map/ppermute | solution.py:257
  28.0 23.1 %unit_spread.1 = (bf16[4,1024,1024]{2,1,0:T(8,128)(2,1)S(1)}, bf16[4,1024,1024]{2,1,0:T(8,128)(2,1)S(1)}, f32[4,8,1024]{2,1,0:T(8,128)S(1)}) custom-call(bf16[8192,1024]{1,0:T(8,128)(2,1)} %x_ref.5, f32[4,1,1024]{2,1,0:T(1,128)S(1)} %unit_means.1.mean_ref.means_ref, f32[8,1024]{1,0:T(8,128)S(1)} %copy-done.1), custom_call_target="tpu_custom_call" | custom-call | tf_op jit(solution)/shard_map/unit_spread/pallas_call | solution.py:67
  51.9 1.2 collective-permute-done.4
  53.3 3.8 %collective-permute-done.5 = f32[8,1024]{1,0:T(8,128)S(1)} collective-permute-done((f32[8,1024]{1,0:T(8,128)S(1)}, f32[8,1024]{1,0:T(8,128)S(1)}, u32[]{:S(2)}, u32[]{:S(2)}) %collective-permute-start.5) | collective-permute-done | bytes 32800 | tf_op jit(solution)/shard_map/ppermute | solution.py:319
  57.3 1.7 %collective-permute-start.7 = (f32[16,1024]{1,0:T(8,128)S(1)}, f32[16,1024]{1,0:T(8,128)S(1)}, u32[]{:S(2)}, u32[]{:S(2)}) collective-permute-start(f32[16,1024]{1,0:T(8,128)S(1)} %pad_maximum_fusion.2), channel_id=1, source_target_pairs={{0,1},{1,0},{2,3},{3,2},{4,5},{5,4},{6,7},{7,6},{8,9},{9,8},{10,11... | collective-permute-start | bytes 196616 | tf_op jit(solution)/shard_map/ppermute | solution.py:257
  59.9 4.0 %step.5 = (f32[4,8,1024]{2,1,0:T(8,128)S(1)}, f32[16,1024]{1,0:T(8,128)S(1)}) custom-call(s32[4]{0:T(128)S(1)} %slice.160.label_ref, f32[4,8,1024]{2,1,0:T(8,128)S(1)} %get-tuple-element.21.image_ref, f32[8,1024]{1,0:T(8,128)S(1)} %get-tuple-element.71.first_ref, f32[8,1024]{1,0:T(8,128)S(1)} %get-tuple-element.70.last_ref, ...), custom_call_target="tpu_custom_call" | custom-call | tf_op jit(solution)/shard_map/step/pallas_call | solution.py:186
  65.3 1.0 collective-permute-start.9
  66.2 3.0 %collective-permute-done.9 = f32[8,1024]{1,0:T(8,128)S(1)} collective-permute-done((f32[8,1024]{1,0:T(8,128)S(1)}, f32[8,1024]{1,0:T(8,128)S(1)}, u32[]{:S(2)}, u32[]{:S(2)}) %collective-permute-start.9) | collective-permute-done | bytes 32800 | tf_op jit(solution)/shard_map/ppermute | solution.py:319
  70.2 3.4 %collective-permute-start.11 = (f32[16,1024]{1,0:T(8,128)S(1)}, f32[16,1024]{1,0:T(8,128)S(1)}, u32[]{:S(2)}, u32[]{:S(2)}) collective-permute-start(f32[16,1024]{1,0:T(8,128)S(1)} %pad_maximum_fusion.3), channel_id=1, source_target_pairs={{0,1},{1,0},{2,3},{3,2},{4,5},{5,4},{6,7},{7,6},{8,9},{9,8},{10,11... | collective-permute-start | bytes 196616 | tf_op jit(solution)/shard_map/ppermute | solution.py:257
  74.5 4.0 %step.6 = (f32[4,8,1024]{2,1,0:T(8,128)S(1)}, f32[16,1024]{1,0:T(8,128)S(1)}) custom-call(s32[4]{0:T(128)S(1)} %slice.160.label_ref, f32[4,8,1024]{2,1,0:T(8,128)S(1)} %get-tuple-element.26.image_ref, f32[8,1024]{1,0:T(8,128)S(1)} %get-tuple-element.69.first_ref, f32[8,1024]{1,0:T(8,128)S(1)} %get-tuple-element.68.last_ref, ...), custom_call_target="tpu_custom_call" | custom-call | tf_op jit(solution)/shard_map/step/pallas_call | solution.py:186
  80.1 3.8 %collective-permute-done.13 = f32[8,1024]{1,0:T(8,128)S(1)} collective-permute-done((f32[8,1024]{1,0:T(8,128)S(1)}, f32[8,1024]{1,0:T(8,128)S(1)}, u32[]{:S(2)}, u32[]{:S(2)}) %collective-permute-start.13) | collective-permute-done | bytes 32800 | tf_op jit(solution)/shard_map/ppermute | solution.py:319
  84.0 1.9 %collective-permute-start.15 = (f32[16,1024]{1,0:T(8,128)S(1)}, f32[16,1024]{1,0:T(8,128)S(1)}, u32[]{:S(2)}, u32[]{:S(2)}) collective-permute-start(f32[16,1024]{1,0:T(8,128)S(1)} %pad_maximum_fusion.4), channel_id=1, source_target_pairs={{0,1},{1,0},{2,3},{3,2},{4,5},{5,4},{6,7},{7,6},{8,9},{9,8},{10,11... | collective-permute-start | bytes 196616 | tf_op jit(solution)/shard_map/ppermute | solution.py:257
  86.8 4.0 %step.7 = (f32[4,8,1024]{2,1,0:T(8,128)S(1)}, f32[16,1024]{1,0:T(8,128)S(1)}) custom-call(s32[4]{0:T(128)S(1)} %slice.160.label_ref, f32[4,8,1024]{2,1,0:T(8,128)S(1)} %get-tuple-element.28.image_ref, f32[8,1024]{1,0:T(8,128)S(1)} %get-tuple-element.67.first_ref, f32[8,1024]{1,0:T(8,128)S(1)} %get-tuple-element.66.last_ref, ...), custom_call_target="tpu_custom_call" | custom-call | tf_op jit(solution)/shard_map/step/pallas_call | solution.py:186
  92.2 1.0 collective-permute-start.17
  93.2 3.0 %collective-permute-done.17 = f32[8,1024]{1,0:T(8,128)S(1)} collective-permute-done((f32[8,1024]{1,0:T(8,128)S(1)}, f32[8,1024]{1,0:T(8,128)S(1)}, u32[]{:S(2)}, u32[]{:S(2)}) %collective-permute-start.17) | collective-permute-done | bytes 32800 | tf_op jit(solution)/shard_map/ppermute | solution.py:319
  97.1 3.4 %collective-permute-start.19 = (f32[16,1024]{1,0:T(8,128)S(1)}, f32[16,1024]{1,0:T(8,128)S(1)}, u32[]{:S(2)}, u32[]{:S(2)}) collective-permute-start(f32[16,1024]{1,0:T(8,128)S(1)} %pad_maximum_fusion.5), channel_id=1, source_target_pairs={{0,1},{1,0},{2,3},{3,2},{4,5},{5,4},{6,7},{7,6},{8,9},{9,8},{10,11... | collective-permute-start | bytes 196616 | tf_op jit(solution)/shard_map/ppermute | solution.py:257
  101.5 4.3 %step.8 = (f32[4,8,1024]{2,1,0:T(8,128)S(1)}, f32[16,1024]{1,0:T(8,128)S(1)}) custom-call(s32[4]{0:T(128)S(1)} %slice.160.label_ref, f32[4,8,1024]{2,1,0:T(8,128)S(1)} %get-tuple-element.30.image_ref, f32[8,1024]{1,0:T(8,128)S(1)} %get-tuple-element.65.first_ref, f32[8,1024]{1,0:T(8,128)S(1)} %get-tuple-element.64.last_ref, ...), custom_call_target="tpu_custom_call" | custom-call | tf_op jit(solution)/shard_map/step/pallas_call | solution.py:186
  107.3 3.8 %collective-permute-done.21 = f32[8,1024]{1,0:T(8,128)S(1)} collective-permute-done((f32[8,1024]{1,0:T(8,128)S(1)}, f32[8,1024]{1,0:T(8,128)S(1)}, u32[]{:S(2)}, u32[]{:S(2)}) %collective-permute-start.21) | collective-permute-done | bytes 32800 | tf_op jit(solution)/shard_map/ppermute | solution.py:319
  111.2 1.9 %collective-permute-start.23 = (f32[16,1024]{1,0:T(8,128)S(1)}, f32[16,1024]{1,0:T(8,128)S(1)}, u32[]{:S(2)}, u32[]{:S(2)}) collective-permute-start(f32[16,1024]{1,0:T(8,128)S(1)} %pad_maximum_fusion.6), channel_id=1, source_target_pairs={{0,1},{1,0},{2,3},{3,2},{4,5},{5,4},{6,7},{7,6},{8,9},{9,8},{10,11... | collective-permute-start | bytes 196616 | tf_op jit(solution)/shard_map/ppermute | solution.py:257
  114.0 4.0 %step.9 = (f32[4,8,1024]{2,1,0:T(8,128)S(1)}, f32[16,1024]{1,0:T(8,128)S(1)}) custom-call(s32[4]{0:T(128)S(1)} %slice.160.label_ref, f32[4,8,1024]{2,1,0:T(8,128)S(1)} %get-tuple-element.32.image_ref, f32[8,1024]{1,0:T(8,128)S(1)} %get-tuple-element.63.first_ref, f32[8,1024]{1,0:T(8,128)S(1)} %get-tuple-element.62.last_ref, ...), custom_call_target="tpu_custom_call" | custom-call | tf_op jit(solution)/shard_map/step/pallas_call | solution.py:186
  119.4 1.0 collective-permute-start.25
  121.7 1.8 %collective-permute-done.25 = f32[8,1024]{1,0:T(8,128)S(1)} collective-permute-done((f32[8,1024]{1,0:T(8,128)S(1)}, f32[8,1024]{1,0:T(8,128)S(1)}, u32[]{:S(2)}, u32[]{:S(2)}) %collective-permute-start.25) | collective-permute-done | bytes 32800 | tf_op jit(solution)/shard_map/ppermute | solution.py:319
  124.4 3.4 %collective-permute-start.27 = (f32[16,1024]{1,0:T(8,128)S(1)}, f32[16,1024]{1,0:T(8,128)S(1)}, u32[]{:S(2)}, u32[]{:S(2)}) collective-permute-start(f32[16,1024]{1,0:T(8,128)S(1)} %pad_maximum_fusion.7), channel_id=1, source_target_pairs={{0,1},{1,0},{2,3},{3,2},{4,5},{5,4},{6,7},{7,6},{8,9},{9,8},{10,11... | collective-permute-start | bytes 196616 | tf_op jit(solution)/shard_map/ppermute | solution.py:257
  128.8 7.3 %last.1 = (f32[4,8,1024]{2,1,0:T(8,128)S(1)}, f32[8,8192]{1,0:T(8,128)}) custom-call(s32[4]{0:T(128)S(1)} %slice.160.label_ref, f32[4,8,1024]{2,1,0:T(8,128)S(1)} %get-tuple-element.34.image_ref, f32[8,1024]{1,0:T(8,128)S(1)} %get-tuple-element.61.first_ref, f32[8,1024]{1,0:T(8,128)S(1)} %get-tuple-element.60.last_ref, ...), custom_call_target="tpu_custom_call" | custom-call | tf_op jit(solution)/shard_map/last/pallas_call | solution.py:220
  136.9 17.1 %all_to_all.5 = f32[16,8,1024]{2,1,0:T(8,128)S(1)} all-to-all(f32[16,8,1024]{2,1,0:T(8,128)S(1)} %copy.8), channel_id=1, replica_groups=mesh['groups'=2,'dp'=16] {'dp'}, dimensions={0} | all-to-all | bytes 1048576 | tf_op jit(solution)/shard_map/all_to_all | solution.py:332
  (94 shorter events, 22.3 us)
Async XLA Ops:
  11.0 17.0 %copy-start.1 = (f32[8,1024]{1,0:T(8,128)S(1)}, f32[8,1024]{1,0:T(8,128)}, u32[]{:S(2)}) copy-start(f32[8,1024]{1,0:T(8,128)} %start_ref.3) | copy-start | bytes 98308
  15.9 1.4 collective-permute-start
  17.5 4.8 %collective-permute-start.1 = (f32[8,1024]{1,0:T(8,128)S(1)}, f32[8,1024]{1,0:T(8,128)S(1)}, u32[]{:S(2)}, u32[]{:S(2)}) collective-permute-start(f32[8,1024]{1,0:T(8,128)S(1)} %get-tuple-element.82), channel_id=1, source_target_pairs={{0,2},{1,15},{2,0},{3,5},{4,6},{5,3},{6,4},{7,9},{8,10},{9,7},{10,... | collective-permute-start | bytes 98312 | tf_op jit(solution)/shard_map/ppermute | solution.py:301
  20.4 3.9 %collective-permute-start.2 = (f32[8,1024]{1,0:T(8,128)S(1)}, f32[8,1024]{1,0:T(8,128)S(1)}, u32[]{:S(2)}, u32[]{:S(2)}) collective-permute-start(f32[8,1024]{1,0:T(8,128)S(1)} %get-tuple-element.83), channel_id=1, source_target_pairs={{0,4},{1,13},{2,6},{3,15},{4,0},{5,9},{6,2},{7,11},{8,12},{9,5},{1... | collective-permute-start | bytes 98312 | tf_op jit(solution)/shard_map/ppermute | solution.py:301
  24.4 26.7 %collective-permute-start.3 = (f32[16,1024]{1,0:T(8,128)S(1)}, f32[16,1024]{1,0:T(8,128)S(1)}, u32[]{:S(2)}, u32[]{:S(2)}) collective-permute-start(f32[16,1024]{1,0:T(8,128)S(1)} %pad_maximum_fusion.1), channel_id=1, source_target_pairs={{0,1},{1,0},{2,3},{3,2},{4,5},{5,4},{6,7},{7,6},{8,9},{9,8},{10,11... | collective-permute-start | bytes 196616 | tf_op jit(solution)/shard_map/ppermute | solution.py:257
  51.8 1.3 collective-permute-start.4
  53.2 4.0 %collective-permute-start.5 = (f32[8,1024]{1,0:T(8,128)S(1)}, f32[8,1024]{1,0:T(8,128)S(1)}, u32[]{:S(2)}, u32[]{:S(2)}) collective-permute-start(f32[8,1024]{1,0:T(8,128)S(1)} %get-tuple-element.58), channel_id=1, source_target_pairs={{0,2},{1,15},{2,0},{3,5},{4,6},{5,3},{6,4},{7,9},{8,10},{9,7},{10,... | collective-permute-start | bytes 98312 | tf_op jit(solution)/shard_map/ppermute | solution.py:319
  53.2 4.0 %collective-permute-start.6 = (f32[8,1024]{1,0:T(8,128)S(1)}, f32[8,1024]{1,0:T(8,128)S(1)}, u32[]{:S(2)}, u32[]{:S(2)}) collective-permute-start(f32[8,1024]{1,0:T(8,128)S(1)} %get-tuple-element.59), channel_id=1, source_target_pairs={{0,4},{1,13},{2,6},{3,15},{4,0},{5,9},{6,2},{7,11},{8,12},{9,5},{1... | collective-permute-start | bytes 98312 | tf_op jit(solution)/shard_map/ppermute | solution.py:319
  57.3 2.6 %collective-permute-start.7 = (f32[16,1024]{1,0:T(8,128)S(1)}, f32[16,1024]{1,0:T(8,128)S(1)}, u32[]{:S(2)}, u32[]{:S(2)}) collective-permute-start(f32[16,1024]{1,0:T(8,128)S(1)} %pad_maximum_fusion.2), channel_id=1, source_target_pairs={{0,1},{1,0},{2,3},{3,2},{4,5},{5,4},{6,7},{7,6},{8,9},{9,8},{10,11... | collective-permute-start | bytes 196616 | tf_op jit(solution)/shard_map/ppermute | solution.py:257
  63.9 1.3 collective-permute-start.8
  65.3 4.0 %collective-permute-start.9 = (f32[8,1024]{1,0:T(8,128)S(1)}, f32[8,1024]{1,0:T(8,128)S(1)}, u32[]{:S(2)}, u32[]{:S(2)}) collective-permute-start(f32[8,1024]{1,0:T(8,128)S(1)} %get-tuple-element.56), channel_id=1, source_target_pairs={{0,2},{1,15},{2,0},{3,5},{4,6},{5,3},{6,4},{7,9},{8,10},{9,7},{10,... | collective-permute-start | bytes 98312 | tf_op jit(solution)/shard_map/ppermute | solution.py:319
  66.2 3.9 %collective-permute-start.10 = (f32[8,1024]{1,0:T(8,128)S(1)}, f32[8,1024]{1,0:T(8,128)S(1)}, u32[]{:S(2)}, u32[]{:S(2)}) collective-permute-start(f32[8,1024]{1,0:T(8,128)S(1)} %get-tuple-element.57), channel_id=1, source_target_pairs={{0,4},{1,13},{2,6},{3,15},{4,0},{5,9},{6,2},{7,11},{8,12},{9,5},{1... | collective-permute-start | bytes 98312 | tf_op jit(solution)/shard_map/ppermute | solution.py:319
  70.2 4.3 %collective-permute-start.11 = (f32[16,1024]{1,0:T(8,128)S(1)}, f32[16,1024]{1,0:T(8,128)S(1)}, u32[]{:S(2)}, u32[]{:S(2)}) collective-permute-start(f32[16,1024]{1,0:T(8,128)S(1)} %pad_maximum_fusion.3), channel_id=1, source_target_pairs={{0,1},{1,0},{2,3},{3,2},{4,5},{5,4},{6,7},{7,6},{8,9},{9,8},{10,11... | collective-permute-start | bytes 196616 | tf_op jit(solution)/shard_map/ppermute | solution.py:257
  78.6 1.3 collective-permute-start.12
  79.9 4.0 %collective-permute-start.13 = (f32[8,1024]{1,0:T(8,128)S(1)}, f32[8,1024]{1,0:T(8,128)S(1)}, u32[]{:S(2)}, u32[]{:S(2)}) collective-permute-start(f32[8,1024]{1,0:T(8,128)S(1)} %get-tuple-element.54), channel_id=1, source_target_pairs={{0,2},{1,15},{2,0},{3,5},{4,6},{5,3},{6,4},{7,9},{8,10},{9,7},{10,... | collective-permute-start | bytes 98312 | tf_op jit(solution)/shard_map/ppermute | solution.py:319
  80.0 4.0 %collective-permute-start.14 = (f32[8,1024]{1,0:T(8,128)S(1)}, f32[8,1024]{1,0:T(8,128)S(1)}, u32[]{:S(2)}, u32[]{:S(2)}) collective-permute-start(f32[8,1024]{1,0:T(8,128)S(1)} %get-tuple-element.55), channel_id=1, source_target_pairs={{0,4},{1,13},{2,6},{3,15},{4,0},{5,9},{6,2},{7,11},{8,12},{9,5},{1... | collective-permute-start | bytes 98312 | tf_op jit(solution)/shard_map/ppermute | solution.py:319
  84.0 2.8 %collective-permute-start.15 = (f32[16,1024]{1,0:T(8,128)S(1)}, f32[16,1024]{1,0:T(8,128)S(1)}, u32[]{:S(2)}, u32[]{:S(2)}) collective-permute-start(f32[16,1024]{1,0:T(8,128)S(1)} %pad_maximum_fusion.4), channel_id=1, source_target_pairs={{0,1},{1,0},{2,3},{3,2},{4,5},{5,4},{6,7},{7,6},{8,9},{9,8},{10,11... | collective-permute-start | bytes 196616 | tf_op jit(solution)/shard_map/ppermute | solution.py:257
  90.9 1.3 collective-permute-start.16
  92.2 4.0 %collective-permute-start.17 = (f32[8,1024]{1,0:T(8,128)S(1)}, f32[8,1024]{1,0:T(8,128)S(1)}, u32[]{:S(2)}, u32[]{:S(2)}) collective-permute-start(f32[8,1024]{1,0:T(8,128)S(1)} %get-tuple-element.52), channel_id=1, source_target_pairs={{0,2},{1,15},{2,0},{3,5},{4,6},{5,3},{6,4},{7,9},{8,10},{9,7},{10,... | collective-permute-start | bytes 98312 | tf_op jit(solution)/shard_map/ppermute | solution.py:319
  93.2 3.9 %collective-permute-start.18 = (f32[8,1024]{1,0:T(8,128)S(1)}, f32[8,1024]{1,0:T(8,128)S(1)}, u32[]{:S(2)}, u32[]{:S(2)}) collective-permute-start(f32[8,1024]{1,0:T(8,128)S(1)} %get-tuple-element.53), channel_id=1, source_target_pairs={{0,4},{1,13},{2,6},{3,15},{4,0},{5,9},{6,2},{7,11},{8,12},{9,5},{1... | collective-permute-start | bytes 98312 | tf_op jit(solution)/shard_map/ppermute | solution.py:319
  97.1 4.3 %collective-permute-start.19 = (f32[16,1024]{1,0:T(8,128)S(1)}, f32[16,1024]{1,0:T(8,128)S(1)}, u32[]{:S(2)}, u32[]{:S(2)}) collective-permute-start(f32[16,1024]{1,0:T(8,128)S(1)} %pad_maximum_fusion.5), channel_id=1, source_target_pairs={{0,1},{1,0},{2,3},{3,2},{4,5},{5,4},{6,7},{7,6},{8,9},{9,8},{10,11... | collective-permute-start | bytes 196616 | tf_op jit(solution)/shard_map/ppermute | solution.py:257
  101.5 27.2 %slice-start = ((s8[16777216]{0:T(1024)(128)(4,1)}), s8[4194304]{0:T(1024)(128)(4,1)S(1)}, s32[]{:S(2)}) async-start(s8[16777216]{0:T(1024)(128)(4,1)} %bitcast.26), calls=%async_computation.1 | async-start | bytes 8388608
  101.5 27.2 %slice-start.1 = ((s8[16777216]{0:T(1024)(128)(4,1)}), s8[4194304]{0:T(1024)(128)(4,1)S(1)}, s32[]{:S(2)}) async-start(s8[16777216]{0:T(1024)(128)(4,1)} %bitcast.26), calls=%async_computation.2 | async-start | bytes 8388608
  105.8 1.3 collective-permute-start.20
  107.1 4.0 %collective-permute-start.21 = (f32[8,1024]{1,0:T(8,128)S(1)}, f32[8,1024]{1,0:T(8,128)S(1)}, u32[]{:S(2)}, u32[]{:S(2)}) collective-permute-start(f32[8,1024]{1,0:T(8,128)S(1)} %get-tuple-element.50), channel_id=1, source_target_pairs={{0,2},{1,15},{2,0},{3,5},{4,6},{5,3},{6,4},{7,9},{8,10},{9,7},{10,... | collective-permute-start | bytes 98312 | tf_op jit(solution)/shard_map/ppermute | solution.py:319
  107.2 4.0 %collective-permute-start.22 = (f32[8,1024]{1,0:T(8,128)S(1)}, f32[8,1024]{1,0:T(8,128)S(1)}, u32[]{:S(2)}, u32[]{:S(2)}) collective-permute-start(f32[8,1024]{1,0:T(8,128)S(1)} %get-tuple-element.51), channel_id=1, source_target_pairs={{0,4},{1,13},{2,6},{3,15},{4,0},{5,9},{6,2},{7,11},{8,12},{9,5},{1... | collective-permute-start | bytes 98312 | tf_op jit(solution)/shard_map/ppermute | solution.py:319
  111.2 2.8 %collective-permute-start.23 = (f32[16,1024]{1,0:T(8,128)S(1)}, f32[16,1024]{1,0:T(8,128)S(1)}, u32[]{:S(2)}, u32[]{:S(2)}) collective-permute-start(f32[16,1024]{1,0:T(8,128)S(1)} %pad_maximum_fusion.6), channel_id=1, source_target_pairs={{0,1},{1,0},{2,3},{3,2},{4,5},{5,4},{6,7},{7,6},{8,9},{9,8},{10,11... | collective-permute-start | bytes 196616 | tf_op jit(solution)/shard_map/ppermute | solution.py:257
  114.0 14.7 %slice-start.2 = ((s8[16777216]{0:T(1024)(128)(4,1)}), s8[4194304]{0:T(1024)(128)(4,1)S(1)}, s32[]{:S(2)}) async-start(s8[16777216]{0:T(1024)(128)(4,1)} %bitcast.26), calls=%async_computation.3 | async-start | bytes 8388608
  118.1 1.3 collective-permute-start.24
  119.4 4.0 %collective-permute-start.25 = (f32[8,1024]{1,0:T(8,128)S(1)}, f32[8,1024]{1,0:T(8,128)S(1)}, u32[]{:S(2)}, u32[]{:S(2)}) collective-permute-start(f32[8,1024]{1,0:T(8,128)S(1)} %get-tuple-element.48), channel_id=1, source_target_pairs={{0,2},{1,15},{2,0},{3,5},{4,6},{5,3},{6,4},{7,9},{8,10},{9,7},{10,... | collective-permute-start | bytes 98312 | tf_op jit(solution)/shard_map/ppermute | solution.py:319
  120.4 3.9 %collective-permute-start.26 = (f32[8,1024]{1,0:T(8,128)S(1)}, f32[8,1024]{1,0:T(8,128)S(1)}, u32[]{:S(2)}, u32[]{:S(2)}) collective-permute-start(f32[8,1024]{1,0:T(8,128)S(1)} %get-tuple-element.49), channel_id=1, source_target_pairs={{0,4},{1,13},{2,6},{3,15},{4,0},{5,9},{6,2},{7,11},{8,12},{9,5},{1... | collective-permute-start | bytes 98312 | tf_op jit(solution)/shard_map/ppermute | solution.py:319
  124.4 4.3 %collective-permute-start.27 = (f32[16,1024]{1,0:T(8,128)S(1)}, f32[16,1024]{1,0:T(8,128)S(1)}, u32[]{:S(2)}, u32[]{:S(2)}) collective-permute-start(f32[16,1024]{1,0:T(8,128)S(1)} %pad_maximum_fusion.7), channel_id=1, source_target_pairs={{0,1},{1,0},{2,3},{3,2},{4,5},{5,4},{6,7},{7,6},{8,9},{9,8},{10,11... | collective-permute-start | bytes 196616 | tf_op jit(solution)/shard_map/ppermute | solution.py:257
  (3 other events, 27.8 us)

commit v3 on v2

--- a/solution.py
+++ b/solution.py
@@ -11,6 +11,9 @@
 ITERS = 6
 UNIT = 2048
 HIGHEST = lax.Precision.HIGHEST
+BLOCK = 256
+CHUNKS = 16
+PART = 1024
 MIB = 1024 * 1024
 
 
@@ -20,50 +23,77 @@
     )
 
 
-def means_kernel(parts, x_ref, out_ref):
-    part = jnp.sum(x_ref[...].astype(jnp.float32), axis=0, keepdims=True) * (1 / UNIT)
-
-    @pl.when(pl.program_id(1) == 0)
-    def _():
-        out_ref[0] = part
-
-    @pl.when(pl.program_id(1) > 0)
-    def _():
-        out_ref[0] += part
-
-
-def unit_means(x, parts=4):
+def fetch(source, target, arrived, first, size):
+    copies = []
+    for i in range(target.shape[0] // size):
+        part = source.at[pl.ds(first + i * size, size)]
+        copies.append(pltpu.make_async_copy(part, target.at[pl.ds(i * size, size)], arrived.at[i]))
+        copies[-1].start()
+    return copies
+
+
+def means_kernel(label_ref, source, means_ref, ends_ref, x_ref, arrived):
+    units = means_ref.shape[0]
+    size = x_ref.shape[0] // CHUNKS
+    copies = fetch(source, x_ref, arrived, 0, size)
+    for i in range(CHUNKS):
+        copies[i].wait()
+        part = jnp.sum(x_ref[i * size : (i + 1) * size].astype(jnp.float32), axis=0, keepdims=True)
+        part = part * (1 / UNIT)
+        u = i * size // UNIT
+        means_ref[u] = part if i * size % UNIT == 0 else means_ref[u] + part
+    same, _, _ = flags(label_ref)
+    ends_ref[...] = jnp.zeros_like(ends_ref)
+    for base, end in ((0, 0), (DIRS, units - 1)):
+        total, count = jnp.zeros_like(part), jnp.zeros_like(part)
+        for v in range(units):
+            total = total + means_ref[v] * same[end][v]
+            count = count + same[end][v]
+        ends_ref[base : base + 1] = total
+        ends_ref[base + 1 : base + 2] = count
+        ends_ref[base + 2 : base + 3] = jnp.zeros_like(part) + label_ref[end].astype(jnp.float32)
+
+
+def unit_means(labels, x):
     rows, width = x.shape
-    return pl.pallas_call(
-        functools.partial(means_kernel, parts),
-        grid=(rows // UNIT, parts),
-        in_specs=[pl.BlockSpec((UNIT // parts, width), lambda u, p: (u * parts + p, 0))],
-        out_specs=pl.BlockSpec((1, 1, width), lambda u, p: (u, 0, 0)),
-        out_shape=jax.ShapeDtypeStruct((rows // UNIT, 1, width), jnp.float32),
-        compiler_params=pltpu.CompilerParams(vmem_limit_bytes=8 * MIB),
+    units = rows // UNIT
+    return pl.pallas_call(
+        means_kernel,
+        in_specs=smem(1) + [pl.BlockSpec(memory_space=pl.ANY)],
+        out_specs=vmem(2),
+        out_shape=[
+            jax.ShapeDtypeStruct((units, 1, width), jnp.float32),
+            jax.ShapeDtypeStruct((2 * DIRS, width), jnp.float32),
+        ],
+        scratch_shapes=[pltpu.VMEM(x.shape, x.dtype), pltpu.SemaphoreType.DMA((CHUNKS,))],
+        compiler_params=pltpu.CompilerParams(vmem_limit_bytes=20 * MIB),
         name="unit_means",
-    )(x)
-
-
-def apply_unit(narrow, high, low):
-    return dot(narrow, high) + dot(narrow, low)
-
-
-def spread_kernel(x_ref, mean_ref, start_ref, high_ref, low_ref, image_ref):
+    )(labels, x)
+
+
+def apply_unit(narrow, spread_ref, u):
+    return dot(narrow, spread_ref[0, u]) + dot(narrow, spread_ref[1, u])
+
+
+def spread_kernel(x_ref, mean_ref, start_ref, spread_ref, image_ref, centered):
     u = pl.program_id(0)
-    centered = (x_ref[...].astype(jnp.float32) - mean_ref[0]).astype(jnp.bfloat16)
-    spread = dot(centered, centered, ((0,), (0,)))
-    high = spread.astype(jnp.bfloat16)
-    high_ref[u] = high
-    low = (spread - high.astype(jnp.float32)).astype(jnp.bfloat16)
-    low_ref[u] = low
-    image_ref[u] = apply_unit(start_ref[...].astype(jnp.bfloat16), high, low)
+    width = centered.shape[1]
+    for a in range(0, UNIT, BLOCK):
+        centered[a : a + BLOCK] = (x_ref[a : a + BLOCK].astype(jnp.float32) - mean_ref[0]).astype(jnp.bfloat16)
+    for a in range(0, width, BLOCK):
+        spread = dot(centered[:, a : a + BLOCK], centered[:, a:], ((0,), (0,)))
+        high = spread.astype(jnp.bfloat16)
+        low = (spread - high.astype(jnp.float32)).astype(jnp.bfloat16)
+        for h, part in enumerate((high, low)):
+            spread_ref[h, u, a : a + BLOCK, a:] = part
+            if a + BLOCK < width:
+                spread_ref[h, u, a + BLOCK :, a : a + BLOCK] = part[:, BLOCK:].T
+    image_ref[u] = apply_unit(start_ref[...].astype(jnp.bfloat16), spread_ref, u)
 
 
 def unit_spread(x, means, start):
     rows, width = x.shape
     units = rows // UNIT
-    half = pltpu.VMEM((units, width, width), jnp.bfloat16)
     return pl.pallas_call(
         spread_kernel,
         grid=(units,),
@@ -72,9 +102,13 @@
             pl.BlockSpec((1, 1, width), lambda u: (u, 0, 0)),
             pl.BlockSpec((DIRS, width), lambda u: (0, 0)),
         ],
-        out_specs=vmem(3),
-        out_shape=[half, half, pltpu.VMEM((units, DIRS, width), jnp.float32)],
-        compiler_params=pltpu.CompilerParams(vmem_limit_bytes=28 * MIB),
+        out_specs=vmem(2),
+        out_shape=[
+            pltpu.VMEM((2, units, width, width), jnp.bfloat16),
+            jax.ShapeDtypeStruct((units, DIRS, width), jnp.float32),
+        ],
+        scratch_shapes=[pltpu.VMEM((UNIT, width), jnp.bfloat16)],
+        compiler_params=pltpu.CompilerParams(vmem_limit_bytes=18 * MIB),
         name="unit_spread",
     )(x, means, start)
 
@@ -172,64 +206,144 @@
     return dot(jnp.concatenate(inverse, axis=0), images, precision=HIGHEST)
 
 
-def step_kernel(label_ref, image_ref, first_ref, last_ref, shift_ref, high_ref, low_ref, out_ref, ends_ref):
+def step_kernel(label_ref, image_ref, first_ref, last_ref, shift_ref, spread_ref, out_ref, ends_ref):
     units = image_ref.shape[0]
     same, at_first, at_last = flags(label_ref)
     basis = orthonormal(at_first, at_last, image_ref, first_ref, last_ref).astype(jnp.bfloat16)
     narrow = [basis[u * DIRS : (u + 1) * DIRS] for u in range(units)]
-    images = [apply_unit(narrow[u], high_ref[u], low_ref[u]) for u in range(units)]
+    images = [apply_unit(narrow[u], spread_ref, u) for u in range(units)]
     merge_units(images, narrow, [shift_ref[u] for u in range(units)], same, out_ref, ends_ref)
 
 
-def step(labels, images, first, last_image, shift, high, low):
+def route_kernel(owner_ref, me_ref, label_ref, *refs):
+    *refs, kept_ref, sent_ref = refs
+    step_kernel(label_ref, *refs)
+    images = [refs[-2][u] for u in range(refs[-2].shape[0])]
+    core = me_ref[0] & 1
+    for j in range(kept_ref.shape[0]):
+        for ref, bit in ((kept_ref, core), (sent_ref, 1 - core)):
+            owner = owner_ref[2 * j + bit]
+            total = jnp.zeros_like(images[0])
+            for u, image in enumerate(images):
+                chosen = label_ref[u] == owner
+                if u > 0:
+                    chosen = chosen & (label_ref[u] != label_ref[u - 1])
+                total = total + image * jnp.where(chosen, 1.0, 0.0)
+            ref[j] = total
+
+
+def step(labels, images, first, last_image, shift, spread):
     units, _, width = images.shape
     return pl.pallas_call(
         step_kernel,
-        in_specs=smem(1) + vmem(6),
+        in_specs=smem(1) + vmem(5),
         out_specs=vmem(2),
         out_shape=image_shapes(units, width),
         compiler_params=pltpu.CompilerParams(vmem_limit_bytes=8 * MIB),
         name="step",
-    )(labels, images, first, last_image, shift, high, low)
-
-
-def last_kernel(label_ref, image_ref, first_ref, last_ref, mean_ref, shift_ref, x_ref, basis_ref, out_ref, narrow):
-    units = image_ref.shape[0]
-    u = pl.program_id(0)
-
-    @pl.when(u == 0)
-    def _():
-        _, at_first, at_last = flags(label_ref)
-        basis = orthonormal(at_first, at_last, image_ref, first_ref, last_ref)
-        for v in range(units):
-            basis_ref[v] = basis[v * DIRS : (v + 1) * DIRS]
-            narrow[v] = basis[v * DIRS : (v + 1) * DIRS].astype(jnp.bfloat16)
-
-    chosen = narrow[u]
-    cluster_mean = mean_ref[u] - shift_ref[u]
-    offset = jnp.sum(chosen.astype(jnp.float32) * cluster_mean, axis=1, keepdims=True)
-    out_ref[...] = dot(chosen, x_ref[...], ((1,), (1,))) - offset
-
-
-def last(labels, images, first, last_image, means, shift, x):
+    )(labels, images, first, last_image, shift, spread)
+
+
+def step_and_route(owners, me, labels, images, first, last_image, shift, spread):
+    units, _, width = images.shape
+    tiles = jax.ShapeDtypeStruct((owners.shape[0] // 2, DIRS, width), jnp.float32)
+    return pl.pallas_call(
+        route_kernel,
+        in_specs=smem(3) + vmem(5),
+        out_specs=vmem(4),
+        out_shape=image_shapes(units, width) + [tiles, tiles],
+        compiler_params=pltpu.CompilerParams(vmem_limit_bytes=8 * MIB),
+        name="step_and_route",
+    )(owners, me.reshape(1), labels, images, first, last_image, shift, spread)
+
+
+def project_half(first, narrow, mean_ref, shift_ref, x_ref, copies, out_ref):
+    size = x_ref.shape[0] // len(copies)
+    for i, copy in enumerate(copies):
+        u = first + i * size // UNIT
+        chosen = narrow[u * DIRS : (u + 1) * DIRS]
+        mean = mean_ref[u] - shift_ref[u]
+        offset = jnp.sum(chosen.astype(jnp.float32) * mean, axis=1, keepdims=True)
+        copy.wait()
+        rows = x_ref[i * size : (i + 1) * size]
+        at = first * UNIT + i * size
+        out_ref[:, at : at + size] = dot(chosen, rows, ((1,), (1,))) - offset
+
+
+def early_kernel(
+    label_ref, image_ref, first_ref, last_ref, mean_ref, shift_ref, source, narrow_ref, out_ref, x_ref, arrived
+):
+    copies = fetch(source, x_ref, arrived, 0, PART)
+    _, at_first, at_last = flags(label_ref)
+    narrow = orthonormal(at_first, at_last, image_ref, first_ref, last_ref).astype(jnp.bfloat16)
+    narrow_ref[...] = narrow
+    project_half(0, narrow, mean_ref, shift_ref, x_ref, copies, out_ref)
+
+
+def late_kernel(narrow_ref, mean_ref, shift_ref, half_ref, source, out_ref, x_ref, arrived):
+    first = mean_ref.shape[0] // 2
+    copies = fetch(source, x_ref, arrived, first * UNIT, PART)
+    out_ref[:, : half_ref.shape[1]] = half_ref[...]
+    project_half(first, narrow_ref[...], mean_ref, shift_ref, x_ref, copies, out_ref)
+
+
+def half_scratch(x):
+    rows, width = x.shape
+    return [
+        pltpu.VMEM((rows // 2, width), x.dtype),
+        pltpu.SemaphoreType.DMA((rows // 2 // PART,)),
+    ]
+
+
+def half_cost(rows, width):
+    return pl.CostEstimate(flops=rows * width * 256, bytes_accessed=rows * width, transcendentals=0)
+
+
+def project_early(labels, images, first, last_image, means, shift, x):
     rows, width = x.shape
     units = rows // UNIT
-    whole = pl.BlockSpec((units, DIRS, width), lambda u: (0, 0, 0))
-    one = pl.BlockSpec((DIRS, width), lambda u: (0, 0))
-    line = pl.BlockSpec((units, 1, width), lambda u: (0, 0, 0))
-    return pl.pallas_call(
-        last_kernel,
-        grid=(units,),
-        in_specs=smem(1) + [whole, one, one, line, line, pl.BlockSpec((UNIT, width), lambda u: (u, 0))],
-        out_specs=[whole, pl.BlockSpec((DIRS, UNIT), lambda u: (0, u))],
+    return pl.pallas_call(
+        early_kernel,
+        in_specs=smem(1) + vmem(5) + [pl.BlockSpec(memory_space=pl.ANY)],
+        out_specs=vmem(2),
+        scratch_shapes=half_scratch(x),
         out_shape=[
-            jax.ShapeDtypeStruct((units, DIRS, width), jnp.float32),
-            jax.ShapeDtypeStruct((DIRS, rows), jnp.float32),
+            jax.ShapeDtypeStruct((units * DIRS, width), jnp.bfloat16),
+            jax.ShapeDtypeStruct((DIRS, units // 2 * UNIT), jnp.float32),
         ],
-        scratch_shapes=[pltpu.VMEM((units, DIRS, width), jnp.bfloat16)],
-        compiler_params=pltpu.CompilerParams(vmem_limit_bytes=14 * MIB),
-        name="last",
+        compiler_params=pltpu.CompilerParams(vmem_limit_bytes=12 * MIB),
+        cost_estimate=half_cost(rows, width),
+        name="project_early",
     )(labels, images, first, last_image, means, shift, x)
+
+
+def project_late(narrow, means, shift, half, x):
+    rows, width = x.shape
+    return pl.pallas_call(
+        late_kernel,
+        in_specs=vmem(4) + [pl.BlockSpec(memory_space=pl.ANY)],
+        out_specs=vmem(1)[0],
+        scratch_shapes=half_scratch(x),
+        out_shape=jax.ShapeDtypeStruct((DIRS, rows), jnp.float32),
+        compiler_params=pltpu.CompilerParams(vmem_limit_bytes=12 * MIB),
+        cost_estimate=half_cost(rows, width),
+        name="project_late",
+    )(narrow, means, shift, half, x)
+
+
+def finish_kernel(kept_ref, got_ref, out_ref):
+    out_ref[0] = orthonormal([1.0], [0.0], kept_ref, got_ref.at[0], got_ref.at[0])
+
+
+def finish(kept, got):
+    return pl.pallas_call(
+        finish_kernel,
+        in_specs=vmem(2),
+        out_specs=vmem(1)[0],
+        out_shape=jax.ShapeDtypeStruct(kept.shape, jnp.float32),
+        compiler_params=pltpu.CompilerParams(vmem_limit_bytes=4 * MIB),
+        name="finish",
+    )(kept, got)
 
 
 def per_device(n_dp, embeddings, cluster_ids, owner_table, start_basis):
@@ -268,16 +382,9 @@
         last_image = at_tail * (right + mate_side[1]) + mate_right * mate[0]
         return first, last_image
 
-    means = unit_means(embeddings)
+    embeddings = pltpu.with_memory_space_constraint(embeddings, pltpu.HBM)
+    means, own = unit_means(labels, embeddings)
     row = lax.broadcasted_iota(jnp.int32, (DIRS, width), 0)
-
-    def ends_stats(label):
-        match = (labels == label).astype(jnp.float32)
-        total = jnp.sum(match[:, None] * means.reshape(units, width), axis=0, keepdims=True)
-        count = jnp.sum(match)
-        return jnp.where(row == 0, total, jnp.where(row == 1, count, label.astype(jnp.float32)))
-
-    own = jnp.concatenate([ends_stats(labels[0]), ends_stats(labels[-1])])
     mate = swap(own)
     own = halves(own)
     head, tail = own[0][2:3], own[1][2:3]
@@ -300,7 +407,8 @@
     arrived = [
         lax.ppermute(jnp.where(up, totals[1], totals[0]), "dp", link) for link, up in zip(links, upward)
     ]
-    high, low, raw = unit_spread(embeddings, means, start_basis)
+    spread, raw = unit_spread(embeddings, means, start_basis)
+    raw, *arrived = lax.optimization_barrier((raw, *arrived))
     left = right = jnp.zeros((DIRS, width), jnp.float32)
     sides = []
     for got, up in zip(arrived, upward):
@@ -321,16 +429,35 @@
             right = right + from_right * got
         return collect(left, right, own, mate, masks)
 
+    def halve(tiles, bit):
+        low, high = tiles[0::2], tiles[1::2]
+        set_here = (me & bit) != 0
+        return jnp.where(set_here, high, low), jnp.where(set_here, low, high)
+
+    def route(sent, bit):
+        return lax.ppermute(sent, "dp", [(i, i ^ bit) for i in range(n_dp)])
+
+    def split(tiles, bit):
+        kept, sent = halve(tiles, bit)
+        return kept + route(sent, bit)
+
     images, ends, shift = first_images(labels, first_stats, last_stats, means, start_basis, raw)
-    for _ in range(ITERS - 1):
-        images, ends = step(labels, images, *exchange(ends), shift, high, low)
-    basis, projections = last(labels, images, *exchange(ends), means, shift, embeddings)
-
-    starts = jnp.concatenate([first_stats[1, :1] == 0, labels[1:] != labels[:-1]])
-    pick = (owner_table[:, None] == labels[None, :]) & starts[None, :]
-    outgoing = jnp.einsum("ku,uid->kid", pick.astype(jnp.float32), basis, precision=HIGHEST)
-    arrived = lax.all_to_all(outgoing, "dp", 0, 0, tiled=True)
-    return jnp.sum(arrived, axis=0, keepdims=True), projections
+    for _ in range(ITERS - 2):
+        images, ends = step(labels, images, *exchange(ends), shift, spread)
+
+    images, ends, kept, sent = step_and_route(
+        owner_table, me, labels, images, *exchange(ends), shift, spread
+    )
+    kept = kept + route(sent, 1)
+    bit = 2
+    while 2 * bit < n_dp:
+        kept = split(kept, bit)
+        bit *= 2
+    kept, sent = halve(kept, bit)
+    got = route(sent, bit)
+    narrow, half = project_early(labels, images, *exchange(ends), means, shift, embeddings)
+    projections = project_late(narrow, means, shift, half, embeddings)
+    return finish(kept, got), projections
 
 
 def solution(mesh):

time: 155 us -> 129 us (0.83)
  blocking collectives: 17.1 us -> 0 us
  local copies, waits for them, and re-layouts: 8.05 us -> 0.86 us
  starting transfers between devices: 29.9 us -> 34.7 us
  other arithmetic: 4.59 us -> 0.71 us
  between operations: 2.91 us -> 0.96 us
    all_to_all x1 -> x0, blocking collectives: 17.1 us -> none  [per_device(): arrived = lax.all_to_all(outgoing, 'dp', 0, 0, tiled=True)]
    pallas_call x7 -> x9, Pallas kernels: 31.3 us -> 38.7 us  [the longest x4 16.4 us: step(): pl.pallas_call(step_kernel, in_specs=smem(1) + vmem(5), out_specs=vmem(2)...]
    pallas_call x1, Pallas kernels: 23.1 us -> 16.6 us  [unit_spread(): pl.pallas_call(spread_kernel, grid=(units,), in_specs=[pl.BlockSpec((UNIT...]
    unnamed x14 -> x4, local copies, waits for them, and re-layouts: 5.8 us -> 0.01 us
    ppermute x0 -> x4, waiting for transfers between devices: none -> 4.64 us  [route(): return lax.ppermute(sent, 'dp', [(i, i ^ bit) for i in range(n_dp)])]
    ppermute x0 -> x4, starting transfers between devices: none -> 4.09 us  [route(): return lax.ppermute(sent, 'dp', [(i, i ^ bit) for i in range(n_dp)])]
    ppermute x12, waiting for transfers between devices: 22.2 us -> 18.4 us  [exchange(): got = lax.ppermute(jnp.where(up, totals[1], totals[0]), 'dp', link)]
    reduce_sum x3 -> x0, other arithmetic: 2.63 us -> none  [the longest x1 1.89 us: ends_stats(): count = jnp.sum(match)]
  transfers between devices with their start and end apart: 28 -> 32, of which waited for: 27 -> 27; matrix products, arithmetic and copies ran while one was open for 0% -> 0% of each run, Pallas kernels for 15% -> 20%
where the time goes in v3:
time: 129 us
  Pallas kernels  56 us (43%)
  waiting for transfers between devices  35.5 us (28%)
  starting transfers between devices  34.7 us (27%)
    ppermute x14, starting transfers between devices, swap(): return halves(lax.ppermute(both, 'dp', mates))  21.9 us
    ppermute x12, waiting for transfers between devices, exchange(): got = lax.ppermute(jnp.where(up, totals[1], totals[0]), 'dp', link)  18.4 us
    pallas_call x1, Pallas kernels, unit_spread(): pl.pallas_call(spread_kernel, grid=(units,), in_specs=[pl.BlockSpec((UNIT...  16.6 us
    pallas_call x4, Pallas kernels, step(): pl.pallas_call(step_kernel, in_specs=smem(1) + vmem(5), out_specs=vmem(2)...  16.4 us
    ppermute x14, waiting for transfers between devices, swap(): return halves(lax.ppermute(both, 'dp', mates))  12.5 us
    pallas_call x1, Pallas kernels, unit_means(): pl.pallas_call(means_kernel, in_specs=smem(1) + [pl.BlockSpec(memory_spac...  6.7 us
    pallas_call x1, Pallas kernels, project_late(): pl.pallas_call(late_kernel, in_specs=vmem(4) + [pl.BlockSpec(memory_space...  4.97 us
    pallas_call x1, Pallas kernels, project_early(): pl.pallas_call(early_kernel, in_specs=smem(1) + vmem(5) + [pl.BlockSpec(m...  4.82 us
  transfers between devices with their start and end apart: 32, of which 27 were waited for; matrix products, arithmetic and copies ran while one was open for 0% of the time, Pallas kernels for 20%

profile of v3, /device:TPU:0, one launch (start us, length us, event | category | flops | bytes accessed | tf_op | source)
XLA Modules:
  0.0 128.7 jit_solution(18019124892685768965)
XLA Ops:
  1.5 6.7 %unit_means.1 = (f32[4,1,1024]{2,1,0:T(1,128)S(1)}, f32[16,1024]{1,0:T(8,128)S(1)}) custom-call(s32[4]{0:T(128)S(1)} %slice.173.label_ref, bf16[8192,1024]{1,0:T(8,128)(2,1)} %source.5), custom_call_target="tpu_custom_call" | custom-call | tf_op jit(solution)/shard_map/unit_means/pallas_call | solution.py:60
  9.7 2.9 %collective-permute-start.1 = (f32[8,1024]{1,0:T(8,128)S(1)}, f32[8,1024]{1,0:T(8,128)S(1)}, u32[]{:S(2)}, u32[]{:S(2)}) collective-permute-start(f32[8,1024]{1,0:T(8,128)S(1)} %get-tuple-element.55), channel_id=1, source_target_pairs={{0,2},{1,15},{2,0},{3,5},{4,6},{5,3},{6,4},{7,9},{8,10},{9,7},{10,... | collective-permute-start | bytes 98312 | tf_op jit(solution)/shard_map/ppermute | solution.py:408
  12.6 1.6 %collective-permute-start.2 = (f32[8,1024]{1,0:T(8,128)S(1)}, f32[8,1024]{1,0:T(8,128)S(1)}, u32[]{:S(2)}, u32[]{:S(2)}) collective-permute-start(f32[8,1024]{1,0:T(8,128)S(1)} %get-tuple-element.54), channel_id=1, source_target_pairs={{0,4},{1,13},{2,6},{3,15},{4,0},{5,9},{6,2},{7,11},{8,12},{9,5},{1... | collective-permute-start | bytes 98312 | tf_op jit(solution)/shard_map/ppermute | solution.py:408
  14.2 16.6 %unit_spread.1 = (bf16[2,4,1024,1024]{3,2,1,0:T(8,128)(2,1)S(1)}, f32[4,8,1024]{2,1,0:T(8,128)S(1)}) custom-call(bf16[8192,1024]{1,0:T(8,128)(2,1)} %source.5, f32[4,1,1024]{2,1,0:T(1,128)S(1)} %get-tuple-element.27.mean_ref.means_ref, f32[8,1024]{1,0:T(8,128)S(1)} %copy-done), custom_call_target="tpu_custom_call" | custom-call | tf_op jit(solution)/shard_map/unit_spread/pallas_call | solution.py:97
  30.9 1.6 %collective-permute-start.3 = (f32[16,1024]{1,0:T(8,128)S(1)}, f32[16,1024]{1,0:T(8,128)S(1)}, u32[]{:S(2)}, u32[]{:S(2)}) collective-permute-start(f32[16,1024]{1,0:T(8,128)S(1)} %pad_maximum_fusion), channel_id=1, source_target_pairs={{0,1},{1,0},{2,3},{3,2},{4,5},{5,4},{6,7},{7,6},{8,9},{9,8},{10,11... | collective-permute-start | bytes 196616 | tf_op jit(solution)/shard_map/ppermute | solution.py:371
  32.5 0.9 collective-permute-done.3
  36.7 2.7 %collective-permute-done.5 = f32[8,1024]{1,0:T(8,128)S(1)} collective-permute-done((f32[8,1024]{1,0:T(8,128)S(1)}, f32[8,1024]{1,0:T(8,128)S(1)}, u32[]{:S(2)}, u32[]{:S(2)}) %collective-permute-start.5) | collective-permute-done | bytes 32800 | tf_op jit(solution)/shard_map/ppermute | solution.py:427
  39.9 1.6 %collective-permute-start.7 = (f32[16,1024]{1,0:T(8,128)S(1)}, f32[16,1024]{1,0:T(8,128)S(1)}, u32[]{:S(2)}, u32[]{:S(2)}) collective-permute-start(f32[16,1024]{1,0:T(8,128)S(1)} %pad_maximum_fusion.1), channel_id=1, source_target_pairs={{0,1},{1,0},{2,3},{3,2},{4,5},{5,4},{6,7},{7,6},{8,9},{9,8},{10,11... | collective-permute-start | bytes 196616 | tf_op jit(solution)/shard_map/ppermute | solution.py:371
  42.5 4.0 %step.4 = (f32[4,8,1024]{2,1,0:T(8,128)S(1)}, f32[16,1024]{1,0:T(8,128)S(1)}) custom-call(s32[4]{0:T(128)S(1)} %slice.173.label_ref, f32[4,8,1024]{2,1,0:T(8,128)S(1)} %get-tuple-element.32.image_ref, f32[8,1024]{1,0:T(8,128)S(1)} %get-tuple-element.79.first_ref, f32[8,1024]{1,0:T(8,128)S(1)} %get-tuple-element.78.last_ref, ...), custom_call_target="tpu_custom_call" | custom-call | tf_op jit(solution)/shard_map/step/pallas_call | solution.py:237
  46.9 0.9 collective-permute-done.8
  47.9 1.7 %collective-permute-start.9 = (f32[8,1024]{1,0:T(8,128)S(1)}, f32[8,1024]{1,0:T(8,128)S(1)}, u32[]{:S(2)}, u32[]{:S(2)}) collective-permute-start(f32[8,1024]{1,0:T(8,128)S(1)} %get-tuple-element.64), channel_id=1, source_target_pairs={{0,2},{1,15},{2,0},{3,5},{4,6},{5,3},{6,4},{7,9},{8,10},{9,7},{10,... | collective-permute-start | bytes 98312 | tf_op jit(solution)/shard_map/ppermute | solution.py:427
  49.6 2.2 %collective-permute-done.10 = f32[8,1024]{1,0:T(8,128)S(1)} collective-permute-done((f32[8,1024]{1,0:T(8,128)S(1)}, f32[8,1024]{1,0:T(8,128)S(1)}, u32[]{:S(2)}, u32[]{:S(2)}) %collective-permute-start.10) | collective-permute-done | bytes 32800 | tf_op jit(solution)/shard_map/ppermute | solution.py:427
  51.9 4.0 %collective-permute-start.11 = (f32[16,1024]{1,0:T(8,128)S(1)}, f32[16,1024]{1,0:T(8,128)S(1)}, u32[]{:S(2)}, u32[]{:S(2)}) collective-permute-start(f32[16,1024]{1,0:T(8,128)S(1)} %pad_maximum_fusion.2), channel_id=1, source_target_pairs={{0,1},{1,0},{2,3},{3,2},{4,5},{5,4},{6,7},{7,6},{8,9},{9,8},{10,11... | collective-permute-start | bytes 196616 | tf_op jit(solution)/shard_map/ppermute | solution.py:371
  56.9 4.0 %step.5 = (f32[4,8,1024]{2,1,0:T(8,128)S(1)}, f32[16,1024]{1,0:T(8,128)S(1)}) custom-call(s32[4]{0:T(128)S(1)} %slice.173.label_ref, f32[4,8,1024]{2,1,0:T(8,128)S(1)} %get-tuple-element.36.image_ref, f32[8,1024]{1,0:T(8,128)S(1)} %get-tuple-element.77.first_ref, f32[8,1024]{1,0:T(8,128)S(1)} %get-tuple-element.76.last_ref, ...), custom_call_target="tpu_custom_call" | custom-call | tf_op jit(solution)/shard_map/step/pallas_call | solution.py:237
  61.4 0.9 collective-permute-done.12
  62.5 3.8 %collective-permute-done.13 = f32[8,1024]{1,0:T(8,128)S(1)} collective-permute-done((f32[8,1024]{1,0:T(8,128)S(1)}, f32[8,1024]{1,0:T(8,128)S(1)}, u32[]{:S(2)}, u32[]{:S(2)}) %collective-permute-start.13) | collective-permute-done | bytes 32800 | tf_op jit(solution)/shard_map/ppermute | solution.py:427
  66.4 2.4 %collective-permute-start.15 = (f32[16,1024]{1,0:T(8,128)S(1)}, f32[16,1024]{1,0:T(8,128)S(1)}, u32[]{:S(2)}, u32[]{:S(2)}) collective-permute-start(f32[16,1024]{1,0:T(8,128)S(1)} %pad_maximum_fusion.3), channel_id=1, source_target_pairs={{0,1},{1,0},{2,3},{3,2},{4,5},{5,4},{6,7},{7,6},{8,9},{9,8},{10,11... | collective-permute-start | bytes 196616 | tf_op jit(solution)/shard_map/ppermute | solution.py:371
  68.8 0.9 collective-permute-done.15
  69.7 4.0 %step.6 = (f32[4,8,1024]{2,1,0:T(8,128)S(1)}, f32[16,1024]{1,0:T(8,128)S(1)}) custom-call(s32[4]{0:T(128)S(1)} %slice.173.label_ref, f32[4,8,1024]{2,1,0:T(8,128)S(1)} %get-tuple-element.38.image_ref, f32[8,1024]{1,0:T(8,128)S(1)} %get-tuple-element.75.first_ref, f32[8,1024]{1,0:T(8,128)S(1)} %get-tuple-element.74.last_ref, ...), custom_call_target="tpu_custom_call" | custom-call | tf_op jit(solution)/shard_map/step/pallas_call | solution.py:237
  75.6 3.5 %collective-permute-done.17 = f32[8,1024]{1,0:T(8,128)S(1)} collective-permute-done((f32[8,1024]{1,0:T(8,128)S(1)}, f32[8,1024]{1,0:T(8,128)S(1)}, u32[]{:S(2)}, u32[]{:S(2)}) %collective-permute-start.17) | collective-permute-done | bytes 32800 | tf_op jit(solution)/shard_map/ppermute | solution.py:427
  79.5 3.4 %collective-permute-start.19 = (f32[16,1024]{1,0:T(8,128)S(1)}, f32[16,1024]{1,0:T(8,128)S(1)}, u32[]{:S(2)}, u32[]{:S(2)}) collective-permute-start(f32[16,1024]{1,0:T(8,128)S(1)} %pad_maximum_fusion.4), channel_id=1, source_target_pairs={{0,1},{1,0},{2,3},{3,2},{4,5},{5,4},{6,7},{7,6},{8,9},{9,8},{10,11... | collective-permute-start | bytes 196616 | tf_op jit(solution)/shard_map/ppermute | solution.py:371
  83.9 4.3 %step.7 = (f32[4,8,1024]{2,1,0:T(8,128)S(1)}, f32[16,1024]{1,0:T(8,128)S(1)}) custom-call(s32[4]{0:T(128)S(1)} %slice.173.label_ref, f32[4,8,1024]{2,1,0:T(8,128)S(1)} %get-tuple-element.40.image_ref, f32[8,1024]{1,0:T(8,128)S(1)} %get-tuple-element.73.first_ref, f32[8,1024]{1,0:T(8,128)S(1)} %get-tuple-element.72.last_ref, ...), custom_call_target="tpu_custom_call" | custom-call | tf_op jit(solution)/shard_map/step/pallas_call | solution.py:237
  89.6 3.8 %collective-permute-done.21 = f32[8,1024]{1,0:T(8,128)S(1)} collective-permute-done((f32[8,1024]{1,0:T(8,128)S(1)}, f32[8,1024]{1,0:T(8,128)S(1)}, u32[]{:S(2)}, u32[]{:S(2)}) %collective-permute-start.21) | collective-permute-done | bytes 32800 | tf_op jit(solution)/shard_map/ppermute | solution.py:427
  93.6 2.4 %collective-permute-start.23 = (f32[16,1024]{1,0:T(8,128)S(1)}, f32[16,1024]{1,0:T(8,128)S(1)}, u32[]{:S(2)}, u32[]{:S(2)}) collective-permute-start(f32[16,1024]{1,0:T(8,128)S(1)} %pad_maximum_fusion.5), channel_id=1, source_target_pairs={{0,1},{1,0},{2,3},{3,2},{4,5},{5,4},{6,7},{7,6},{8,9},{9,8},{10,11... | collective-permute-start | bytes 196616 | tf_op jit(solution)/shard_map/ppermute | solution.py:371
  96.9 4.1 %step_and_route.1 = (f32[4,8,1024]{2,1,0:T(8,128)S(1)}, f32[16,1024]{1,0:T(8,128)S(1)}, f32[8,8,1024]{2,1,0:T(8,128)S(1)}, f32[8,8,1024]{2,1,0:T(8,128)S(1)}) custom-call(s32[16]{0:T(128)S(1)} %copy-done.1, s32[1]{0:T(128)} %bitcast.me_ref, s32[4]{0:T(128)S(1)} %slice.173.label_ref, f32[4,8,1024]{2,1,0:T(8,128)S(1)} %get-tuple-element.42.refs_0_, ...), custom_call_target="tpu_custom_call" | custom-call | tf_op jit(solution)/shard_map/step_and_route/pallas_call | solution.py:250
  102.9 2.7 %collective-permute-start.24 = (f32[8,8,1024]{2,1,0:T(8,128)S(1)}, f32[8,8,1024]{2,1,0:T(8,128)S(1)}, u32[]{:S(2)}, u32[]{:S(2)}) collective-permute-start(f32[8,8,1024]{2,1,0:T(8,128)S(1)} %get-tuple-element.45), channel_id=1, source_target_pairs={{0,1},{1,0},{2,3},{3,2},{4,5},{5,4},{6,7},{7,6},{8,9},{9,8},{10,11... | collective-permute-start | bytes 786440 | tf_op jit(solution)/shard_map/ppermute | solution.py:438
  106.8 3.4 %collective-permute-start.31 = (f32[16,1024]{1,0:T(8,128)S(1)}, f32[16,1024]{1,0:T(8,128)S(1)}, u32[]{:S(2)}, u32[]{:S(2)}) collective-permute-start(f32[16,1024]{1,0:T(8,128)S(1)} %pad_maximum_fusion.6), channel_id=1, source_target_pairs={{0,1},{1,0},{2,3},{3,2},{4,5},{5,4},{6,7},{7,6},{8,9},{9,8},{10,11... | collective-permute-start | bytes 196616 | tf_op jit(solution)/shard_map/ppermute | solution.py:371
  111.1 4.6 %collective-permute-done.25 = f32[4,8,1024]{2,1,0:T(8,128)S(1)} collective-permute-done((f32[4,8,1024]{2,1,0:T(8,128)S(1)}, f32[4,8,1024]{2,1,0:T(8,128)S(1)}, u32[]{:S(2)}, u32[]{:S(2)}) %collective-permute-start.25) | collective-permute-done | bytes 131104 | tf_op jit(solution)/shard_map/ppermute | solution.py:438
  115.9 4.8 %project_early.1 = (bf16[32,1024]{1,0:T(8,128)(2,1)S(1)}, f32[8,4096]{1,0:T(8,128)S(1)}) custom-call(s32[4]{0:T(128)S(1)} %slice.173.label_ref, f32[4,8,1024]{2,1,0:T(8,128)S(1)} %get-tuple-element.46.image_ref, f32[8,1024]{1,0:T(8,128)S(1)} %get-tuple-element.69.first_ref, f32[8,1024]{1,0:T(8,128)S(1)} %get-tuple-element.68.last_ref, ...), custom_call_target="tpu_custom_call" | custom-call | flops 2147483648 | bytes 8388608 | tf_op jit(solution)/shard_map/project_early/pallas_call | solution.py:305
  120.8 1.2 collective-permute-start.27
  122.0 5.0 %project_late.1 = f32[8,8192]{1,0:T(8,128)} custom-call(bf16[32,1024]{1,0:T(8,128)(2,1)S(1)} %get-tuple-element.48.narrow_ref, f32[4,1,1024]{2,1,0:T(1,128)S(1)} %get-tuple-element.27.mean_ref.means_ref, f32[4,1,1024]{2,1,0:T(1,128)S(1)} %get-tuple-element.34.shift_ref.refs_3_, f32[8,4096]{1,0:T(8,128)S(1)} %get-tuple-element.49.half_ref, ...), custom_call_target="tpu_custom_call" | custom-call | flops 2147483648 | bytes 8388608 | tf_op jit(solution)/shard_map/project_late/pallas_call | solution.py:322
  127.0 1.7 %finish.1 = f32[1,8,1024]{2,1,0:T(8,128)} custom-call(f32[1,8,1024]{2,1,0:T(8,128)S(1)} %get-tuple-element.93.kept_ref, f32[1,8,1024]{2,1,0:T(8,128)S(1)} %collective-permute-done.27.got_ref), custom_call_target="tpu_custom_call" | custom-call | tf_op jit(solution)/shard_map/finish/pallas_call | solution.py:339
  (85 shorter events, 19.2 us)
Async XLA Ops:
  8.2 1.4 %collective-permute-start = (f32[16,1024]{1,0:T(8,128)S(1)}, f32[16,1024]{1,0:T(8,128)S(1)}, u32[]{:S(2)}, u32[]{:S(2)}) collective-permute-start(f32[16,1024]{1,0:T(8,128)S(1)} %get-tuple-element.26), channel_id=1, source_target_pairs={{0,1},{1,0},{2,3},{3,2},{4,5},{5,4},{6,7},{7,6},{8,9},{9,8},{10,11... | collective-permute-start | bytes 196616 | tf_op jit(solution)/shard_map/ppermute | solution.py:371
  9.7 21.1 %collective-permute-start.1 = (f32[8,1024]{1,0:T(8,128)S(1)}, f32[8,1024]{1,0:T(8,128)S(1)}, u32[]{:S(2)}, u32[]{:S(2)}) collective-permute-start(f32[8,1024]{1,0:T(8,128)S(1)} %get-tuple-element.55), channel_id=1, source_target_pairs={{0,2},{1,15},{2,0},{3,5},{4,6},{5,3},{6,4},{7,9},{8,10},{9,7},{10,... | collective-permute-start | bytes 98312 | tf_op jit(solution)/shard_map/ppermute | solution.py:408
  12.6 18.2 %collective-permute-start.2 = (f32[8,1024]{1,0:T(8,128)S(1)}, f32[8,1024]{1,0:T(8,128)S(1)}, u32[]{:S(2)}, u32[]{:S(2)}) collective-permute-start(f32[8,1024]{1,0:T(8,128)S(1)} %get-tuple-element.54), channel_id=1, source_target_pairs={{0,4},{1,13},{2,6},{3,15},{4,0},{5,9},{6,2},{7,11},{8,12},{9,5},{1... | collective-permute-start | bytes 98312 | tf_op jit(solution)/shard_map/ppermute | solution.py:408
  30.9 2.5 %collective-permute-start.3 = (f32[16,1024]{1,0:T(8,128)S(1)}, f32[16,1024]{1,0:T(8,128)S(1)}, u32[]{:S(2)}, u32[]{:S(2)}) collective-permute-start(f32[16,1024]{1,0:T(8,128)S(1)} %pad_maximum_fusion), channel_id=1, source_target_pairs={{0,1},{1,0},{2,3},{3,2},{4,5},{5,4},{6,7},{7,6},{8,9},{9,8},{10,11... | collective-permute-start | bytes 196616 | tf_op jit(solution)/shard_map/ppermute | solution.py:371
  34.1 1.3 %collective-permute-start.4 = (f32[16,1024]{1,0:T(8,128)S(1)}, f32[16,1024]{1,0:T(8,128)S(1)}, u32[]{:S(2)}, u32[]{:S(2)}) collective-permute-start(f32[16,1024]{1,0:T(8,128)S(1)} %get-tuple-element.33), channel_id=1, source_target_pairs={{0,1},{1,0},{2,3},{3,2},{4,5},{5,4},{6,7},{7,6},{8,9},{9,8},{10,11... | collective-permute-start | bytes 196616 | tf_op jit(solution)/shard_map/ppermute | solution.py:371
  35.4 4.0 %collective-permute-start.5 = (f32[8,1024]{1,0:T(8,128)S(1)}, f32[8,1024]{1,0:T(8,128)S(1)}, u32[]{:S(2)}, u32[]{:S(2)}) collective-permute-start(f32[8,1024]{1,0:T(8,128)S(1)} %get-tuple-element.66), channel_id=1, source_target_pairs={{0,2},{1,15},{2,0},{3,5},{4,6},{5,3},{6,4},{7,9},{8,10},{9,7},{10,... | collective-permute-start | bytes 98312 | tf_op jit(solution)/shard_map/ppermute | solution.py:427
  36.0 3.9 %collective-permute-start.6 = (f32[8,1024]{1,0:T(8,128)S(1)}, f32[8,1024]{1,0:T(8,128)S(1)}, u32[]{:S(2)}, u32[]{:S(2)}) collective-permute-start(f32[8,1024]{1,0:T(8,128)S(1)} %get-tuple-element.67), channel_id=1, source_target_pairs={{0,4},{1,13},{2,6},{3,15},{4,0},{5,9},{6,2},{7,11},{8,12},{9,5},{1... | collective-permute-start | bytes 98312 | tf_op jit(solution)/shard_map/ppermute | solution.py:427
  39.9 2.5 %collective-permute-start.7 = (f32[16,1024]{1,0:T(8,128)S(1)}, f32[16,1024]{1,0:T(8,128)S(1)}, u32[]{:S(2)}, u32[]{:S(2)}) collective-permute-start(f32[16,1024]{1,0:T(8,128)S(1)} %pad_maximum_fusion.1), channel_id=1, source_target_pairs={{0,1},{1,0},{2,3},{3,2},{4,5},{5,4},{6,7},{7,6},{8,9},{9,8},{10,11... | collective-permute-start | bytes 196616 | tf_op jit(solution)/shard_map/ppermute | solution.py:371
  46.5 1.3 %collective-permute-start.8 = (f32[16,1024]{1,0:T(8,128)S(1)}, f32[16,1024]{1,0:T(8,128)S(1)}, u32[]{:S(2)}, u32[]{:S(2)}) collective-permute-start(f32[16,1024]{1,0:T(8,128)S(1)} %get-tuple-element.37), channel_id=1, source_target_pairs={{0,1},{1,0},{2,3},{3,2},{4,5},{5,4},{6,7},{7,6},{8,9},{9,8},{10,11... | collective-permute-start | bytes 196616 | tf_op jit(solution)/shard_map/ppermute | solution.py:371
  47.8 4.0 %collective-permute-start.10 = (f32[8,1024]{1,0:T(8,128)S(1)}, f32[8,1024]{1,0:T(8,128)S(1)}, u32[]{:S(2)}, u32[]{:S(2)}) collective-permute-start(f32[8,1024]{1,0:T(8,128)S(1)} %get-tuple-element.65), channel_id=1, source_target_pairs={{0,4},{1,13},{2,6},{3,15},{4,0},{5,9},{6,2},{7,11},{8,12},{9,5},{1... | collective-permute-start | bytes 98312 | tf_op jit(solution)/shard_map/ppermute | solution.py:427
  47.9 4.0 %collective-permute-start.9 = (f32[8,1024]{1,0:T(8,128)S(1)}, f32[8,1024]{1,0:T(8,128)S(1)}, u32[]{:S(2)}, u32[]{:S(2)}) collective-permute-start(f32[8,1024]{1,0:T(8,128)S(1)} %get-tuple-element.64), channel_id=1, source_target_pairs={{0,2},{1,15},{2,0},{3,5},{4,6},{5,3},{6,4},{7,9},{8,10},{9,7},{10,... | collective-permute-start | bytes 98312 | tf_op jit(solution)/shard_map/ppermute | solution.py:427
  51.9 4.9 %collective-permute-start.11 = (f32[16,1024]{1,0:T(8,128)S(1)}, f32[16,1024]{1,0:T(8,128)S(1)}, u32[]{:S(2)}, u32[]{:S(2)}) collective-permute-start(f32[16,1024]{1,0:T(8,128)S(1)} %pad_maximum_fusion.2), channel_id=1, source_target_pairs={{0,1},{1,0},{2,3},{3,2},{4,5},{5,4},{6,7},{7,6},{8,9},{9,8},{10,11... | collective-permute-start | bytes 196616 | tf_op jit(solution)/shard_map/ppermute | solution.py:371
  60.9 1.3 %collective-permute-start.12 = (f32[16,1024]{1,0:T(8,128)S(1)}, f32[16,1024]{1,0:T(8,128)S(1)}, u32[]{:S(2)}, u32[]{:S(2)}) collective-permute-start(f32[16,1024]{1,0:T(8,128)S(1)} %get-tuple-element.39), channel_id=1, source_target_pairs={{0,1},{1,0},{2,3},{3,2},{4,5},{5,4},{6,7},{7,6},{8,9},{9,8},{10,11... | collective-permute-start | bytes 196616 | tf_op jit(solution)/shard_map/ppermute | solution.py:371
  62.3 4.0 %collective-permute-start.13 = (f32[8,1024]{1,0:T(8,128)S(1)}, f32[8,1024]{1,0:T(8,128)S(1)}, u32[]{:S(2)}, u32[]{:S(2)}) collective-permute-start(f32[8,1024]{1,0:T(8,128)S(1)} %get-tuple-element.62), channel_id=1, source_target_pairs={{0,2},{1,15},{2,0},{3,5},{4,6},{5,3},{6,4},{7,9},{8,10},{9,7},{10,... | collective-permute-start | bytes 98312 | tf_op jit(solution)/shard_map/ppermute | solution.py:427
  62.4 4.0 %collective-permute-start.14 = (f32[8,1024]{1,0:T(8,128)S(1)}, f32[8,1024]{1,0:T(8,128)S(1)}, u32[]{:S(2)}, u32[]{:S(2)}) collective-permute-start(f32[8,1024]{1,0:T(8,128)S(1)} %get-tuple-element.63), channel_id=1, source_target_pairs={{0,4},{1,13},{2,6},{3,15},{4,0},{5,9},{6,2},{7,11},{8,12},{9,5},{1... | collective-permute-start | bytes 98312 | tf_op jit(solution)/shard_map/ppermute | solution.py:427
  66.4 3.3 %collective-permute-start.15 = (f32[16,1024]{1,0:T(8,128)S(1)}, f32[16,1024]{1,0:T(8,128)S(1)}, u32[]{:S(2)}, u32[]{:S(2)}) collective-permute-start(f32[16,1024]{1,0:T(8,128)S(1)} %pad_maximum_fusion.3), channel_id=1, source_target_pairs={{0,1},{1,0},{2,3},{3,2},{4,5},{5,4},{6,7},{7,6},{8,9},{9,8},{10,11... | collective-permute-start | bytes 196616 | tf_op jit(solution)/shard_map/ppermute | solution.py:371
  73.8 1.3 %collective-permute-start.16 = (f32[16,1024]{1,0:T(8,128)S(1)}, f32[16,1024]{1,0:T(8,128)S(1)}, u32[]{:S(2)}, u32[]{:S(2)}) collective-permute-start(f32[16,1024]{1,0:T(8,128)S(1)} %get-tuple-element.41), channel_id=1, source_target_pairs={{0,1},{1,0},{2,3},{3,2},{4,5},{5,4},{6,7},{7,6},{8,9},{9,8},{10,11... | collective-permute-start | bytes 196616 | tf_op jit(solution)/shard_map/ppermute | solution.py:371
  75.1 4.0 %collective-permute-start.17 = (f32[8,1024]{1,0:T(8,128)S(1)}, f32[8,1024]{1,0:T(8,128)S(1)}, u32[]{:S(2)}, u32[]{:S(2)}) collective-permute-start(f32[8,1024]{1,0:T(8,128)S(1)} %get-tuple-element.60), channel_id=1, source_target_pairs={{0,2},{1,15},{2,0},{3,5},{4,6},{5,3},{6,4},{7,9},{8,10},{9,7},{10,... | collective-permute-start | bytes 98312 | tf_op jit(solution)/shard_map/ppermute | solution.py:427
  75.6 3.9 %collective-permute-start.18 = (f32[8,1024]{1,0:T(8,128)S(1)}, f32[8,1024]{1,0:T(8,128)S(1)}, u32[]{:S(2)}, u32[]{:S(2)}) collective-permute-start(f32[8,1024]{1,0:T(8,128)S(1)} %get-tuple-element.61), channel_id=1, source_target_pairs={{0,4},{1,13},{2,6},{3,15},{4,0},{5,9},{6,2},{7,11},{8,12},{9,5},{1... | collective-permute-start | bytes 98312 | tf_op jit(solution)/shard_map/ppermute | solution.py:427
  79.5 4.3 %collective-permute-start.19 = (f32[16,1024]{1,0:T(8,128)S(1)}, f32[16,1024]{1,0:T(8,128)S(1)}, u32[]{:S(2)}, u32[]{:S(2)}) collective-permute-start(f32[16,1024]{1,0:T(8,128)S(1)} %pad_maximum_fusion.4), channel_id=1, source_target_pairs={{0,1},{1,0},{2,3},{3,2},{4,5},{5,4},{6,7},{7,6},{8,9},{9,8},{10,11... | collective-permute-start | bytes 196616 | tf_op jit(solution)/shard_map/ppermute | solution.py:371
  88.1 1.3 %collective-permute-start.20 = (f32[16,1024]{1,0:T(8,128)S(1)}, f32[16,1024]{1,0:T(8,128)S(1)}, u32[]{:S(2)}, u32[]{:S(2)}) collective-permute-start(f32[16,1024]{1,0:T(8,128)S(1)} %get-tuple-element.43), channel_id=1, source_target_pairs={{0,1},{1,0},{2,3},{3,2},{4,5},{5,4},{6,7},{7,6},{8,9},{9,8},{10,11... | collective-permute-start | bytes 196616 | tf_op jit(solution)/shard_map/ppermute | solution.py:371
  89.5 4.0 %collective-permute-start.21 = (f32[8,1024]{1,0:T(8,128)S(1)}, f32[8,1024]{1,0:T(8,128)S(1)}, u32[]{:S(2)}, u32[]{:S(2)}) collective-permute-start(f32[8,1024]{1,0:T(8,128)S(1)} %get-tuple-element.58), channel_id=1, source_target_pairs={{0,2},{1,15},{2,0},{3,5},{4,6},{5,3},{6,4},{7,9},{8,10},{9,7},{10,... | collective-permute-start | bytes 98312 | tf_op jit(solution)/shard_map/ppermute | solution.py:427
  89.5 4.0 %collective-permute-start.22 = (f32[8,1024]{1,0:T(8,128)S(1)}, f32[8,1024]{1,0:T(8,128)S(1)}, u32[]{:S(2)}, u32[]{:S(2)}) collective-permute-start(f32[8,1024]{1,0:T(8,128)S(1)} %get-tuple-element.59), channel_id=1, source_target_pairs={{0,4},{1,13},{2,6},{3,15},{4,0},{5,9},{6,2},{7,11},{8,12},{9,5},{1... | collective-permute-start | bytes 98312 | tf_op jit(solution)/shard_map/ppermute | solution.py:427
  93.6 3.3 %collective-permute-start.23 = (f32[16,1024]{1,0:T(8,128)S(1)}, f32[16,1024]{1,0:T(8,128)S(1)}, u32[]{:S(2)}, u32[]{:S(2)}) collective-permute-start(f32[16,1024]{1,0:T(8,128)S(1)} %pad_maximum_fusion.5), channel_id=1, source_target_pairs={{0,1},{1,0},{2,3},{3,2},{4,5},{5,4},{6,7},{7,6},{8,9},{9,8},{10,11... | collective-permute-start | bytes 196616 | tf_op jit(solution)/shard_map/ppermute | solution.py:371
  101.0 1.3 %collective-permute-start.28 = (f32[16,1024]{1,0:T(8,128)S(1)}, f32[16,1024]{1,0:T(8,128)S(1)}, u32[]{:S(2)}, u32[]{:S(2)}) collective-permute-start(f32[16,1024]{1,0:T(8,128)S(1)} %get-tuple-element.47), channel_id=1, source_target_pairs={{0,1},{1,0},{2,3},{3,2},{4,5},{5,4},{6,7},{7,6},{8,9},{9,8},{10,11... | collective-permute-start | bytes 196616 | tf_op jit(solution)/shard_map/ppermute | solution.py:371
  102.4 4.0 %collective-permute-start.29 = (f32[8,1024]{1,0:T(8,128)S(1)}, f32[8,1024]{1,0:T(8,128)S(1)}, u32[]{:S(2)}, u32[]{:S(2)}) collective-permute-start(f32[8,1024]{1,0:T(8,128)S(1)} %get-tuple-element.56), channel_id=1, source_target_pairs={{0,2},{1,15},{2,0},{3,5},{4,6},{5,3},{6,4},{7,9},{8,10},{9,7},{10,... | collective-permute-start | bytes 98312 | tf_op jit(solution)/shard_map/ppermute | solution.py:427
  102.8 3.9 %collective-permute-start.30 = (f32[8,1024]{1,0:T(8,128)S(1)}, f32[8,1024]{1,0:T(8,128)S(1)}, u32[]{:S(2)}, u32[]{:S(2)}) collective-permute-start(f32[8,1024]{1,0:T(8,128)S(1)} %get-tuple-element.57), channel_id=1, source_target_pairs={{0,4},{1,13},{2,6},{3,15},{4,0},{5,9},{6,2},{7,11},{8,12},{9,5},{1... | collective-permute-start | bytes 98312 | tf_op jit(solution)/shard_map/ppermute | solution.py:427
  102.9 7.4 %collective-permute-start.24 = (f32[8,8,1024]{2,1,0:T(8,128)S(1)}, f32[8,8,1024]{2,1,0:T(8,128)S(1)}, u32[]{:S(2)}, u32[]{:S(2)}) collective-permute-start(f32[8,8,1024]{2,1,0:T(8,128)S(1)} %get-tuple-element.45), channel_id=1, source_target_pairs={{0,1},{1,0},{2,3},{3,2},{4,5},{5,4},{6,7},{7,6},{8,9},{9,8},{10,11... | collective-permute-start | bytes 786440 | tf_op jit(solution)/shard_map/ppermute | solution.py:438
  106.8 4.3 %collective-permute-start.31 = (f32[16,1024]{1,0:T(8,128)S(1)}, f32[16,1024]{1,0:T(8,128)S(1)}, u32[]{:S(2)}, u32[]{:S(2)}) collective-permute-start(f32[16,1024]{1,0:T(8,128)S(1)} %pad_maximum_fusion.6), channel_id=1, source_target_pairs={{0,1},{1,0},{2,3},{3,2},{4,5},{5,4},{6,7},{7,6},{8,9},{9,8},{10,11... | collective-permute-start | bytes 196616 | tf_op jit(solution)/shard_map/ppermute | solution.py:371
  110.3 5.5 %collective-permute-start.25 = (f32[4,8,1024]{2,1,0:T(8,128)S(1)}, f32[4,8,1024]{2,1,0:T(8,128)S(1)}, u32[]{:S(2)}, u32[]{:S(2)}) collective-permute-start(f32[4,8,1024]{2,1,0:T(8,128)S(1)} %slice_select_fusion), channel_id=1, source_target_pairs={{0,2},{1,3},{2,0},{3,1},{4,6},{5,7},{6,4},{7,5},{8,10},{9,11},{10,... | collective-permute-start | bytes 393224 | tf_op jit(solution)/shard_map/ppermute | solution.py:438
  115.8 4.9 %collective-permute-start.26 = (f32[2,8,1024]{2,1,0:T(8,128)S(1)}, f32[2,8,1024]{2,1,0:T(8,128)S(1)}, u32[]{:S(2)}, u32[]{:S(2)}) collective-permute-start(f32[2,8,1024]{2,1,0:T(8,128)S(1)} %slice_select_fusion.1), channel_id=1, source_target_pairs={{0,4},{1,5},{2,6},{3,7},{4,0},{5,1},{6,2},{7,3},{8,12},{9,13},{10,... | collective-permute-start | bytes 196616 | tf_op jit(solution)/shard_map/ppermute | solution.py:438
  120.8 6.2 %collective-permute-start.27 = (f32[1,8,1024]{2,1,0:T(8,128)S(1)}, f32[1,8,1024]{2,1,0:T(8,128)S(1)}, u32[]{:S(2)}, u32[]{:S(2)}) collective-permute-start(f32[1,8,1024]{2,1,0:T(8,128)S(1)} %get-tuple-element.92), channel_id=1, source_target_pairs={{0,8},{1,9},{2,10},{3,11},{4,12},{5,13},{6,14},{7,15},{8,0},{9,1},... | collective-permute-start | bytes 98312 | tf_op jit(solution)/shard_map/ppermute | solution.py:438
  (2 other events, 40.7 us)

commit v4 on v3

--- a/solution.py
+++ b/solution.py
@@ -136,7 +136,7 @@
         if u == 0:
             ends_ref[:DIRS] = total
         if u == units - 1:
-            ends_ref[DIRS:] = total
+            ends_ref[DIRS : 2 * DIRS] = total
 
 
 def first_kernel(label_ref, first_ref, last_ref, means_ref, start_ref, image_ref, out_ref, ends_ref, shift_ref):
@@ -182,28 +182,32 @@
     )(labels, first, last_stats, means, start, images)
 
 
+def inverse_factor(images, row, lane):
+    shape = row.shape
+    columns = [
+        jnp.broadcast_to(jnp.sum(images * images[j : j + 1], axis=1, keepdims=True), shape)
+        for j in range(DIRS)
+    ]
+    inverse = (lane == row).astype(jnp.float32)
+    scale = jnp.zeros(shape, jnp.float32)
+    for k in range(DIRS):
+        pivot = columns[k][k : k + 1]
+        scale = jnp.where(row == k, lax.rsqrt(pivot), scale)
+        factor = jnp.where(row > k, columns[k] * (1.0 / pivot), 0.0)
+        inverse = inverse - factor * inverse[k : k + 1]
+        for j in range(k + 1, DIRS):
+            columns[j] = columns[j] - factor * columns[j][k : k + 1]
+    return inverse * scale
+
+
 def orthonormal(at_first, at_last, image_ref, first_ref, last_ref):
     units = image_ref.shape[0]
-    size = units * DIRS
     first, last = first_ref[...], last_ref[...]
-    images = jnp.concatenate(
-        [image_ref[u] + first * at_first[u] + last * at_last[u] for u in range(units)], axis=0
-    )
-    gram = dot(images, images, ((1,), (1,)), HIGHEST)
-    row = lax.broadcasted_iota(jnp.int32, (DIRS, size), 0)
-    lane = lax.broadcasted_iota(jnp.int32, (DIRS, size), 1)
-    inverse = []
-    for u in range(units):
-        left = gram[u * DIRS : (u + 1) * DIRS]
-        right = (lane == row + u * DIRS).astype(jnp.float32)
-        for k in range(DIRS - 1):
-            c = u * DIRS + k
-            factor = jnp.where(row[:, :1] > k, left[:, c : c + 1] / left[k : k + 1, c : c + 1], 0.0)
-            right = right - factor * right[k : k + 1]
-            left = left - factor * left[k : k + 1]
-        diagonal = jnp.sum(jnp.where(lane == row + u * DIRS, left, 0.0), axis=1, keepdims=True)
-        inverse.append(right / jnp.sqrt(diagonal))
-    return dot(jnp.concatenate(inverse, axis=0), images, precision=HIGHEST)
+    images = [image_ref[u] + first * at_first[u] + last * at_last[u] for u in range(units)]
+    row = lax.broadcasted_iota(jnp.int32, (DIRS, units * DIRS), 0)
+    lane = lax.broadcasted_iota(jnp.int32, (DIRS, units * DIRS), 1)
+    inverse = [inverse_factor(images[u], row, lane - u * DIRS) for u in range(units)]
+    return dot(jnp.concatenate(inverse, axis=0), jnp.concatenate(images, axis=0), precision=HIGHEST)
 
 
 def step_kernel(label_ref, image_ref, first_ref, last_ref, shift_ref, spread_ref, out_ref, ends_ref):
@@ -216,12 +220,13 @@
 
 
 def route_kernel(owner_ref, me_ref, label_ref, *refs):
-    *refs, kept_ref, sent_ref = refs
-    step_kernel(label_ref, *refs)
-    images = [refs[-2][u] for u in range(refs[-2].shape[0])]
+    *refs, ends_ref, kept_ref = refs
+    step_kernel(label_ref, *refs, ends_ref)
+    images = [refs[-1][u] for u in range(refs[-1].shape[0])]
     core = me_ref[0] & 1
-    for j in range(kept_ref.shape[0]):
-        for ref, bit in ((kept_ref, core), (sent_ref, 1 - core)):
+    count = kept_ref.shape[0] // DIRS
+    for j in range(count):
+        for ref, first, bit in ((kept_ref, 0, core), (ends_ref, 2 * DIRS, 1 - core)):
             owner = owner_ref[2 * j + bit]
             total = jnp.zeros_like(images[0])
             for u, image in enumerate(images):
@@ -229,7 +234,7 @@
                 if u > 0:
                     chosen = chosen & (label_ref[u] != label_ref[u - 1])
                 total = total + image * jnp.where(chosen, 1.0, 0.0)
-            ref[j] = total
+            ref[first + j * DIRS : first + (j + 1) * DIRS] = total
 
 
 def step(labels, images, first, last_image, shift, spread):
@@ -246,89 +251,50 @@
 
 def step_and_route(owners, me, labels, images, first, last_image, shift, spread):
     units, _, width = images.shape
-    tiles = jax.ShapeDtypeStruct((owners.shape[0] // 2, DIRS, width), jnp.float32)
+    tiles = owners.shape[0] // 2 * DIRS
+    shapes = image_shapes(units, width)
+    shapes[1] = jax.ShapeDtypeStruct((2 * DIRS + tiles, width), jnp.float32)
+    shapes.append(jax.ShapeDtypeStruct((tiles, width), jnp.float32))
     return pl.pallas_call(
         route_kernel,
         in_specs=smem(3) + vmem(5),
-        out_specs=vmem(4),
-        out_shape=image_shapes(units, width) + [tiles, tiles],
+        out_specs=vmem(3),
+        out_shape=shapes,
         compiler_params=pltpu.CompilerParams(vmem_limit_bytes=8 * MIB),
         name="step_and_route",
     )(owners, me.reshape(1), labels, images, first, last_image, shift, spread)
 
 
-def project_half(first, narrow, mean_ref, shift_ref, x_ref, copies, out_ref):
-    size = x_ref.shape[0] // len(copies)
+def project_kernel(
+    label_ref, image_ref, first_ref, last_ref, mean_ref, shift_ref, source, out_ref, x_ref, arrived
+):
+    copies = fetch(source, x_ref, arrived, 0, PART)
+    _, at_first, at_last = flags(label_ref)
+    narrow = orthonormal(at_first, at_last, image_ref, first_ref, last_ref).astype(jnp.bfloat16)
     for i, copy in enumerate(copies):
-        u = first + i * size // UNIT
+        u = i * PART // UNIT
         chosen = narrow[u * DIRS : (u + 1) * DIRS]
         mean = mean_ref[u] - shift_ref[u]
         offset = jnp.sum(chosen.astype(jnp.float32) * mean, axis=1, keepdims=True)
         copy.wait()
-        rows = x_ref[i * size : (i + 1) * size]
-        at = first * UNIT + i * size
-        out_ref[:, at : at + size] = dot(chosen, rows, ((1,), (1,))) - offset
-
-
-def early_kernel(
-    label_ref, image_ref, first_ref, last_ref, mean_ref, shift_ref, source, narrow_ref, out_ref, x_ref, arrived
-):
-    copies = fetch(source, x_ref, arrived, 0, PART)
-    _, at_first, at_last = flags(label_ref)
-    narrow = orthonormal(at_first, at_last, image_ref, first_ref, last_ref).astype(jnp.bfloat16)
-    narrow_ref[...] = narrow
-    project_half(0, narrow, mean_ref, shift_ref, x_ref, copies, out_ref)
-
-
-def late_kernel(narrow_ref, mean_ref, shift_ref, half_ref, source, out_ref, x_ref, arrived):
-    first = mean_ref.shape[0] // 2
-    copies = fetch(source, x_ref, arrived, first * UNIT, PART)
-    out_ref[:, : half_ref.shape[1]] = half_ref[...]
-    project_half(first, narrow_ref[...], mean_ref, shift_ref, x_ref, copies, out_ref)
-
-
-def half_scratch(x):
+        rows = slice(i * PART, (i + 1) * PART)
+        out_ref[:, rows] = dot(chosen, x_ref[rows], ((1,), (1,))) - offset
+
+
+def project(labels, images, first, last_image, means, shift, x):
     rows, width = x.shape
-    return [
-        pltpu.VMEM((rows // 2, width), x.dtype),
-        pltpu.SemaphoreType.DMA((rows // 2 // PART,)),
-    ]
-
-
-def half_cost(rows, width):
-    return pl.CostEstimate(flops=rows * width * 256, bytes_accessed=rows * width, transcendentals=0)
-
-
-def project_early(labels, images, first, last_image, means, shift, x):
-    rows, width = x.shape
-    units = rows // UNIT
-    return pl.pallas_call(
-        early_kernel,
+    return pl.pallas_call(
+        project_kernel,
         in_specs=smem(1) + vmem(5) + [pl.BlockSpec(memory_space=pl.ANY)],
-        out_specs=vmem(2),
-        scratch_shapes=half_scratch(x),
-        out_shape=[
-            jax.ShapeDtypeStruct((units * DIRS, width), jnp.bfloat16),
-            jax.ShapeDtypeStruct((DIRS, units // 2 * UNIT), jnp.float32),
-        ],
-        compiler_params=pltpu.CompilerParams(vmem_limit_bytes=12 * MIB),
-        cost_estimate=half_cost(rows, width),
-        name="project_early",
+        out_specs=vmem(1)[0],
+        out_shape=jax.ShapeDtypeStruct((DIRS, rows), jnp.float32),
+        scratch_shapes=[pltpu.VMEM(x.shape, x.dtype), pltpu.SemaphoreType.DMA((rows // PART,))],
+        compiler_params=pltpu.CompilerParams(vmem_limit_bytes=24 * MIB),
+        cost_estimate=pl.CostEstimate(
+            flops=2 * rows * width * 256, bytes_accessed=2 * rows * width, transcendentals=0
+        ),
+        name="project",
     )(labels, images, first, last_image, means, shift, x)
-
-
-def project_late(narrow, means, shift, half, x):
-    rows, width = x.shape
-    return pl.pallas_call(
-        late_kernel,
-        in_specs=vmem(4) + [pl.BlockSpec(memory_space=pl.ANY)],
-        out_specs=vmem(1)[0],
-        scratch_shapes=half_scratch(x),
-        out_shape=jax.ShapeDtypeStruct((DIRS, rows), jnp.float32),
-        compiler_params=pltpu.CompilerParams(vmem_limit_bytes=12 * MIB),
-        cost_estimate=half_cost(rows, width),
-        name="project_late",
-    )(narrow, means, shift, half, x)
 
 
 def finish_kernel(kept_ref, got_ref, out_ref):
@@ -419,15 +385,18 @@
         right = right + from_right * got
     first_stats, last_stats = collect(left, right, own, mate, masks)
 
-    def exchange(ends):
-        mate, own = swap(ends), halves(ends)
+    def exchange(ends, mate=None, beside=lambda: ()):
+        mate, own = mate or swap(ends), halves(ends)
         totals = chip_totals(own, mate, joins)
+        arrived = [
+            lax.ppermute(jnp.where(up, totals[1], totals[0]), "dp", link) for link, up in zip(links, upward)
+        ]
+        arrived, other = lax.optimization_barrier((arrived, beside()))
         left = right = jnp.zeros_like(own[0])
-        for link, up, (from_left, from_right) in zip(links, upward, sides):
-            got = lax.ppermute(jnp.where(up, totals[1], totals[0]), "dp", link)
+        for got, (from_left, from_right) in zip(arrived, sides):
             left = left + from_left * got
             right = right + from_right * got
-        return collect(left, right, own, mate, masks)
+        return *collect(left, right, own, mate, masks), other
 
     def halve(tiles, bit):
         low, high = tiles[0::2], tiles[1::2]
@@ -443,20 +412,23 @@
 
     images, ends, shift = first_images(labels, first_stats, last_stats, means, start_basis, raw)
     for _ in range(ITERS - 2):
-        images, ends = step(labels, images, *exchange(ends), shift, spread)
-
-    images, ends, kept, sent = step_and_route(
-        owner_table, me, labels, images, *exchange(ends), shift, spread
+        images, ends = step(labels, images, *exchange(ends)[:2], shift, spread)
+
+    images, ends, kept = step_and_route(
+        owner_table, me, labels, images, *exchange(ends)[:2], shift, spread
     )
-    kept = kept + route(sent, 1)
-    bit = 2
+    got = lax.ppermute(ends, "dp", mates)
+    kept = (kept + got[2 * DIRS :]).reshape(n_dp // 2, DIRS, width)
+    kept, sent = halve(kept, 2)
+    first, last_image, got = exchange(ends[: 2 * DIRS], halves(got[: 2 * DIRS]), lambda: route(sent, 2))
+    kept = kept + got
+    bit = 4
     while 2 * bit < n_dp:
         kept = split(kept, bit)
         bit *= 2
     kept, sent = halve(kept, bit)
     got = route(sent, bit)
-    narrow, half = project_early(labels, images, *exchange(ends), means, shift, embeddings)
-    projections = project_late(narrow, means, shift, half, embeddings)
+    projections = project(labels, images, first, last_image, means, shift, embeddings)
     return finish(kept, got), projections
 
 

time: 129 us -> 120 us (0.930)
  Pallas kernels: 56 us -> 49.6 us
  starting transfers between devices: 34.7 us -> 30.4 us
  waiting for transfers between devices: 35.5 us -> 36.9 us
    ppermute x12 -> x13, waiting for transfers between devices: 18.4 us -> 22.8 us  [the longest x12 21.5 us: exchange(): lax.ppermute(jnp.where(up, totals[1], totals[0]), 'dp', link)]
    ppermute x4 -> x3, starting transfers between devices: 4.09 us -> 0.67 us  [route(): return lax.ppermute(sent, 'dp', [(i, i ^ bit) for i in range(n_dp)])]
    pallas_call x4, Pallas kernels: 16.4 us -> 13.1 us  [step(): pl.pallas_call(step_kernel, in_specs=smem(1) + vmem(5), out_specs=vmem(2)...]
    ppermute x14 -> x13, starting transfers between devices: 21.9 us -> 19.4 us  [swap(): return halves(lax.ppermute(both, 'dp', mates))]
    pallas_call x3 -> x2, Pallas kernels: 13.9 us -> 11.5 us  [the longest x1 8.19 us: project(): pl.pallas_call(project_kernel, in_specs=smem(1) + vmem(5) + [pl.BlockSpec...]
    ppermute x14 -> x13, waiting for transfers between devices: 12.5 us -> 10.8 us  [swap(): return halves(lax.ppermute(both, 'dp', mates))]
    ppermute x12 -> x13, starting transfers between devices: 4.26 us -> 5.89 us  [the longest x12 5.47 us: exchange(): lax.ppermute(jnp.where(up, totals[1], totals[0]), 'dp', link)]
    ppermute x4 -> x3, waiting for transfers between devices: 4.64 us -> 3.28 us  [route(): return lax.ppermute(sent, 'dp', [(i, i ^ bit) for i in range(n_dp)])]
  transfers between devices with their start and end apart: 32 -> 31, of which waited for: 27 -> 25; matrix products, arithmetic and copies ran while one was open for 0% -> 0% of each run, Pallas kernels for 20% -> 21%
where the time goes in v4:
time: 120 us; the launch traced here: 119 us
  Pallas kernels  49.6 us (41%)
  waiting for transfers between devices  36.9 us (31%)
  starting transfers between devices  30.4 us (25%)
    ppermute x12, waiting for transfers between devices, exchange(): lax.ppermute(jnp.where(up, totals[1], totals[0]), 'dp', link)  21.5 us
    ppermute x13, starting transfers between devices, swap(): return halves(lax.ppermute(both, 'dp', mates))  19.4 us
    pallas_call x1, Pallas kernels, unit_spread(): pl.pallas_call(spread_kernel, grid=(units,), in_specs=[pl.BlockSpec((UNIT...  16.6 us
    pallas_call x4, Pallas kernels, step(): pl.pallas_call(step_kernel, in_specs=smem(1) + vmem(5), out_specs=vmem(2)...  13.1 us
    ppermute x13, waiting for transfers between devices, swap(): return halves(lax.ppermute(both, 'dp', mates))  10.8 us
    pallas_call x1, Pallas kernels, project(): pl.pallas_call(project_kernel, in_specs=smem(1) + vmem(5) + [pl.BlockSpec...  8.19 us
    pallas_call x1, Pallas kernels, unit_means(): pl.pallas_call(means_kernel, in_specs=smem(1) + [pl.BlockSpec(memory_spac...  6.7 us
    ppermute x12, starting transfers between devices, exchange(): lax.ppermute(jnp.where(up, totals[1], totals[0]), 'dp', link)  5.47 us
  transfers between devices with their start and end apart: 31, of which 25 were waited for; matrix products, arithmetic and copies ran while one was open for 0% of the time, Pallas kernels for 21%

profile of v4, /device:TPU:0, one launch (start us, length us, event | category | flops | bytes accessed | tf_op | source)
XLA Modules:
  0.0 119.4 jit_solution(4941899429271798185)
XLA Ops:
  1.5 6.7 %unit_means.1 = (f32[4,1,1024]{2,1,0:T(1,128)S(1)}, f32[16,1024]{1,0:T(8,128)S(1)}) custom-call(s32[4]{0:T(128)S(1)} %slice.182.label_ref, bf16[8192,1024]{1,0:T(8,128)(2,1)} %source.3), custom_call_target="tpu_custom_call" | custom-call | tf_op jit(solution)/shard_map/unit_means/pallas_call | solution.py:60
  9.7 2.9 %collective-permute-start.1 = (f32[8,1024]{1,0:T(8,128)S(1)}, f32[8,1024]{1,0:T(8,128)S(1)}, u32[]{:S(2)}, u32[]{:S(2)}) collective-permute-start(f32[8,1024]{1,0:T(8,128)S(1)} %get-tuple-element.79), channel_id=1, source_target_pairs={{0,2},{1,15},{2,0},{3,5},{4,6},{5,3},{6,4},{7,9},{8,10},{9,7},{10,... | collective-permute-start | bytes 98312 | tf_op jit(solution)/shard_map/ppermute | solution.py:374
  12.6 1.6 %collective-permute-start.2 = (f32[8,1024]{1,0:T(8,128)S(1)}, f32[8,1024]{1,0:T(8,128)S(1)}, u32[]{:S(2)}, u32[]{:S(2)}) collective-permute-start(f32[8,1024]{1,0:T(8,128)S(1)} %get-tuple-element.78), channel_id=1, source_target_pairs={{0,4},{1,13},{2,6},{3,15},{4,0},{5,9},{6,2},{7,11},{8,12},{9,5},{1... | collective-permute-start | bytes 98312 | tf_op jit(solution)/shard_map/ppermute | solution.py:374
  14.2 16.6 %unit_spread.1 = (bf16[2,4,1024,1024]{3,2,1,0:T(8,128)(2,1)S(1)}, f32[4,8,1024]{2,1,0:T(8,128)S(1)}) custom-call(bf16[8192,1024]{1,0:T(8,128)(2,1)} %source.3, f32[4,1,1024]{2,1,0:T(1,128)S(1)} %get-tuple-element.37.mean_ref.means_ref, f32[8,1024]{1,0:T(8,128)S(1)} %copy-done), custom_call_target="tpu_custom_call" | custom-call | tf_op jit(solution)/shard_map/unit_spread/pallas_call | solution.py:97
  30.9 1.6 %collective-permute-start.3 = (f32[16,1024]{1,0:T(8,128)S(1)}, f32[16,1024]{1,0:T(8,128)S(1)}, u32[]{:S(2)}, u32[]{:S(2)}) collective-permute-start(f32[16,1024]{1,0:T(8,128)S(1)} %pad_maximum_fusion), channel_id=1, source_target_pairs={{0,1},{1,0},{2,3},{3,2},{4,5},{5,4},{6,7},{7,6},{8,9},{9,8},{10,11... | collective-permute-start | bytes 196616 | tf_op jit(solution)/shard_map/ppermute | solution.py:337
  32.5 0.9 collective-permute-done.3
  34.5 0.9 collective-permute-done.4
  36.7 2.7 %collective-permute-done.5 = f32[8,1024]{1,0:T(8,128)S(1)} collective-permute-done((f32[8,1024]{1,0:T(8,128)S(1)}, f32[8,1024]{1,0:T(8,128)S(1)}, u32[]{:S(2)}, u32[]{:S(2)}) %collective-permute-start.5) | collective-permute-done | bytes 32800 | tf_op jit(solution)/shard_map/ppermute | solution.py:392
  39.9 1.6 %collective-permute-start.7 = (f32[16,1024]{1,0:T(8,128)S(1)}, f32[16,1024]{1,0:T(8,128)S(1)}, u32[]{:S(2)}, u32[]{:S(2)}) collective-permute-start(f32[16,1024]{1,0:T(8,128)S(1)} %pad_maximum_fusion.1), channel_id=1, source_target_pairs={{0,1},{1,0},{2,3},{3,2},{4,5},{5,4},{6,7},{7,6},{8,9},{9,8},{10,11... | collective-permute-start | bytes 196616 | tf_op jit(solution)/shard_map/ppermute | solution.py:337
  42.5 3.2 %step.4 = (f32[4,8,1024]{2,1,0:T(8,128)S(1)}, f32[16,1024]{1,0:T(8,128)S(1)}) custom-call(s32[4]{0:T(128)S(1)} %slice.182.label_ref, f32[4,8,1024]{2,1,0:T(8,128)S(1)} %get-tuple-element.42.image_ref, f32[8,1024]{1,0:T(8,128)S(1)} %get-tuple-element.99.first_ref, f32[8,1024]{1,0:T(8,128)S(1)} %get-tuple-element.98.last_ref, ...), custom_call_target="tpu_custom_call" | custom-call | tf_op jit(solution)/shard_map/step/pallas_call | solution.py:242
  47.1 1.7 %collective-permute-start.9 = (f32[8,1024]{1,0:T(8,128)S(1)}, f32[8,1024]{1,0:T(8,128)S(1)}, u32[]{:S(2)}, u32[]{:S(2)}) collective-permute-start(f32[8,1024]{1,0:T(8,128)S(1)} %get-tuple-element.87), channel_id=1, source_target_pairs={{0,2},{1,15},{2,0},{3,5},{4,6},{5,3},{6,4},{7,9},{8,10},{9,7},{10,... | collective-permute-start | bytes 98312 | tf_op jit(solution)/shard_map/ppermute | solution.py:392
  48.8 2.2 %collective-permute-done.10 = f32[8,1024]{1,0:T(8,128)S(1)} collective-permute-done((f32[8,1024]{1,0:T(8,128)S(1)}, f32[8,1024]{1,0:T(8,128)S(1)}, u32[]{:S(2)}, u32[]{:S(2)}) %collective-permute-start.10) | collective-permute-done | bytes 32800 | tf_op jit(solution)/shard_map/ppermute | solution.py:392
  51.1 4.0 %collective-permute-start.11 = (f32[16,1024]{1,0:T(8,128)S(1)}, f32[16,1024]{1,0:T(8,128)S(1)}, u32[]{:S(2)}, u32[]{:S(2)}) collective-permute-start(f32[16,1024]{1,0:T(8,128)S(1)} %pad_maximum_fusion.2), channel_id=1, source_target_pairs={{0,1},{1,0},{2,3},{3,2},{4,5},{5,4},{6,7},{7,6},{8,9},{9,8},{10,11... | collective-permute-start | bytes 196616 | tf_op jit(solution)/shard_map/ppermute | solution.py:337
  56.1 3.2 %step.5 = (f32[4,8,1024]{2,1,0:T(8,128)S(1)}, f32[16,1024]{1,0:T(8,128)S(1)}) custom-call(s32[4]{0:T(128)S(1)} %slice.182.label_ref, f32[4,8,1024]{2,1,0:T(8,128)S(1)} %get-tuple-element.48.image_ref, f32[8,1024]{1,0:T(8,128)S(1)} %get-tuple-element.97.first_ref, f32[8,1024]{1,0:T(8,128)S(1)} %get-tuple-element.96.last_ref, ...), custom_call_target="tpu_custom_call" | custom-call | tf_op jit(solution)/shard_map/step/pallas_call | solution.py:242
  60.8 3.8 %collective-permute-done.13 = f32[8,1024]{1,0:T(8,128)S(1)} collective-permute-done((f32[8,1024]{1,0:T(8,128)S(1)}, f32[8,1024]{1,0:T(8,128)S(1)}, u32[]{:S(2)}, u32[]{:S(2)}) %collective-permute-start.13) | collective-permute-done | bytes 32800 | tf_op jit(solution)/shard_map/ppermute | solution.py:392
  64.8 2.4 %collective-permute-start.15 = (f32[16,1024]{1,0:T(8,128)S(1)}, f32[16,1024]{1,0:T(8,128)S(1)}, u32[]{:S(2)}, u32[]{:S(2)}) collective-permute-start(f32[16,1024]{1,0:T(8,128)S(1)} %pad_maximum_fusion.3), channel_id=1, source_target_pairs={{0,1},{1,0},{2,3},{3,2},{4,5},{5,4},{6,7},{7,6},{8,9},{9,8},{10,11... | collective-permute-start | bytes 196616 | tf_op jit(solution)/shard_map/ppermute | solution.py:337
  68.1 3.2 %step.6 = (f32[4,8,1024]{2,1,0:T(8,128)S(1)}, f32[16,1024]{1,0:T(8,128)S(1)}) custom-call(s32[4]{0:T(128)S(1)} %slice.182.label_ref, f32[4,8,1024]{2,1,0:T(8,128)S(1)} %get-tuple-element.52.image_ref, f32[8,1024]{1,0:T(8,128)S(1)} %get-tuple-element.95.first_ref, f32[8,1024]{1,0:T(8,128)S(1)} %get-tuple-element.94.last_ref, ...), custom_call_target="tpu_custom_call" | custom-call | tf_op jit(solution)/shard_map/step/pallas_call | solution.py:242
  73.1 3.5 %collective-permute-done.17 = f32[8,1024]{1,0:T(8,128)S(1)} collective-permute-done((f32[8,1024]{1,0:T(8,128)S(1)}, f32[8,1024]{1,0:T(8,128)S(1)}, u32[]{:S(2)}, u32[]{:S(2)}) %collective-permute-start.17) | collective-permute-done | bytes 32800 | tf_op jit(solution)/shard_map/ppermute | solution.py:392
  77.1 3.4 %collective-permute-start.19 = (f32[16,1024]{1,0:T(8,128)S(1)}, f32[16,1024]{1,0:T(8,128)S(1)}, u32[]{:S(2)}, u32[]{:S(2)}) collective-permute-start(f32[16,1024]{1,0:T(8,128)S(1)} %pad_maximum_fusion.4), channel_id=1, source_target_pairs={{0,1},{1,0},{2,3},{3,2},{4,5},{5,4},{6,7},{7,6},{8,9},{9,8},{10,11... | collective-permute-start | bytes 196616 | tf_op jit(solution)/shard_map/ppermute | solution.py:337
  80.5 0.9 collective-permute-done.19
  81.4 3.4 %step.7 = (f32[4,8,1024]{2,1,0:T(8,128)S(1)}, f32[16,1024]{1,0:T(8,128)S(1)}) custom-call(s32[4]{0:T(128)S(1)} %slice.182.label_ref, f32[4,8,1024]{2,1,0:T(8,128)S(1)} %get-tuple-element.56.image_ref, f32[8,1024]{1,0:T(8,128)S(1)} %get-tuple-element.93.first_ref, f32[8,1024]{1,0:T(8,128)S(1)} %get-tuple-element.92.last_ref, ...), custom_call_target="tpu_custom_call" | custom-call | tf_op jit(solution)/shard_map/step/pallas_call | solution.py:242
  85.3 0.9 collective-permute-done.20
  86.4 3.8 %collective-permute-done.21 = f32[8,1024]{1,0:T(8,128)S(1)} collective-permute-done((f32[8,1024]{1,0:T(8,128)S(1)}, f32[8,1024]{1,0:T(8,128)S(1)}, u32[]{:S(2)}, u32[]{:S(2)}) %collective-permute-start.21) | collective-permute-done | bytes 32800 | tf_op jit(solution)/shard_map/ppermute | solution.py:392
  90.3 2.4 %collective-permute-start.23 = (f32[16,1024]{1,0:T(8,128)S(1)}, f32[16,1024]{1,0:T(8,128)S(1)}, u32[]{:S(2)}, u32[]{:S(2)}) collective-permute-start(f32[16,1024]{1,0:T(8,128)S(1)} %pad_maximum_fusion.5), channel_id=1, source_target_pairs={{0,1},{1,0},{2,3},{3,2},{4,5},{5,4},{6,7},{7,6},{8,9},{9,8},{10,11... | collective-permute-start | bytes 196616 | tf_op jit(solution)/shard_map/ppermute | solution.py:337
  93.6 3.3 %step_and_route.1 = (f32[4,8,1024]{2,1,0:T(8,128)S(1)}, f32[80,1024]{1,0:T(8,128)S(1)}, f32[64,1024]{1,0:T(8,128)S(1)}) custom-call(s32[16]{0:T(128)S(1)} %copy-done.1, s32[1]{0:T(128)} %bitcast.me_ref, s32[4]{0:T(128)S(1)} %slice.182.label_ref, f32[4,8,1024]{2,1,0:T(8,128)S(1)} %get-tuple-element.60.refs_0_, f32[8,1024]{1,0:T(8,128)S(1)} %get-tuple-element.91.refs_1_, ...), custom_call_target="tpu_custom_call" | custom-call | tf_op jit(solution)/shard_map/step_and_route/pallas_call | solution.py:258
  97.4 1.3 %collective-permute-done.24 = f32[80,1024]{1,0:T(8,128)S(1)} collective-permute-done((f32[80,1024]{1,0:T(8,128)S(1)}, f32[80,1024]{1,0:T(8,128)S(1)}, u32[]{:S(2)}, u32[]{:S(2)}) %collective-permute-start.24) | collective-permute-done | bytes 327712 | tf_op jit(solution)/shard_map/ppermute | solution.py:420
  99.2 1.7 %collective-permute-start.25 = (f32[8,1024]{1,0:T(8,128)S(1)}, f32[8,1024]{1,0:T(8,128)S(1)}, u32[]{:S(2)}, u32[]{:S(2)}) collective-permute-start(f32[8,1024]{1,0:T(8,128)S(1)} %get-tuple-element.75), channel_id=1, source_target_pairs={{0,2},{1,15},{2,0},{3,5},{4,6},{5,3},{6,4},{7,9},{8,10},{9,7},{10,... | collective-permute-start | bytes 98312 | tf_op jit(solution)/shard_map/ppermute | solution.py:392
  100.9 4.3 %collective-permute-done.25 = f32[8,1024]{1,0:T(8,128)S(1)} collective-permute-done((f32[8,1024]{1,0:T(8,128)S(1)}, f32[8,1024]{1,0:T(8,128)S(1)}, u32[]{:S(2)}, u32[]{:S(2)}) %collective-permute-start.25) | collective-permute-done | bytes 32800 | tf_op jit(solution)/shard_map/ppermute | solution.py:392
  105.4 1.4 %collective-permute-start.30 = (f32[16,1024]{1,0:T(8,128)S(1)}, f32[16,1024]{1,0:T(8,128)S(1)}, u32[]{:S(2)}, u32[]{:S(2)}) collective-permute-start(f32[16,1024]{1,0:T(8,128)S(1)} %pad_maximum_fusion.6), channel_id=1, source_target_pairs={{0,1},{1,0},{2,3},{3,2},{4,5},{5,4},{6,7},{7,6},{8,9},{9,8},{10,11... | collective-permute-start | bytes 196616 | tf_op jit(solution)/shard_map/ppermute | solution.py:337
  106.8 3.3 %collective-permute-done.28 = f32[2,8,1024]{2,1,0:T(8,128)S(1)} collective-permute-done((f32[2,8,1024]{2,1,0:T(8,128)S(1)}, f32[2,8,1024]{2,1,0:T(8,128)S(1)}, u32[]{:S(2)}, u32[]{:S(2)}) %collective-permute-start.28) | collective-permute-done | bytes 65568 | tf_op jit(solution)/shard_map/ppermute | solution.py:407
  110.3 8.2 %project.1 = f32[8,8192]{1,0:T(8,128)} custom-call(s32[4]{0:T(128)S(1)} %slice.182.label_ref, f32[4,8,1024]{2,1,0:T(8,128)S(1)} %get-tuple-element.67.image_ref, f32[8,1024]{1,0:T(8,128)S(1)} %get-tuple-element.77.first_ref, f32[8,1024]{1,0:T(8,128)S(1)} %get-tuple-element.76.last_ref, f32[4,1,1024]{2,1,0:T(1,128)S(1)} %get-tuple-element.37.mean_ref.means_ref, ...), custom_call_target="tpu_custom_call" | custom-call | flops 4294967296 | bytes 16777216 | tf_op jit(solution)/shard_map/project/pallas_call | solution.py:286
  118.5 1.0 finish.1
  (82 shorter events, 16.4 us)
Async XLA Ops:
  8.2 1.4 %collective-permute-start = (f32[16,1024]{1,0:T(8,128)S(1)}, f32[16,1024]{1,0:T(8,128)S(1)}, u32[]{:S(2)}, u32[]{:S(2)}) collective-permute-start(f32[16,1024]{1,0:T(8,128)S(1)} %get-tuple-element.36), channel_id=1, source_target_pairs={{0,1},{1,0},{2,3},{3,2},{4,5},{5,4},{6,7},{7,6},{8,9},{9,8},{10,11... | collective-permute-start | bytes 196616 | tf_op jit(solution)/shard_map/ppermute | solution.py:337
  9.7 21.1 %collective-permute-start.1 = (f32[8,1024]{1,0:T(8,128)S(1)}, f32[8,1024]{1,0:T(8,128)S(1)}, u32[]{:S(2)}, u32[]{:S(2)}) collective-permute-start(f32[8,1024]{1,0:T(8,128)S(1)} %get-tuple-element.79), channel_id=1, source_target_pairs={{0,2},{1,15},{2,0},{3,5},{4,6},{5,3},{6,4},{7,9},{8,10},{9,7},{10,... | collective-permute-start | bytes 98312 | tf_op jit(solution)/shard_map/ppermute | solution.py:374
  12.6 18.2 %collective-permute-start.2 = (f32[8,1024]{1,0:T(8,128)S(1)}, f32[8,1024]{1,0:T(8,128)S(1)}, u32[]{:S(2)}, u32[]{:S(2)}) collective-permute-start(f32[8,1024]{1,0:T(8,128)S(1)} %get-tuple-element.78), channel_id=1, source_target_pairs={{0,4},{1,13},{2,6},{3,15},{4,0},{5,9},{6,2},{7,11},{8,12},{9,5},{1... | collective-permute-start | bytes 98312 | tf_op jit(solution)/shard_map/ppermute | solution.py:374
  30.9 2.5 %collective-permute-start.3 = (f32[16,1024]{1,0:T(8,128)S(1)}, f32[16,1024]{1,0:T(8,128)S(1)}, u32[]{:S(2)}, u32[]{:S(2)}) collective-permute-start(f32[16,1024]{1,0:T(8,128)S(1)} %pad_maximum_fusion), channel_id=1, source_target_pairs={{0,1},{1,0},{2,3},{3,2},{4,5},{5,4},{6,7},{7,6},{8,9},{9,8},{10,11... | collective-permute-start | bytes 196616 | tf_op jit(solution)/shard_map/ppermute | solution.py:337
  34.1 1.3 %collective-permute-start.4 = (f32[16,1024]{1,0:T(8,128)S(1)}, f32[16,1024]{1,0:T(8,128)S(1)}, u32[]{:S(2)}, u32[]{:S(2)}) collective-permute-start(f32[16,1024]{1,0:T(8,128)S(1)} %get-tuple-element.43), channel_id=1, source_target_pairs={{0,1},{1,0},{2,3},{3,2},{4,5},{5,4},{6,7},{7,6},{8,9},{9,8},{10,11... | collective-permute-start | bytes 196616 | tf_op jit(solution)/shard_map/ppermute | solution.py:337
  35.4 4.0 %collective-permute-start.5 = (f32[8,1024]{1,0:T(8,128)S(1)}, f32[8,1024]{1,0:T(8,128)S(1)}, u32[]{:S(2)}, u32[]{:S(2)}) collective-permute-start(f32[8,1024]{1,0:T(8,128)S(1)} %get-tuple-element.89), channel_id=1, source_target_pairs={{0,2},{1,15},{2,0},{3,5},{4,6},{5,3},{6,4},{7,9},{8,10},{9,7},{10,... | collective-permute-start | bytes 98312 | tf_op jit(solution)/shard_map/ppermute | solution.py:392
  36.0 3.9 %collective-permute-start.6 = (f32[8,1024]{1,0:T(8,128)S(1)}, f32[8,1024]{1,0:T(8,128)S(1)}, u32[]{:S(2)}, u32[]{:S(2)}) collective-permute-start(f32[8,1024]{1,0:T(8,128)S(1)} %get-tuple-element.88), channel_id=1, source_target_pairs={{0,4},{1,13},{2,6},{3,15},{4,0},{5,9},{6,2},{7,11},{8,12},{9,5},{1... | collective-permute-start | bytes 98312 | tf_op jit(solution)/shard_map/ppermute | solution.py:392
  39.9 2.5 %collective-permute-start.7 = (f32[16,1024]{1,0:T(8,128)S(1)}, f32[16,1024]{1,0:T(8,128)S(1)}, u32[]{:S(2)}, u32[]{:S(2)}) collective-permute-start(f32[16,1024]{1,0:T(8,128)S(1)} %pad_maximum_fusion.1), channel_id=1, source_target_pairs={{0,1},{1,0},{2,3},{3,2},{4,5},{5,4},{6,7},{7,6},{8,9},{9,8},{10,11... | collective-permute-start | bytes 196616 | tf_op jit(solution)/shard_map/ppermute | solution.py:337
  45.7 1.3 %collective-permute-start.8 = (f32[16,1024]{1,0:T(8,128)S(1)}, f32[16,1024]{1,0:T(8,128)S(1)}, u32[]{:S(2)}, u32[]{:S(2)}) collective-permute-start(f32[16,1024]{1,0:T(8,128)S(1)} %get-tuple-element.49), channel_id=1, source_target_pairs={{0,1},{1,0},{2,3},{3,2},{4,5},{5,4},{6,7},{7,6},{8,9},{9,8},{10,11... | collective-permute-start | bytes 196616 | tf_op jit(solution)/shard_map/ppermute | solution.py:337
  47.0 4.0 %collective-permute-start.10 = (f32[8,1024]{1,0:T(8,128)S(1)}, f32[8,1024]{1,0:T(8,128)S(1)}, u32[]{:S(2)}, u32[]{:S(2)}) collective-permute-start(f32[8,1024]{1,0:T(8,128)S(1)} %get-tuple-element.86), channel_id=1, source_target_pairs={{0,4},{1,13},{2,6},{3,15},{4,0},{5,9},{6,2},{7,11},{8,12},{9,5},{1... | collective-permute-start | bytes 98312 | tf_op jit(solution)/shard_map/ppermute | solution.py:392
  47.1 4.0 %collective-permute-start.9 = (f32[8,1024]{1,0:T(8,128)S(1)}, f32[8,1024]{1,0:T(8,128)S(1)}, u32[]{:S(2)}, u32[]{:S(2)}) collective-permute-start(f32[8,1024]{1,0:T(8,128)S(1)} %get-tuple-element.87), channel_id=1, source_target_pairs={{0,2},{1,15},{2,0},{3,5},{4,6},{5,3},{6,4},{7,9},{8,10},{9,7},{10,... | collective-permute-start | bytes 98312 | tf_op jit(solution)/shard_map/ppermute | solution.py:392
  51.1 4.9 %collective-permute-start.11 = (f32[16,1024]{1,0:T(8,128)S(1)}, f32[16,1024]{1,0:T(8,128)S(1)}, u32[]{:S(2)}, u32[]{:S(2)}) collective-permute-start(f32[16,1024]{1,0:T(8,128)S(1)} %pad_maximum_fusion.2), channel_id=1, source_target_pairs={{0,1},{1,0},{2,3},{3,2},{4,5},{5,4},{6,7},{7,6},{8,9},{9,8},{10,11... | collective-permute-start | bytes 196616 | tf_op jit(solution)/shard_map/ppermute | solution.py:337
  59.3 1.3 %collective-permute-start.12 = (f32[16,1024]{1,0:T(8,128)S(1)}, f32[16,1024]{1,0:T(8,128)S(1)}, u32[]{:S(2)}, u32[]{:S(2)}) collective-permute-start(f32[16,1024]{1,0:T(8,128)S(1)} %get-tuple-element.53), channel_id=1, source_target_pairs={{0,1},{1,0},{2,3},{3,2},{4,5},{5,4},{6,7},{7,6},{8,9},{9,8},{10,11... | collective-permute-start | bytes 196616 | tf_op jit(solution)/shard_map/ppermute | solution.py:337
  60.7 4.0 %collective-permute-start.13 = (f32[8,1024]{1,0:T(8,128)S(1)}, f32[8,1024]{1,0:T(8,128)S(1)}, u32[]{:S(2)}, u32[]{:S(2)}) collective-permute-start(f32[8,1024]{1,0:T(8,128)S(1)} %get-tuple-element.85), channel_id=1, source_target_pairs={{0,2},{1,15},{2,0},{3,5},{4,6},{5,3},{6,4},{7,9},{8,10},{9,7},{10,... | collective-permute-start | bytes 98312 | tf_op jit(solution)/shard_map/ppermute | solution.py:392
  60.7 4.0 %collective-permute-start.14 = (f32[8,1024]{1,0:T(8,128)S(1)}, f32[8,1024]{1,0:T(8,128)S(1)}, u32[]{:S(2)}, u32[]{:S(2)}) collective-permute-start(f32[8,1024]{1,0:T(8,128)S(1)} %get-tuple-element.84), channel_id=1, source_target_pairs={{0,4},{1,13},{2,6},{3,15},{4,0},{5,9},{6,2},{7,11},{8,12},{9,5},{1... | collective-permute-start | bytes 98312 | tf_op jit(solution)/shard_map/ppermute | solution.py:392
  64.8 3.3 %collective-permute-start.15 = (f32[16,1024]{1,0:T(8,128)S(1)}, f32[16,1024]{1,0:T(8,128)S(1)}, u32[]{:S(2)}, u32[]{:S(2)}) collective-permute-start(f32[16,1024]{1,0:T(8,128)S(1)} %pad_maximum_fusion.3), channel_id=1, source_target_pairs={{0,1},{1,0},{2,3},{3,2},{4,5},{5,4},{6,7},{7,6},{8,9},{9,8},{10,11... | collective-permute-start | bytes 196616 | tf_op jit(solution)/shard_map/ppermute | solution.py:337
  68.1 25.5 %copy-start.1 = (s32[16]{0:T(128)S(1)}, s32[16]{0:T(128)}, u32[]{:S(2)}) copy-start(s32[16]{0:T(128)} %owner_ref.1) | copy-start | bytes 196
  71.3 1.3 %collective-permute-start.16 = (f32[16,1024]{1,0:T(8,128)S(1)}, f32[16,1024]{1,0:T(8,128)S(1)}, u32[]{:S(2)}, u32[]{:S(2)}) collective-permute-start(f32[16,1024]{1,0:T(8,128)S(1)} %get-tuple-element.57), channel_id=1, source_target_pairs={{0,1},{1,0},{2,3},{3,2},{4,5},{5,4},{6,7},{7,6},{8,9},{9,8},{10,11... | collective-permute-start | bytes 196616 | tf_op jit(solution)/shard_map/ppermute | solution.py:337
  72.7 4.0 %collective-permute-start.17 = (f32[8,1024]{1,0:T(8,128)S(1)}, f32[8,1024]{1,0:T(8,128)S(1)}, u32[]{:S(2)}, u32[]{:S(2)}) collective-permute-start(f32[8,1024]{1,0:T(8,128)S(1)} %get-tuple-element.83), channel_id=1, source_target_pairs={{0,2},{1,15},{2,0},{3,5},{4,6},{5,3},{6,4},{7,9},{8,10},{9,7},{10,... | collective-permute-start | bytes 98312 | tf_op jit(solution)/shard_map/ppermute | solution.py:392
  73.1 3.9 %collective-permute-start.18 = (f32[8,1024]{1,0:T(8,128)S(1)}, f32[8,1024]{1,0:T(8,128)S(1)}, u32[]{:S(2)}, u32[]{:S(2)}) collective-permute-start(f32[8,1024]{1,0:T(8,128)S(1)} %get-tuple-element.82), channel_id=1, source_target_pairs={{0,4},{1,13},{2,6},{3,15},{4,0},{5,9},{6,2},{7,11},{8,12},{9,5},{1... | collective-permute-start | bytes 98312 | tf_op jit(solution)/shard_map/ppermute | solution.py:392
  77.1 4.3 %collective-permute-start.19 = (f32[16,1024]{1,0:T(8,128)S(1)}, f32[16,1024]{1,0:T(8,128)S(1)}, u32[]{:S(2)}, u32[]{:S(2)}) collective-permute-start(f32[16,1024]{1,0:T(8,128)S(1)} %pad_maximum_fusion.4), channel_id=1, source_target_pairs={{0,1},{1,0},{2,3},{3,2},{4,5},{5,4},{6,7},{7,6},{8,9},{9,8},{10,11... | collective-permute-start | bytes 196616 | tf_op jit(solution)/shard_map/ppermute | solution.py:337
  84.9 1.3 %collective-permute-start.20 = (f32[16,1024]{1,0:T(8,128)S(1)}, f32[16,1024]{1,0:T(8,128)S(1)}, u32[]{:S(2)}, u32[]{:S(2)}) collective-permute-start(f32[16,1024]{1,0:T(8,128)S(1)} %get-tuple-element.61), channel_id=1, source_target_pairs={{0,1},{1,0},{2,3},{3,2},{4,5},{5,4},{6,7},{7,6},{8,9},{9,8},{10,11... | collective-permute-start | bytes 196616 | tf_op jit(solution)/shard_map/ppermute | solution.py:337
  86.2 4.0 %collective-permute-start.21 = (f32[8,1024]{1,0:T(8,128)S(1)}, f32[8,1024]{1,0:T(8,128)S(1)}, u32[]{:S(2)}, u32[]{:S(2)}) collective-permute-start(f32[8,1024]{1,0:T(8,128)S(1)} %get-tuple-element.81), channel_id=1, source_target_pairs={{0,2},{1,15},{2,0},{3,5},{4,6},{5,3},{6,4},{7,9},{8,10},{9,7},{10,... | collective-permute-start | bytes 98312 | tf_op jit(solution)/shard_map/ppermute | solution.py:392
  86.3 4.0 %collective-permute-start.22 = (f32[8,1024]{1,0:T(8,128)S(1)}, f32[8,1024]{1,0:T(8,128)S(1)}, u32[]{:S(2)}, u32[]{:S(2)}) collective-permute-start(f32[8,1024]{1,0:T(8,128)S(1)} %get-tuple-element.80), channel_id=1, source_target_pairs={{0,4},{1,13},{2,6},{3,15},{4,0},{5,9},{6,2},{7,11},{8,12},{9,5},{1... | collective-permute-start | bytes 98312 | tf_op jit(solution)/shard_map/ppermute | solution.py:392
  90.3 3.3 %collective-permute-start.23 = (f32[16,1024]{1,0:T(8,128)S(1)}, f32[16,1024]{1,0:T(8,128)S(1)}, u32[]{:S(2)}, u32[]{:S(2)}) collective-permute-start(f32[16,1024]{1,0:T(8,128)S(1)} %pad_maximum_fusion.5), channel_id=1, source_target_pairs={{0,1},{1,0},{2,3},{3,2},{4,5},{5,4},{6,7},{7,6},{8,9},{9,8},{10,11... | collective-permute-start | bytes 196616 | tf_op jit(solution)/shard_map/ppermute | solution.py:337
  96.9 1.7 %collective-permute-start.24 = (f32[80,1024]{1,0:T(8,128)S(1)}, f32[80,1024]{1,0:T(8,128)S(1)}, u32[]{:S(2)}, u32[]{:S(2)}) collective-permute-start(f32[80,1024]{1,0:T(8,128)S(1)} %get-tuple-element.65), channel_id=1, source_target_pairs={{0,1},{1,0},{2,3},{3,2},{4,5},{5,4},{6,7},{7,6},{8,9},{9,8},{10,11... | collective-permute-start | bytes 983048 | tf_op jit(solution)/shard_map/ppermute | solution.py:420
  98.7 6.5 %collective-permute-start.27 = (f32[4,8,1024]{2,1,0:T(8,128)S(1)}, f32[4,8,1024]{2,1,0:T(8,128)S(1)}, u32[]{:S(2)}, u32[]{:S(2)}) collective-permute-start(f32[4,8,1024]{2,1,0:T(8,128)S(1)} %slice_select_fusion), channel_id=1, source_target_pairs={{0,2},{1,3},{2,0},{3,1},{4,6},{5,7},{6,4},{7,5},{8,10},{9,11},{10,... | collective-permute-start | bytes 393224 | tf_op jit(solution)/shard_map/ppermute | solution.py:407
  99.2 6.0 %collective-permute-start.25 = (f32[8,1024]{1,0:T(8,128)S(1)}, f32[8,1024]{1,0:T(8,128)S(1)}, u32[]{:S(2)}, u32[]{:S(2)}) collective-permute-start(f32[8,1024]{1,0:T(8,128)S(1)} %get-tuple-element.75), channel_id=1, source_target_pairs={{0,2},{1,15},{2,0},{3,5},{4,6},{5,3},{6,4},{7,9},{8,10},{9,7},{10,... | collective-permute-start | bytes 98312 | tf_op jit(solution)/shard_map/ppermute | solution.py:392
  100.9 4.3 %collective-permute-start.26 = (f32[8,1024]{1,0:T(8,128)S(1)}, f32[8,1024]{1,0:T(8,128)S(1)}, u32[]{:S(2)}, u32[]{:S(2)}) collective-permute-start(f32[8,1024]{1,0:T(8,128)S(1)} %get-tuple-element.74), channel_id=1, source_target_pairs={{0,4},{1,13},{2,6},{3,15},{4,0},{5,9},{6,2},{7,11},{8,12},{9,5},{1... | collective-permute-start | bytes 98312 | tf_op jit(solution)/shard_map/ppermute | solution.py:392
  105.3 4.8 %collective-permute-start.28 = (f32[2,8,1024]{2,1,0:T(8,128)S(1)}, f32[2,8,1024]{2,1,0:T(8,128)S(1)}, u32[]{:S(2)}, u32[]{:S(2)}) collective-permute-start(f32[2,8,1024]{2,1,0:T(8,128)S(1)} %slice_select_fusion.1), channel_id=1, source_target_pairs={{0,4},{1,5},{2,6},{3,7},{4,0},{5,1},{6,2},{7,3},{8,12},{9,13},{10,... | collective-permute-start | bytes 196616 | tf_op jit(solution)/shard_map/ppermute | solution.py:407
  105.4 4.8 %collective-permute-start.30 = (f32[16,1024]{1,0:T(8,128)S(1)}, f32[16,1024]{1,0:T(8,128)S(1)}, u32[]{:S(2)}, u32[]{:S(2)}) collective-permute-start(f32[16,1024]{1,0:T(8,128)S(1)} %pad_maximum_fusion.6), channel_id=1, source_target_pairs={{0,1},{1,0},{2,3},{3,2},{4,5},{5,4},{6,7},{7,6},{8,9},{9,8},{10,11... | collective-permute-start | bytes 196616 | tf_op jit(solution)/shard_map/ppermute | solution.py:337
  110.1 8.4 %collective-permute-start.29 = (f32[1,8,1024]{2,1,0:T(8,128)S(1)}, f32[1,8,1024]{2,1,0:T(8,128)S(1)}, u32[]{:S(2)}, u32[]{:S(2)}) collective-permute-start(f32[1,8,1024]{2,1,0:T(8,128)S(1)} %get-tuple-element.112), channel_id=1, source_target_pairs={{0,8},{1,9},{2,10},{3,11},{4,12},{5,13},{6,14},{7,15},{8,0},{9,1},... | collective-permute-start | bytes 98312 | tf_op jit(solution)/shard_map/ppermute | solution.py:407
  (1 other events, 13.6 us)

commit v5 on v4

--- a/solution.py
+++ b/solution.py
@@ -12,7 +12,6 @@
 UNIT = 2048
 HIGHEST = lax.Precision.HIGHEST
 BLOCK = 256
-CHUNKS = 16
 PART = 1024
 MIB = 1024 * 1024
 
@@ -32,85 +31,80 @@
     return copies
 
 
-def means_kernel(label_ref, source, means_ref, ends_ref, x_ref, arrived):
-    units = means_ref.shape[0]
-    size = x_ref.shape[0] // CHUNKS
-    copies = fetch(source, x_ref, arrived, 0, size)
-    for i in range(CHUNKS):
-        copies[i].wait()
-        part = jnp.sum(x_ref[i * size : (i + 1) * size].astype(jnp.float32), axis=0, keepdims=True)
-        part = part * (1 / UNIT)
-        u = i * size // UNIT
-        means_ref[u] = part if i * size % UNIT == 0 else means_ref[u] + part
-    same, _, _ = flags(label_ref)
-    ends_ref[...] = jnp.zeros_like(ends_ref)
-    for base, end in ((0, 0), (DIRS, units - 1)):
-        total, count = jnp.zeros_like(part), jnp.zeros_like(part)
-        for v in range(units):
-            total = total + means_ref[v] * same[end][v]
-            count = count + same[end][v]
-        ends_ref[base : base + 1] = total
-        ends_ref[base + 1 : base + 2] = count
-        ends_ref[base + 2 : base + 3] = jnp.zeros_like(part) + label_ref[end].astype(jnp.float32)
-
-
-def unit_means(labels, x):
-    rows, width = x.shape
-    units = rows // UNIT
-    return pl.pallas_call(
-        means_kernel,
-        in_specs=smem(1) + [pl.BlockSpec(memory_space=pl.ANY)],
-        out_specs=vmem(2),
-        out_shape=[
-            jax.ShapeDtypeStruct((units, 1, width), jnp.float32),
-            jax.ShapeDtypeStruct((2 * DIRS, width), jnp.float32),
-        ],
-        scratch_shapes=[pltpu.VMEM(x.shape, x.dtype), pltpu.SemaphoreType.DMA((CHUNKS,))],
-        compiler_params=pltpu.CompilerParams(vmem_limit_bytes=20 * MIB),
-        name="unit_means",
-    )(labels, x)
-
-
 def apply_unit(narrow, spread_ref, u):
     return dot(narrow, spread_ref[0, u]) + dot(narrow, spread_ref[1, u])
 
 
-def spread_kernel(x_ref, mean_ref, start_ref, spread_ref, image_ref, centered):
+def spread_kernel(label_ref, x_ref, start_ref, spread_ref, image_ref, mean_ref, ends_ref, centered):
     u = pl.program_id(0)
     width = centered.shape[1]
+    ones = jnp.ones((DIRS, UNIT), jnp.bfloat16)
+    mean = dot(ones, x_ref[...])[:1] * (1 / UNIT)
+    mean_ref[u] = mean
     for a in range(0, UNIT, BLOCK):
-        centered[a : a + BLOCK] = (x_ref[a : a + BLOCK].astype(jnp.float32) - mean_ref[0]).astype(jnp.bfloat16)
+        centered[a : a + BLOCK] = (x_ref[a : a + BLOCK].astype(jnp.float32) - mean).astype(jnp.bfloat16)
     for a in range(0, width, BLOCK):
         spread = dot(centered[:, a : a + BLOCK], centered[:, a:], ((0,), (0,)))
         high = spread.astype(jnp.bfloat16)
         low = (spread - high.astype(jnp.float32)).astype(jnp.bfloat16)
         for h, part in enumerate((high, low)):
-            spread_ref[h, u, a : a + BLOCK, a:] = part
+            spread_ref[h, 0, a : a + BLOCK, a:] = part
             if a + BLOCK < width:
-                spread_ref[h, u, a + BLOCK :, a : a + BLOCK] = part[:, BLOCK:].T
-    image_ref[u] = apply_unit(start_ref[...].astype(jnp.bfloat16), spread_ref, u)
-
-
-def unit_spread(x, means, start):
+                spread_ref[h, 0, a + BLOCK :, a : a + BLOCK] = part[:, BLOCK:].T
+    narrow = start_ref[...].astype(jnp.bfloat16)
+    image_ref[u] = apply_unit(narrow, spread_ref, 0)
+
+    @pl.when(u == pl.num_programs(0) - 1)
+    def _():
+        same, _, _ = flags(label_ref)
+        units = image_ref.shape[0]
+        for first, end in ((0, 0), (2 * DIRS, units - 1)):
+            joined = join_units(end, same, narrow, image_ref, mean_ref)
+            line = jnp.zeros_like(mean)
+            parts = joined[0], joined[1], line + joined[2]
+            put_block(ends_ref, first, parts, line + label_ref[end].astype(jnp.float32))
+
+
+def join(narrow, a, b, mask):
+    number = b[2] * mask
+    total = a[2] + number
+    share = number / jnp.maximum(total, 1.0)
+    apart = b[1] - a[1]
+    along = jnp.sum(narrow.astype(jnp.float32) * apart, axis=1, keepdims=True)
+    images = a[0] + mask * b[0] + along * (UNIT * a[2] * share * apart)
+    return images, a[1] + share * apart, total
+
+
+def join_units(u, same, narrow, image_ref, mean_ref):
+    joined = image_ref[u], mean_ref[u], jnp.float32(1.0)
+    for v in range(image_ref.shape[0]):
+        if v != u:
+            joined = join(narrow, joined, (image_ref[v], mean_ref[v], jnp.float32(1.0)), same[u][v])
+    return joined
+
+
+def unit_spread(labels, x, start):
     rows, width = x.shape
     units = rows // UNIT
     return pl.pallas_call(
         spread_kernel,
         grid=(units,),
         in_specs=[
+            *smem(1),
             pl.BlockSpec((UNIT, width), lambda u: (u, 0)),
-            pl.BlockSpec((1, 1, width), lambda u: (u, 0, 0)),
             pl.BlockSpec((DIRS, width), lambda u: (0, 0)),
         ],
-        out_specs=vmem(2),
+        out_specs=[pl.BlockSpec((2, 1, width, width), lambda u: (0, u, 0, 0)), *vmem(3)],
         out_shape=[
-            pltpu.VMEM((2, units, width, width), jnp.bfloat16),
+            pltpu.HBM((2, units, width, width), jnp.bfloat16),
             jax.ShapeDtypeStruct((units, DIRS, width), jnp.float32),
+            jax.ShapeDtypeStruct((units, 1, width), jnp.float32),
+            jax.ShapeDtypeStruct((4 * DIRS, width), jnp.float32),
         ],
         scratch_shapes=[pltpu.VMEM((UNIT, width), jnp.bfloat16)],
-        compiler_params=pltpu.CompilerParams(vmem_limit_bytes=18 * MIB),
+        compiler_params=pltpu.CompilerParams(vmem_limit_bytes=26 * MIB),
         name="unit_spread",
-    )(x, means, start)
+    )(labels, x, start)
 
 
 def flags(label_ref):
@@ -139,22 +133,6 @@
             ends_ref[DIRS : 2 * DIRS] = total
 
 
-def first_kernel(label_ref, first_ref, last_ref, means_ref, start_ref, image_ref, out_ref, ends_ref, shift_ref):
-    units = means_ref.shape[0]
-    same, at_first, at_last = flags(label_ref)
-    narrow = start_ref[...].astype(jnp.bfloat16)
-    shift = []
-    for u in range(units):
-        total = first_ref[0:1] * at_first[u] + last_ref[0:1] * at_last[u]
-        count = first_ref[1:2] * at_first[u] + last_ref[1:2] * at_last[u]
-        for v in range(units):
-            total = total + means_ref[v] * same[u][v]
-            count = count + same[u][v]
-        shift.append(means_ref[u] - total / count)
-        shift_ref[u] = shift[u]
-    merge_units([image_ref[u] for u in range(units)], [narrow] * units, shift, same, out_ref, ends_ref)
-
-
 def vmem(count):
     return [pl.BlockSpec(memory_space=pltpu.VMEM)] * count
 
@@ -168,18 +146,6 @@
         jax.ShapeDtypeStruct((units, DIRS, width), jnp.float32),
         jax.ShapeDtypeStruct((2 * DIRS, width), jnp.float32),
     ]
-
-
-def first_images(labels, first, last_stats, means, start, images):
-    units, _, width = means.shape
-    return pl.pallas_call(
-        first_kernel,
-        in_specs=smem(1) + vmem(5),
-        out_specs=vmem(3),
-        out_shape=image_shapes(units, width) + [jax.ShapeDtypeStruct((units, 1, width), jnp.float32)],
-        compiler_params=pltpu.CompilerParams(vmem_limit_bytes=4 * MIB),
-        name="first_images",
-    )(labels, first, last_stats, means, start, images)
 
 
 def inverse_factor(images, row, lane):
@@ -200,23 +166,182 @@
     return inverse * scale
 
 
-def orthonormal(at_first, at_last, image_ref, first_ref, last_ref):
-    units = image_ref.shape[0]
-    first, last = first_ref[...], last_ref[...]
-    images = [image_ref[u] + first * at_first[u] + last * at_last[u] for u in range(units)]
+def orthonormal(images):
+    units = len(images)
     row = lax.broadcasted_iota(jnp.int32, (DIRS, units * DIRS), 0)
     lane = lax.broadcasted_iota(jnp.int32, (DIRS, units * DIRS), 1)
     inverse = [inverse_factor(images[u], row, lane - u * DIRS) for u in range(units)]
     return dot(jnp.concatenate(inverse, axis=0), jnp.concatenate(images, axis=0), precision=HIGHEST)
 
 
+def whole_images(at_first, at_last, image_ref, first_ref, last_ref):
+    first, last = first_ref[...], last_ref[...]
+    return [
+        image_ref[u] + first * at_first[u] + last * at_last[u] for u in range(image_ref.shape[0])
+    ]
+
+
+def multiply(totals, shift, same, spread_ref, out_ref, ends_ref, copies=()):
+    units = len(totals)
+    basis = orthonormal(totals).astype(jnp.bfloat16)
+    narrow = [basis[u * DIRS : (u + 1) * DIRS] for u in range(units)]
+    images = []
+    for u in range(units):
+        if copies:
+            copies[u].wait()
+        images.append(apply_unit(narrow[u], spread_ref, u))
+    merge_units(images, narrow, shift, same, out_ref, ends_ref)
+
+
+def block_at(ref, first):
+    rest = first + DIRS
+    return ref[first:rest], ref[rest : rest + 1], ref[rest + 1 : rest + 2], ref[rest + 2 : rest + 3]
+
+
+def put_block(ref, first, parts, label):
+    rest = first + DIRS
+    ref[first:rest] = parts[0]
+    for i, line in enumerate((parts[1], parts[2], label)):
+        ref[rest + i : rest + i + 1] = line
+    ref[rest + 3 : rest + DIRS] = jnp.zeros((DIRS - 3, ref.shape[1]), jnp.float32)
+
+
+def upward(me):
+    chip, core = me >> 1, me & 1
+    return (chip & 1) == core, ((chip >> 1) & 1) == core
+
+
+def flag(value):
+    return jnp.where(value, 1.0, 0.0)
+
+
+def chip_kernel(me_ref, own_ref, mate_ref, start_ref, near_ref, far_ref, mask_ref):
+    even = (me_ref[0] & 1) == 0
+    narrow = start_ref[...].astype(jnp.bfloat16)
+    own = block_at(own_ref, 0), block_at(own_ref, 2 * DIRS)
+    mate = block_at(mate_ref, 0), block_at(mate_ref, 2 * DIRS)
+    head, tail, mate_head, mate_tail = own[0][3], own[1][3], mate[0][3], mate[1][3]
+    chip_head = jnp.where(even, head, mate_head)
+    chip_tail = jnp.where(even, mate_tail, tail)
+    masks = [
+        flag(head == mate_head),
+        flag(tail == mate_tail),
+        jnp.where(even, 0.0, flag(mate_tail == head)),
+        jnp.where(even, flag(mate_head == tail), 0.0),
+        flag(head == chip_head),
+        flag(tail == chip_tail),
+        chip_head,
+        chip_tail,
+    ]
+    for i, line in enumerate(masks):
+        mask_ref[i : i + 1] = line
+
+    def order(a, b):
+        return [jnp.where(even, x, y) for x, y in zip(a, b)], [jnp.where(even, y, x) for x, y in zip(a, b)]
+
+    at_head = join(narrow, *order(own[0], mate[0]), masks[0])
+    at_tail = join(narrow, *order(mate[1], own[1]), masks[1])
+    for ref, up in zip((near_ref, far_ref), upward(me_ref[0])):
+        parts = [jnp.where(up, x, y) for x, y in zip(at_tail, at_head)]
+        put_block(ref, 0, parts, jnp.where(up, chip_tail, chip_head))
+
+
+def join_chip(me, own, mate, start):
+    width = own.shape[1]
+    part = jax.ShapeDtypeStruct((2 * DIRS, width), jnp.float32)
+    return pl.pallas_call(
+        chip_kernel,
+        in_specs=smem(1) + vmem(3),
+        out_specs=vmem(3),
+        out_shape=[part, part, jax.ShapeDtypeStruct((DIRS, width), jnp.float32)],
+        compiler_params=pltpu.CompilerParams(vmem_limit_bytes=4 * MIB),
+        name="join_chip",
+    )(me, own, mate, start)
+
+
+def sides_kernel(me_ref, near_ref, far_ref, mask_ref, start_ref, side_ref, from_ref):
+    narrow = start_ref[...].astype(jnp.bfloat16)
+    chip_head, chip_tail = mask_ref[6:7], mask_ref[7:8]
+    line = jnp.zeros_like(chip_head)
+    left = right = (jnp.zeros(start_ref.shape, jnp.float32), line, line)
+    from_ref[...] = jnp.zeros_like(from_ref)
+    for i, (ref, up) in enumerate(zip((near_ref, far_ref), upward(me_ref[0]))):
+        got = block_at(ref, 0)
+        from_left = jnp.where(up, 0.0, flag(got[3] == chip_head))
+        from_right = jnp.where(up, flag(got[3] == chip_tail), 0.0)
+        from_ref[2 * i : 2 * i + 1] = from_left
+        from_ref[2 * i + 1 : 2 * i + 2] = from_right
+        left = join(narrow, left, got, from_left)
+        right = join(narrow, right, got, from_right)
+    put_block(side_ref, 0, left, line)
+    put_block(side_ref, 2 * DIRS, right, line)
+
+
+def join_sides(me, near, far, masks, start):
+    width = near.shape[1]
+    return pl.pallas_call(
+        sides_kernel,
+        in_specs=smem(1) + vmem(4),
+        out_specs=vmem(2),
+        out_shape=[
+            jax.ShapeDtypeStruct((4 * DIRS, width), jnp.float32),
+            jax.ShapeDtypeStruct((DIRS, width), jnp.float32),
+        ],
+        compiler_params=pltpu.CompilerParams(vmem_limit_bytes=4 * MIB),
+        name="join_sides",
+    )(me, near, far, masks, start)
+
+
+def first_kernel(
+    label_ref, image_ref, mean_ref, mate_ref, side_ref, other_ref, mask_ref, start_ref, source,
+    out_ref, ends_ref, shift_ref, spread_ref, arrived,
+):
+    units = image_ref.shape[0]
+    copies = []
+    for u in range(units):
+        copies.append(pltpu.make_async_copy(source.at[:, u], spread_ref.at[:, u], arrived.at[u]))
+        copies[u].start()
+    same, at_first, at_last = flags(label_ref)
+    narrow = start_ref[...].astype(jnp.bfloat16)
+    outer = []
+    for first, mate_first, row in ((0, 2 * DIRS, 0), (2 * DIRS, 0, 1)):
+        side = join(narrow, block_at(side_ref, first), block_at(other_ref, first), 1.0)
+        mask = mask_ref[4 + row : 5 + row]
+        side = side[0] * mask, side[1], side[2] * mask
+        outer.append(join(narrow, side, block_at(mate_ref, mate_first), mask_ref[2 + row : 3 + row]))
+    totals, shift = [], []
+    for u in range(units):
+        joined = join_units(u, same, narrow, image_ref, mean_ref)
+        joined = join(narrow, joined, outer[0], at_first[u])
+        joined = join(narrow, joined, outer[1], at_last[u])
+        totals.append(joined[0])
+        shift.append(mean_ref[u] - joined[1])
+        shift_ref[u] = shift[u]
+    multiply(totals, shift, same, spread_ref, out_ref, ends_ref, copies)
+
+
+def first_step(labels, images, means, mate, side, other, masks, start, spread):
+    units, _, width = images.shape
+    return pl.pallas_call(
+        first_kernel,
+        in_specs=smem(1) + vmem(7) + [pl.BlockSpec(memory_space=pl.ANY)],
+        out_specs=vmem(4),
+        out_shape=[
+            *image_shapes(units, width),
+            jax.ShapeDtypeStruct((units, 1, width), jnp.float32),
+            pltpu.VMEM(spread.shape, spread.dtype),
+        ],
+        scratch_shapes=[pltpu.SemaphoreType.DMA((units,))],
+        compiler_params=pltpu.CompilerParams(vmem_limit_bytes=8 * MIB),
+        name="first_step",
+    )(labels, images, means, mate, side, other, masks, start, spread)
+
+
 def step_kernel(label_ref, image_ref, first_ref, last_ref, shift_ref, spread_ref, out_ref, ends_ref):
-    units = image_ref.shape[0]
     same, at_first, at_last = flags(label_ref)
-    basis = orthonormal(at_first, at_last, image_ref, first_ref, last_ref).astype(jnp.bfloat16)
-    narrow = [basis[u * DIRS : (u + 1) * DIRS] for u in range(units)]
-    images = [apply_unit(narrow[u], spread_ref, u) for u in range(units)]
-    merge_units(images, narrow, [shift_ref[u] for u in range(units)], same, out_ref, ends_ref)
+    totals = whole_images(at_first, at_last, image_ref, first_ref, last_ref)
+    shift = [shift_ref[u] for u in range(image_ref.shape[0])]
+    multiply(totals, shift, same, spread_ref, out_ref, ends_ref)
 
 
 def route_kernel(owner_ref, me_ref, label_ref, *refs):
@@ -262,7 +387,7 @@
         out_shape=shapes,
         compiler_params=pltpu.CompilerParams(vmem_limit_bytes=8 * MIB),
         name="step_and_route",
-    )(owners, me.reshape(1), labels, images, first, last_image, shift, spread)
+    )(owners, me, labels, images, first, last_image, shift, spread)
 
 
 def project_kernel(
@@ -270,7 +395,8 @@
 ):
     copies = fetch(source, x_ref, arrived, 0, PART)
     _, at_first, at_last = flags(label_ref)
-    narrow = orthonormal(at_first, at_last, image_ref, first_ref, last_ref).astype(jnp.bfloat16)
+    totals = whole_images(at_first, at_last, image_ref, first_ref, last_ref)
+    narrow = orthonormal(totals).astype(jnp.bfloat16)
     for i, copy in enumerate(copies):
         u = i * PART // UNIT
         chosen = narrow[u * DIRS : (u + 1) * DIRS]
@@ -298,7 +424,7 @@
 
 
 def finish_kernel(kept_ref, got_ref, out_ref):
-    out_ref[0] = orthonormal([1.0], [0.0], kept_ref, got_ref.at[0], got_ref.at[0])
+    out_ref[0] = orthonormal([kept_ref[0] + got_ref[0]])
 
 
 def finish(kept, got):
@@ -317,8 +443,7 @@
     units = rows // UNIT
     chips = n_dp // 2
     me = lax.axis_index("dp")
-    chip, core = me >> 1, me & 1
-    even = core == 0
+    even = (me & 1) == 0
     labels = cluster_ids[::UNIT]
 
     near = (lambda p: p ^ 1, lambda p: (p + 1) % chips if p % 2 else (p - 1) % chips)
@@ -327,7 +452,6 @@
         [(2 * p + c, 2 * pairing[c](p) + c) for p in range(chips) for c in range(2)]
         for pairing in (near, far)
     ]
-    upward = [(chip & 1) == core, ((chip >> 1) & 1) == core]
     mates = [(i, i ^ 1) for i in range(n_dp)]
 
     def halves(both):
@@ -349,47 +473,28 @@
         return first, last_image
 
     embeddings = pltpu.with_memory_space_constraint(embeddings, pltpu.HBM)
-    means, own = unit_means(labels, embeddings)
-    row = lax.broadcasted_iota(jnp.int32, (DIRS, width), 0)
-    mate = swap(own)
-    own = halves(own)
-    head, tail = own[0][2:3], own[1][2:3]
-    mate_head, mate_tail = mate[0][2:3], mate[1][2:3]
-    chip_head = jnp.where(even, head, mate_head)
-    chip_tail = jnp.where(even, mate_tail, tail)
-
-    def flag(value):
-        return value.astype(jnp.float32)
-
-    joins = flag(head == mate_head), flag(tail == mate_tail)
-    masks = (
-        flag(~even & (mate_tail == head)),
-        flag(even & (mate_head == tail)),
-        flag(head == chip_head),
-        flag(tail == chip_tail),
+    spread, raw, means, own = unit_spread(labels, embeddings, start_basis)
+
+    place = me.reshape(1)
+    mate = lax.ppermute(own, "dp", mates)
+    near, far, masks = join_chip(place, own, mate, start_basis)
+    near, far = (lax.ppermute(part, "dp", link) for part, link in zip((near, far), links))
+    side, origins = join_sides(place, near, far, masks, start_basis)
+    other = lax.ppermute(side, "dp", mates)
+    images, ends, shift, spread = first_step(
+        labels, raw, means, mate, side, other, masks, start_basis,
+        pltpu.with_memory_space_constraint(spread, pltpu.HBM),
     )
-    totals = chip_totals(own, mate, joins)
-    totals = jnp.where(row < 2, totals[0], chip_head), jnp.where(row < 2, totals[1], chip_tail)
-    arrived = [
-        lax.ppermute(jnp.where(up, totals[1], totals[0]), "dp", link) for link, up in zip(links, upward)
-    ]
-    spread, raw = unit_spread(embeddings, means, start_basis)
-    raw, *arrived = lax.optimization_barrier((raw, *arrived))
-    left = right = jnp.zeros((DIRS, width), jnp.float32)
-    sides = []
-    for got, up in zip(arrived, upward):
-        from_left = flag(~up & (got[2:3] == chip_head))
-        from_right = flag(up & (got[2:3] == chip_tail))
-        sides.append((from_left, from_right))
-        left = left + from_left * got
-        right = right + from_right * got
-    first_stats, last_stats = collect(left, right, own, mate, masks)
+    joins = masks[0:1], masks[1:2]
+    masks = tuple(masks[i : i + 1] for i in range(2, 6))
+    sides = [(origins[i : i + 1], origins[i + 1 : i + 2]) for i in (0, 2)]
+    ups = upward(me)
 
     def exchange(ends, mate=None, beside=lambda: ()):
         mate, own = mate or swap(ends), halves(ends)
         totals = chip_totals(own, mate, joins)
         arrived = [
-            lax.ppermute(jnp.where(up, totals[1], totals[0]), "dp", link) for link, up in zip(links, upward)
+            lax.ppermute(jnp.where(up, totals[1], totals[0]), "dp", link) for link, up in zip(links, ups)
         ]
         arrived, other = lax.optimization_barrier((arrived, beside()))
         left = right = jnp.zeros_like(own[0])
@@ -410,12 +515,11 @@
         kept, sent = halve(tiles, bit)
         return kept + route(sent, bit)
 
-    images, ends, shift = first_images(labels, first_stats, last_stats, means, start_basis, raw)
-    for _ in range(ITERS - 2):
+    for _ in range(ITERS - 3):
         images, ends = step(labels, images, *exchange(ends)[:2], shift, spread)
 
     images, ends, kept = step_and_route(
-        owner_table, me, labels, images, *exchange(ends)[:2], shift, spread
+        owner_table, place, labels, images, *exchange(ends)[:2], shift, spread
     )
     got = lax.ppermute(ends, "dp", mates)
     kept = (kept + got[2 * DIRS :]).reshape(n_dp // 2, DIRS, width)

time: 120 us -> 116 us (0.967)
  waiting for transfers between devices: 36.9 us -> 34.1 us
  starting transfers between devices: 30.4 us -> 28.1 us
    ppermute x13 -> x9, starting transfers between devices: 19.4 us -> 12.7 us  [swap(): return halves(lax.ppermute(both, 'dp', mates))]
    ppermute x2 -> x4, waiting for transfers between devices: 0.01 us -> 4.65 us  [the longest x2 2.68 us: per_device(): lax.ppermute(part, 'dp', link)]
    ppermute x2 -> x4, starting transfers between devices: 4.46 us -> 8.6 us  [the longest x2 4.53 us: per_device(): lax.ppermute(part, 'dp', link)]
    pallas_call x3 -> x4, Pallas kernels: 24 us -> 28.1 us  [the longest x1 20.7 us: unit_spread(): pl.pallas_call(spread_kernel, grid=(units,), in_specs=[*smem(1), pl.Block...]
    ppermute x13 -> x9, waiting for transfers between devices: 10.8 us -> 7.2 us  [swap(): return halves(lax.ppermute(both, 'dp', mates))]
    pallas_call x4 -> x3, Pallas kernels: 13.1 us -> 9.9 us  [step(): pl.pallas_call(step_kernel, in_specs=smem(1) + vmem(5), out_specs=vmem(2)...]
    ppermute x12 -> x10, waiting for transfers between devices: 21.5 us -> 18.8 us  [exchange(): lax.ppermute(jnp.where(up, totals[1], totals[0]), 'dp', link)]
    ppermute x3, starting transfers between devices: 0.67 us -> 2.17 us  [route(): return lax.ppermute(sent, 'dp', [(i, i ^ bit) for i in range(n_dp)])]
  transfers between devices with their start and end apart: 31 -> 27, of which waited for: 25 -> 23; matrix products, arithmetic and copies ran while one was open for 0% -> 0% of each run, Pallas kernels for 21% -> 7%
where the time goes in v5:
time: 116 us
  Pallas kernels  50.4 us (43%)
  waiting for transfers between devices  34.1 us (29%)
  starting transfers between devices  28.1 us (24%)
  local copies, waits for them, and re-layouts  1.64 us (1%)
    pallas_call x1, Pallas kernels, unit_spread(): pl.pallas_call(spread_kernel, grid=(units,), in_specs=[*smem(1), pl.Block...  20.7 us
    ppermute x10, waiting for transfers between devices, exchange(): lax.ppermute(jnp.where(up, totals[1], totals[0]), 'dp', link)  18.8 us
    ppermute x9, starting transfers between devices, swap(): return halves(lax.ppermute(both, 'dp', mates))  12.7 us
    pallas_call x3, Pallas kernels, step(): pl.pallas_call(step_kernel, in_specs=smem(1) + vmem(5), out_specs=vmem(2)...  9.9 us
    pallas_call x1, Pallas kernels, project(): pl.pallas_call(project_kernel, in_specs=smem(1) + vmem(5) + [pl.BlockSpec...  8.19 us
    ppermute x9, waiting for transfers between devices, swap(): return halves(lax.ppermute(both, 'dp', mates))  7.2 us
    pallas_call x1, Pallas kernels, first_step(): pl.pallas_call(first_kernel, in_specs=smem(1) + vmem(7) + [pl.BlockSpec(m...  7.17 us
    ppermute x2, starting transfers between devices, per_device(): lax.ppermute(part, 'dp', link)  4.53 us
  transfers between devices with their start and end apart: 27, of which 23 were waited for; matrix products, arithmetic and copies ran while one was open for 0% of the time, Pallas kernels for 7%

profile of v5, /device:TPU:0, one launch (start us, length us, event | category | flops | bytes accessed | tf_op | source)
XLA Modules:
  0.0 115.5 jit_solution(184565830461839930)
XLA Ops:
  2.2 20.7 %unit_spread.1 = (bf16[2,4,1024,1024]{3,2,1,0:T(8,128)(2,1)}, f32[4,8,1024]{2,1,0:T(8,128)S(1)}, f32[4,1,1024]{2,1,0:T(1,128)S(1)}, f32[32,1024]{1,0:T(8,128)S(1)}) custom-call(s32[4]{0:T(128)S(1)} %slice.152.label_ref, bf16[8192,1024]{1,0:T(8,128)(2,1)} %source.1, f32[8,1024]{1,0:T(8,128)S(1)} %copy-done), custom_call_target="tpu_custom_call" | custom-call | tf_op jit(solution)/shard_map/unit_spread/pallas_call | solution.py:89
  23.4 1.0 collective-permute-done.mate_ref
  24.5 2.9 %collective-permute-start.1 = (f32[16,1024]{1,0:T(8,128)S(1)}, f32[16,1024]{1,0:T(8,128)S(1)}, u32[]{:S(2)}, u32[]{:S(2)}) collective-permute-start(f32[16,1024]{1,0:T(8,128)S(1)} %get-tuple-element.38), channel_id=1, source_target_pairs={{0,2},{1,15},{2,0},{3,5},{4,6},{5,3},{6,4},{7,9},{8,10},{9,7},{10,... | collective-permute-start | bytes 196616 | tf_op jit(solution)/shard_map/ppermute | solution.py:481
  27.4 1.6 %collective-permute-start.2 = (f32[16,1024]{1,0:T(8,128)S(1)}, f32[16,1024]{1,0:T(8,128)S(1)}, u32[]{:S(2)}, u32[]{:S(2)}) collective-permute-start(f32[16,1024]{1,0:T(8,128)S(1)} %get-tuple-element.39), channel_id=1, source_target_pairs={{0,4},{1,13},{2,6},{3,15},{4,0},{5,9},{6,2},{7,11},{8,12},{9,5},{1... | collective-permute-start | bytes 196616 | tf_op jit(solution)/shard_map/ppermute | solution.py:481
  29.0 0.9 collective-permute-done.1.near_ref
  29.9 1.7 %collective-permute-done.2.far_ref = f32[16,1024]{1,0:T(8,128)S(1)} collective-permute-done((f32[16,1024]{1,0:T(8,128)S(1)}, f32[16,1024]{1,0:T(8,128)S(1)}, u32[]{:S(2)}, u32[]{:S(2)}) %collective-permute-start.2) | collective-permute-done | bytes 65568 | tf_op jit(solution)/shard_map/ppermute | solution.py:481
  31.8 3.6 %collective-permute-start.3 = (f32[32,1024]{1,0:T(8,128)S(1)}, f32[32,1024]{1,0:T(8,128)S(1)}, u32[]{:S(2)}, u32[]{:S(2)}) collective-permute-start(f32[32,1024]{1,0:T(8,128)S(1)} %get-tuple-element.41.side_ref), channel_id=1, source_target_pairs={{0,1},{1,0},{2,3},{3,2},{4,5},{5,4},{6,7},{7,6},{8,9},{9,8},{10,11... | collective-permute-start | bytes 393224 | tf_op jit(solution)/shard_map/ppermute | solution.py:483
  35.4 1.0 collective-permute-done.3.other_ref
  36.4 7.2 %first_step.1 = (f32[4,8,1024]{2,1,0:T(8,128)S(1)}, f32[16,1024]{1,0:T(8,128)S(1)}, f32[4,1,1024]{2,1,0:T(1,128)S(1)}, bf16[2,4,1024,1024]{3,2,1,0:T(8,128)(2,1)S(1)}) custom-call(s32[4]{0:T(128)S(1)} %slice.152.label_ref, f32[4,8,1024]{2,1,0:T(8,128)S(1)} %get-tuple-element.35.image_ref, f32[4,1,1024]{2,1,0:T(1,128)S(1)} %get-tuple-element.36.mean_ref, ...), custom_call_target="tpu_custom_call" | custom-call | tf_op jit(solution)/shard_map/first_step/pallas_call | solution.py:325
  45.1 3.8 %collective-permute-done.5 = f32[8,1024]{1,0:T(8,128)S(1)} collective-permute-done((f32[8,1024]{1,0:T(8,128)S(1)}, f32[8,1024]{1,0:T(8,128)S(1)}, u32[]{:S(2)}, u32[]{:S(2)}) %collective-permute-start.5) | collective-permute-done | bytes 32800 | tf_op jit(solution)/shard_map/ppermute | solution.py:497
  49.0 2.0 %collective-permute-start.7 = (f32[16,1024]{1,0:T(8,128)S(1)}, f32[16,1024]{1,0:T(8,128)S(1)}, u32[]{:S(2)}, u32[]{:S(2)}) collective-permute-start(f32[16,1024]{1,0:T(8,128)S(1)} %pad_maximum_fusion), channel_id=1, source_target_pairs={{0,1},{1,0},{2,3},{3,2},{4,5},{5,4},{6,7},{7,6},{8,9},{9,8},{10,11... | collective-permute-start | bytes 196616 | tf_op jit(solution)/shard_map/ppermute | solution.py:461
  52.0 3.2 %step.3 = (f32[4,8,1024]{2,1,0:T(8,128)S(1)}, f32[16,1024]{1,0:T(8,128)S(1)}) custom-call(s32[4]{0:T(128)S(1)} %slice.152.label_ref, f32[4,8,1024]{2,1,0:T(8,128)S(1)} %get-tuple-element.43.image_ref, f32[8,1024]{1,0:T(8,128)S(1)} %get-tuple-element.87.first_ref, f32[8,1024]{1,0:T(8,128)S(1)} %get-tuple-element.86.last_ref, ...), custom_call_target="tpu_custom_call" | custom-call | tf_op jit(solution)/shard_map/step/pallas_call | solution.py:367
  55.6 0.9 collective-permute-done.8
  57.5 3.0 %collective-permute-done.10 = f32[8,1024]{1,0:T(8,128)S(1)} collective-permute-done((f32[8,1024]{1,0:T(8,128)S(1)}, f32[8,1024]{1,0:T(8,128)S(1)}, u32[]{:S(2)}, u32[]{:S(2)}) %collective-permute-start.10) | collective-permute-done | bytes 32800 | tf_op jit(solution)/shard_map/ppermute | solution.py:497
  60.6 2.3 %collective-permute-start.11 = (f32[16,1024]{1,0:T(8,128)S(1)}, f32[16,1024]{1,0:T(8,128)S(1)}, u32[]{:S(2)}, u32[]{:S(2)}) collective-permute-start(f32[16,1024]{1,0:T(8,128)S(1)} %pad_maximum_fusion.1), channel_id=1, source_target_pairs={{0,1},{1,0},{2,3},{3,2},{4,5},{5,4},{6,7},{7,6},{8,9},{9,8},{10,11... | collective-permute-start | bytes 196616 | tf_op jit(solution)/shard_map/ppermute | solution.py:461
  63.8 3.2 %step.4 = (f32[4,8,1024]{2,1,0:T(8,128)S(1)}, f32[16,1024]{1,0:T(8,128)S(1)}) custom-call(s32[4]{0:T(128)S(1)} %slice.152.label_ref, f32[4,8,1024]{2,1,0:T(8,128)S(1)} %get-tuple-element.50.image_ref, f32[8,1024]{1,0:T(8,128)S(1)} %get-tuple-element.85.first_ref, f32[8,1024]{1,0:T(8,128)S(1)} %get-tuple-element.84.last_ref, ...), custom_call_target="tpu_custom_call" | custom-call | tf_op jit(solution)/shard_map/step/pallas_call | solution.py:367
  68.4 1.6 %collective-permute-start.13 = (f32[8,1024]{1,0:T(8,128)S(1)}, f32[8,1024]{1,0:T(8,128)S(1)}, u32[]{:S(2)}, u32[]{:S(2)}) collective-permute-start(f32[8,1024]{1,0:T(8,128)S(1)} %get-tuple-element.75), channel_id=1, source_target_pairs={{0,2},{1,15},{2,0},{3,5},{4,6},{5,3},{6,4},{7,9},{8,10},{9,7},{10,... | collective-permute-start | bytes 98312 | tf_op jit(solution)/shard_map/ppermute | solution.py:497
  70.0 2.4 %collective-permute-done.13 = f32[8,1024]{1,0:T(8,128)S(1)} collective-permute-done((f32[8,1024]{1,0:T(8,128)S(1)}, f32[8,1024]{1,0:T(8,128)S(1)}, u32[]{:S(2)}, u32[]{:S(2)}) %collective-permute-start.13) | collective-permute-done | bytes 32800 | tf_op jit(solution)/shard_map/ppermute | solution.py:497
  72.4 1.5 %collective-permute-done.14 = f32[8,1024]{1,0:T(8,128)S(1)} collective-permute-done((f32[8,1024]{1,0:T(8,128)S(1)}, f32[8,1024]{1,0:T(8,128)S(1)}, u32[]{:S(2)}, u32[]{:S(2)}) %collective-permute-start.14) | collective-permute-done | bytes 32800 | tf_op jit(solution)/shard_map/ppermute | solution.py:497
  73.9 2.6 %collective-permute-start.15 = (f32[16,1024]{1,0:T(8,128)S(1)}, f32[16,1024]{1,0:T(8,128)S(1)}, u32[]{:S(2)}, u32[]{:S(2)}) collective-permute-start(f32[16,1024]{1,0:T(8,128)S(1)} %pad_maximum_fusion.2), channel_id=1, source_target_pairs={{0,1},{1,0},{2,3},{3,2},{4,5},{5,4},{6,7},{7,6},{8,9},{9,8},{10,11... | collective-permute-start | bytes 196616 | tf_op jit(solution)/shard_map/ppermute | solution.py:461
  77.5 3.4 %step.5 = (f32[4,8,1024]{2,1,0:T(8,128)S(1)}, f32[16,1024]{1,0:T(8,128)S(1)}) custom-call(s32[4]{0:T(128)S(1)} %slice.152.label_ref, f32[4,8,1024]{2,1,0:T(8,128)S(1)} %get-tuple-element.54.image_ref, f32[8,1024]{1,0:T(8,128)S(1)} %get-tuple-element.83.first_ref, f32[8,1024]{1,0:T(8,128)S(1)} %get-tuple-element.82.last_ref, ...), custom_call_target="tpu_custom_call" | custom-call | tf_op jit(solution)/shard_map/step/pallas_call | solution.py:367
  82.5 3.8 %collective-permute-done.17 = f32[8,1024]{1,0:T(8,128)S(1)} collective-permute-done((f32[8,1024]{1,0:T(8,128)S(1)}, f32[8,1024]{1,0:T(8,128)S(1)}, u32[]{:S(2)}, u32[]{:S(2)}) %collective-permute-start.17) | collective-permute-done | bytes 32800 | tf_op jit(solution)/shard_map/ppermute | solution.py:497
  86.4 2.0 %collective-permute-start.19 = (f32[16,1024]{1,0:T(8,128)S(1)}, f32[16,1024]{1,0:T(8,128)S(1)}, u32[]{:S(2)}, u32[]{:S(2)}) collective-permute-start(f32[16,1024]{1,0:T(8,128)S(1)} %pad_maximum_fusion.3), channel_id=1, source_target_pairs={{0,1},{1,0},{2,3},{3,2},{4,5},{5,4},{6,7},{7,6},{8,9},{9,8},{10,11... | collective-permute-start | bytes 196616 | tf_op jit(solution)/shard_map/ppermute | solution.py:461
  89.4 3.3 %step_and_route.1 = (f32[4,8,1024]{2,1,0:T(8,128)S(1)}, f32[80,1024]{1,0:T(8,128)S(1)}, f32[64,1024]{1,0:T(8,128)S(1)}) custom-call(s32[16]{0:T(128)S(1)} %copy-done.2, s32[1]{0:T(128)} %bitcast.me_ref, s32[4]{0:T(128)S(1)} %slice.152.label_ref, f32[4,8,1024]{2,1,0:T(8,128)S(1)} %get-tuple-element.58.refs_0_, f32[8,1024]{1,0:T(8,128)S(1)} %get-tuple-element.81.refs_1_, ...), custom_call_target="tpu_custom_call" | custom-call | tf_op jit(solution)/shard_map/step_and_route/pallas_call | solution.py:383
  93.1 1.3 %collective-permute-done.20 = f32[80,1024]{1,0:T(8,128)S(1)} collective-permute-done((f32[80,1024]{1,0:T(8,128)S(1)}, f32[80,1024]{1,0:T(8,128)S(1)}, u32[]{:S(2)}, u32[]{:S(2)}) %collective-permute-start.20) | collective-permute-done | bytes 327712 | tf_op jit(solution)/shard_map/ppermute | solution.py:524
  95.3 1.3 %collective-permute-start.21 = (f32[8,1024]{1,0:T(8,128)S(1)}, f32[8,1024]{1,0:T(8,128)S(1)}, u32[]{:S(2)}, u32[]{:S(2)}) collective-permute-start(f32[8,1024]{1,0:T(8,128)S(1)} %get-tuple-element.69), channel_id=1, source_target_pairs={{0,2},{1,15},{2,0},{3,5},{4,6},{5,3},{6,4},{7,9},{8,10},{9,7},{10,... | collective-permute-start | bytes 98312 | tf_op jit(solution)/shard_map/ppermute | solution.py:497
  96.7 4.0 %collective-permute-done.21 = f32[8,1024]{1,0:T(8,128)S(1)} collective-permute-done((f32[8,1024]{1,0:T(8,128)S(1)}, f32[8,1024]{1,0:T(8,128)S(1)}, u32[]{:S(2)}, u32[]{:S(2)}) %collective-permute-start.21) | collective-permute-done | bytes 32800 | tf_op jit(solution)/shard_map/ppermute | solution.py:497
  100.8 2.1 %collective-permute-start.26 = (f32[16,1024]{1,0:T(8,128)S(1)}, f32[16,1024]{1,0:T(8,128)S(1)}, u32[]{:S(2)}, u32[]{:S(2)}) collective-permute-start(f32[16,1024]{1,0:T(8,128)S(1)} %pad_maximum_fusion.4), channel_id=1, source_target_pairs={{0,1},{1,0},{2,3},{3,2},{4,5},{5,4},{6,7},{7,6},{8,9},{9,8},{10,11... | collective-permute-start | bytes 196616 | tf_op jit(solution)/shard_map/ppermute | solution.py:461
  102.9 2.1 %collective-permute-done.24 = f32[2,8,1024]{2,1,0:T(8,128)S(1)} collective-permute-done((f32[2,8,1024]{2,1,0:T(8,128)S(1)}, f32[2,8,1024]{2,1,0:T(8,128)S(1)}, u32[]{:S(2)}, u32[]{:S(2)}) %collective-permute-start.24) | collective-permute-done | bytes 65568 | tf_op jit(solution)/shard_map/ppermute | solution.py:512
  105.1 1.3 %collective-permute-start.25 = (f32[1,8,1024]{2,1,0:T(8,128)S(1)}, f32[1,8,1024]{2,1,0:T(8,128)S(1)}, u32[]{:S(2)}, u32[]{:S(2)}) collective-permute-start(f32[1,8,1024]{2,1,0:T(8,128)S(1)} %get-tuple-element.90), channel_id=1, source_target_pairs={{0,8},{1,9},{2,10},{3,11},{4,12},{5,13},{6,14},{7,15},{8,0},{9,1},... | collective-permute-start | bytes 98312 | tf_op jit(solution)/shard_map/ppermute | solution.py:512
  106.4 8.2 %project.1 = f32[8,8192]{1,0:T(8,128)} custom-call(s32[4]{0:T(128)S(1)} %slice.152.label_ref, f32[4,8,1024]{2,1,0:T(8,128)S(1)} %get-tuple-element.65.image_ref, f32[8,1024]{1,0:T(8,128)S(1)} %get-tuple-element.71.first_ref, f32[8,1024]{1,0:T(8,128)S(1)} %get-tuple-element.70.last_ref, f32[4,1,1024]{2,1,0:T(1,128)S(1)} %get-tuple-element.36.mean_ref, ...), custom_call_target="tpu_custom_call" | custom-call | flops 4294967296 | bytes 16777216 | tf_op jit(solution)/shard_map/project/pallas_call | solution.py:412
  114.6 1.0 finish.1
  (67 shorter events, 13.5 us)
Async XLA Ops:
  1.5 0.8 copy-start
  2.2 22.1 %copy-start.1 = (f32[8,1024]{1,0:T(8,128)S(1)}, f32[8,1024]{1,0:T(8,128)}, u32[]{:S(2)}) copy-start(f32[8,1024]{1,0:T(8,128)} %start_ref.7) | copy-start | bytes 98308
  22.9 1.4 %collective-permute-start = (f32[32,1024]{1,0:T(8,128)S(1)}, f32[32,1024]{1,0:T(8,128)S(1)}, u32[]{:S(2)}, u32[]{:S(2)}) collective-permute-start(f32[32,1024]{1,0:T(8,128)S(1)} %get-tuple-element.37.own_ref), channel_id=1, source_target_pairs={{0,1},{1,0},{2,3},{3,2},{4,5},{5,4},{6,7},{7,6},{8,9},{9,8},{10,11... | collective-permute-start | bytes 393224 | tf_op jit(solution)/shard_map/ppermute | solution.py:479
  24.5 5.5 %collective-permute-start.1 = (f32[16,1024]{1,0:T(8,128)S(1)}, f32[16,1024]{1,0:T(8,128)S(1)}, u32[]{:S(2)}, u32[]{:S(2)}) collective-permute-start(f32[16,1024]{1,0:T(8,128)S(1)} %get-tuple-element.38), channel_id=1, source_target_pairs={{0,2},{1,15},{2,0},{3,5},{4,6},{5,3},{6,4},{7,9},{8,10},{9,7},{10,... | collective-permute-start | bytes 196616 | tf_op jit(solution)/shard_map/ppermute | solution.py:481
  27.4 4.3 %collective-permute-start.2 = (f32[16,1024]{1,0:T(8,128)S(1)}, f32[16,1024]{1,0:T(8,128)S(1)}, u32[]{:S(2)}, u32[]{:S(2)}) collective-permute-start(f32[16,1024]{1,0:T(8,128)S(1)} %get-tuple-element.39), channel_id=1, source_target_pairs={{0,4},{1,13},{2,6},{3,15},{4,0},{5,9},{6,2},{7,11},{8,12},{9,5},{1... | collective-permute-start | bytes 196616 | tf_op jit(solution)/shard_map/ppermute | solution.py:481
  31.8 4.6 %collective-permute-start.3 = (f32[32,1024]{1,0:T(8,128)S(1)}, f32[32,1024]{1,0:T(8,128)S(1)}, u32[]{:S(2)}, u32[]{:S(2)}) collective-permute-start(f32[32,1024]{1,0:T(8,128)S(1)} %get-tuple-element.41.side_ref), channel_id=1, source_target_pairs={{0,1},{1,0},{2,3},{3,2},{4,5},{5,4},{6,7},{7,6},{8,9},{9,8},{10,11... | collective-permute-start | bytes 393224 | tf_op jit(solution)/shard_map/ppermute | solution.py:483
  43.6 1.3 %collective-permute-start.4 = (f32[16,1024]{1,0:T(8,128)S(1)}, f32[16,1024]{1,0:T(8,128)S(1)}, u32[]{:S(2)}, u32[]{:S(2)}) collective-permute-start(f32[16,1024]{1,0:T(8,128)S(1)} %get-tuple-element.45), channel_id=1, source_target_pairs={{0,1},{1,0},{2,3},{3,2},{4,5},{5,4},{6,7},{7,6},{8,9},{9,8},{10,11... | collective-permute-start | bytes 196616 | tf_op jit(solution)/shard_map/ppermute | solution.py:461
  44.9 4.0 %collective-permute-start.5 = (f32[8,1024]{1,0:T(8,128)S(1)}, f32[8,1024]{1,0:T(8,128)S(1)}, u32[]{:S(2)}, u32[]{:S(2)}) collective-permute-start(f32[8,1024]{1,0:T(8,128)S(1)} %get-tuple-element.79), channel_id=1, source_target_pairs={{0,2},{1,15},{2,0},{3,5},{4,6},{5,3},{6,4},{7,9},{8,10},{9,7},{10,... | collective-permute-start | bytes 98312 | tf_op jit(solution)/shard_map/ppermute | solution.py:497
  45.0 4.0 %collective-permute-start.6 = (f32[8,1024]{1,0:T(8,128)S(1)}, f32[8,1024]{1,0:T(8,128)S(1)}, u32[]{:S(2)}, u32[]{:S(2)}) collective-permute-start(f32[8,1024]{1,0:T(8,128)S(1)} %get-tuple-element.78), channel_id=1, source_target_pairs={{0,4},{1,13},{2,6},{3,15},{4,0},{5,9},{6,2},{7,11},{8,12},{9,5},{1... | collective-permute-start | bytes 98312 | tf_op jit(solution)/shard_map/ppermute | solution.py:497
  49.0 2.9 %collective-permute-start.7 = (f32[16,1024]{1,0:T(8,128)S(1)}, f32[16,1024]{1,0:T(8,128)S(1)}, u32[]{:S(2)}, u32[]{:S(2)}) collective-permute-start(f32[16,1024]{1,0:T(8,128)S(1)} %pad_maximum_fusion), channel_id=1, source_target_pairs={{0,1},{1,0},{2,3},{3,2},{4,5},{5,4},{6,7},{7,6},{8,9},{9,8},{10,11... | collective-permute-start | bytes 196616 | tf_op jit(solution)/shard_map/ppermute | solution.py:461
  55.2 1.3 %collective-permute-start.8 = (f32[16,1024]{1,0:T(8,128)S(1)}, f32[16,1024]{1,0:T(8,128)S(1)}, u32[]{:S(2)}, u32[]{:S(2)}) collective-permute-start(f32[16,1024]{1,0:T(8,128)S(1)} %get-tuple-element.51), channel_id=1, source_target_pairs={{0,1},{1,0},{2,3},{3,2},{4,5},{5,4},{6,7},{7,6},{8,9},{9,8},{10,11... | collective-permute-start | bytes 196616 | tf_op jit(solution)/shard_map/ppermute | solution.py:461
  56.5 4.0 %collective-permute-start.10 = (f32[8,1024]{1,0:T(8,128)S(1)}, f32[8,1024]{1,0:T(8,128)S(1)}, u32[]{:S(2)}, u32[]{:S(2)}) collective-permute-start(f32[8,1024]{1,0:T(8,128)S(1)} %get-tuple-element.76), channel_id=1, source_target_pairs={{0,4},{1,13},{2,6},{3,15},{4,0},{5,9},{6,2},{7,11},{8,12},{9,5},{1... | collective-permute-start | bytes 98312 | tf_op jit(solution)/shard_map/ppermute | solution.py:497
  56.6 4.0 %collective-permute-start.9 = (f32[8,1024]{1,0:T(8,128)S(1)}, f32[8,1024]{1,0:T(8,128)S(1)}, u32[]{:S(2)}, u32[]{:S(2)}) collective-permute-start(f32[8,1024]{1,0:T(8,128)S(1)} %get-tuple-element.77), channel_id=1, source_target_pairs={{0,2},{1,15},{2,0},{3,5},{4,6},{5,3},{6,4},{7,9},{8,10},{9,7},{10,... | collective-permute-start | bytes 98312 | tf_op jit(solution)/shard_map/ppermute | solution.py:497
  60.6 3.2 %collective-permute-start.11 = (f32[16,1024]{1,0:T(8,128)S(1)}, f32[16,1024]{1,0:T(8,128)S(1)}, u32[]{:S(2)}, u32[]{:S(2)}) collective-permute-start(f32[16,1024]{1,0:T(8,128)S(1)} %pad_maximum_fusion.1), channel_id=1, source_target_pairs={{0,1},{1,0},{2,3},{3,2},{4,5},{5,4},{6,7},{7,6},{8,9},{9,8},{10,11... | collective-permute-start | bytes 196616 | tf_op jit(solution)/shard_map/ppermute | solution.py:461
  63.8 25.6 %copy-start.2 = (s32[16]{0:T(128)S(1)}, s32[16]{0:T(128)}, u32[]{:S(2)}) copy-start(s32[16]{0:T(128)} %owner_ref.1) | copy-start | bytes 196
  67.1 1.3 %collective-permute-start.12 = (f32[16,1024]{1,0:T(8,128)S(1)}, f32[16,1024]{1,0:T(8,128)S(1)}, u32[]{:S(2)}, u32[]{:S(2)}) collective-permute-start(f32[16,1024]{1,0:T(8,128)S(1)} %get-tuple-element.55), channel_id=1, source_target_pairs={{0,1},{1,0},{2,3},{3,2},{4,5},{5,4},{6,7},{7,6},{8,9},{9,8},{10,11... | collective-permute-start | bytes 196616 | tf_op jit(solution)/shard_map/ppermute | solution.py:461
  68.4 4.0 %collective-permute-start.13 = (f32[8,1024]{1,0:T(8,128)S(1)}, f32[8,1024]{1,0:T(8,128)S(1)}, u32[]{:S(2)}, u32[]{:S(2)}) collective-permute-start(f32[8,1024]{1,0:T(8,128)S(1)} %get-tuple-element.75), channel_id=1, source_target_pairs={{0,2},{1,15},{2,0},{3,5},{4,6},{5,3},{6,4},{7,9},{8,10},{9,7},{10,... | collective-permute-start | bytes 98312 | tf_op jit(solution)/shard_map/ppermute | solution.py:497
  70.0 3.9 %collective-permute-start.14 = (f32[8,1024]{1,0:T(8,128)S(1)}, f32[8,1024]{1,0:T(8,128)S(1)}, u32[]{:S(2)}, u32[]{:S(2)}) collective-permute-start(f32[8,1024]{1,0:T(8,128)S(1)} %get-tuple-element.74), channel_id=1, source_target_pairs={{0,4},{1,13},{2,6},{3,15},{4,0},{5,9},{6,2},{7,11},{8,12},{9,5},{1... | collective-permute-start | bytes 98312 | tf_op jit(solution)/shard_map/ppermute | solution.py:497
  73.9 3.6 %collective-permute-start.15 = (f32[16,1024]{1,0:T(8,128)S(1)}, f32[16,1024]{1,0:T(8,128)S(1)}, u32[]{:S(2)}, u32[]{:S(2)}) collective-permute-start(f32[16,1024]{1,0:T(8,128)S(1)} %pad_maximum_fusion.2), channel_id=1, source_target_pairs={{0,1},{1,0},{2,3},{3,2},{4,5},{5,4},{6,7},{7,6},{8,9},{9,8},{10,11... | collective-permute-start | bytes 196616 | tf_op jit(solution)/shard_map/ppermute | solution.py:461
  81.0 1.3 %collective-permute-start.16 = (f32[16,1024]{1,0:T(8,128)S(1)}, f32[16,1024]{1,0:T(8,128)S(1)}, u32[]{:S(2)}, u32[]{:S(2)}) collective-permute-start(f32[16,1024]{1,0:T(8,128)S(1)} %get-tuple-element.59), channel_id=1, source_target_pairs={{0,1},{1,0},{2,3},{3,2},{4,5},{5,4},{6,7},{7,6},{8,9},{9,8},{10,11... | collective-permute-start | bytes 196616 | tf_op jit(solution)/shard_map/ppermute | solution.py:461
  82.3 4.0 %collective-permute-start.17 = (f32[8,1024]{1,0:T(8,128)S(1)}, f32[8,1024]{1,0:T(8,128)S(1)}, u32[]{:S(2)}, u32[]{:S(2)}) collective-permute-start(f32[8,1024]{1,0:T(8,128)S(1)} %get-tuple-element.73), channel_id=1, source_target_pairs={{0,2},{1,15},{2,0},{3,5},{4,6},{5,3},{6,4},{7,9},{8,10},{9,7},{10,... | collective-permute-start | bytes 98312 | tf_op jit(solution)/shard_map/ppermute | solution.py:497
  82.4 4.0 %collective-permute-start.18 = (f32[8,1024]{1,0:T(8,128)S(1)}, f32[8,1024]{1,0:T(8,128)S(1)}, u32[]{:S(2)}, u32[]{:S(2)}) collective-permute-start(f32[8,1024]{1,0:T(8,128)S(1)} %get-tuple-element.72), channel_id=1, source_target_pairs={{0,4},{1,13},{2,6},{3,15},{4,0},{5,9},{6,2},{7,11},{8,12},{9,5},{1... | collective-permute-start | bytes 98312 | tf_op jit(solution)/shard_map/ppermute | solution.py:497
  86.4 2.9 %collective-permute-start.19 = (f32[16,1024]{1,0:T(8,128)S(1)}, f32[16,1024]{1,0:T(8,128)S(1)}, u32[]{:S(2)}, u32[]{:S(2)}) collective-permute-start(f32[16,1024]{1,0:T(8,128)S(1)} %pad_maximum_fusion.3), channel_id=1, source_target_pairs={{0,1},{1,0},{2,3},{3,2},{4,5},{5,4},{6,7},{7,6},{8,9},{9,8},{10,11... | collective-permute-start | bytes 196616 | tf_op jit(solution)/shard_map/ppermute | solution.py:461
  92.7 1.7 %collective-permute-start.20 = (f32[80,1024]{1,0:T(8,128)S(1)}, f32[80,1024]{1,0:T(8,128)S(1)}, u32[]{:S(2)}, u32[]{:S(2)}) collective-permute-start(f32[80,1024]{1,0:T(8,128)S(1)} %get-tuple-element.63), channel_id=1, source_target_pairs={{0,1},{1,0},{2,3},{3,2},{4,5},{5,4},{6,7},{7,6},{8,9},{9,8},{10,11... | collective-permute-start | bytes 983048 | tf_op jit(solution)/shard_map/ppermute | solution.py:524
  94.5 6.2 %collective-permute-start.23 = (f32[4,8,1024]{2,1,0:T(8,128)S(1)}, f32[4,8,1024]{2,1,0:T(8,128)S(1)}, u32[]{:S(2)}, u32[]{:S(2)}) collective-permute-start(f32[4,8,1024]{2,1,0:T(8,128)S(1)} %slice_select_fusion), channel_id=1, source_target_pairs={{0,2},{1,3},{2,0},{3,1},{4,6},{5,7},{6,4},{7,5},{8,10},{9,11},{10,... | collective-permute-start | bytes 393224 | tf_op jit(solution)/shard_map/ppermute | solution.py:512
  95.3 5.3 %collective-permute-start.21 = (f32[8,1024]{1,0:T(8,128)S(1)}, f32[8,1024]{1,0:T(8,128)S(1)}, u32[]{:S(2)}, u32[]{:S(2)}) collective-permute-start(f32[8,1024]{1,0:T(8,128)S(1)} %get-tuple-element.69), channel_id=1, source_target_pairs={{0,2},{1,15},{2,0},{3,5},{4,6},{5,3},{6,4},{7,9},{8,10},{9,7},{10,... | collective-permute-start | bytes 98312 | tf_op jit(solution)/shard_map/ppermute | solution.py:497
  96.6 4.0 %collective-permute-start.22 = (f32[8,1024]{1,0:T(8,128)S(1)}, f32[8,1024]{1,0:T(8,128)S(1)}, u32[]{:S(2)}, u32[]{:S(2)}) collective-permute-start(f32[8,1024]{1,0:T(8,128)S(1)} %get-tuple-element.68), channel_id=1, source_target_pairs={{0,4},{1,13},{2,6},{3,15},{4,0},{5,9},{6,2},{7,11},{8,12},{9,5},{1... | collective-permute-start | bytes 98312 | tf_op jit(solution)/shard_map/ppermute | solution.py:497
  100.7 4.3 %collective-permute-start.24 = (f32[2,8,1024]{2,1,0:T(8,128)S(1)}, f32[2,8,1024]{2,1,0:T(8,128)S(1)}, u32[]{:S(2)}, u32[]{:S(2)}) collective-permute-start(f32[2,8,1024]{2,1,0:T(8,128)S(1)} %slice_select_fusion.1), channel_id=1, source_target_pairs={{0,4},{1,5},{2,6},{3,7},{4,0},{5,1},{6,2},{7,3},{8,12},{9,13},{10,... | collective-permute-start | bytes 196616 | tf_op jit(solution)/shard_map/ppermute | solution.py:512
  100.8 5.5 %collective-permute-start.26 = (f32[16,1024]{1,0:T(8,128)S(1)}, f32[16,1024]{1,0:T(8,128)S(1)}, u32[]{:S(2)}, u32[]{:S(2)}) collective-permute-start(f32[16,1024]{1,0:T(8,128)S(1)} %pad_maximum_fusion.4), channel_id=1, source_target_pairs={{0,1},{1,0},{2,3},{3,2},{4,5},{5,4},{6,7},{7,6},{8,9},{9,8},{10,11... | collective-permute-start | bytes 196616 | tf_op jit(solution)/shard_map/ppermute | solution.py:461
  105.1 9.5 %collective-permute-start.25 = (f32[1,8,1024]{2,1,0:T(8,128)S(1)}, f32[1,8,1024]{2,1,0:T(8,128)S(1)}, u32[]{:S(2)}, u32[]{:S(2)}) collective-permute-start(f32[1,8,1024]{2,1,0:T(8,128)S(1)} %get-tuple-element.90), channel_id=1, source_target_pairs={{0,8},{1,9},{2,10},{3,11},{4,12},{5,13},{6,14},{7,15},{8,0},{9,1},... | collective-permute-start | bytes 98312 | tf_op jit(solution)/shard_map/ppermute | solution.py:512

commit v6 on v5

--- a/solution.py
+++ b/solution.py
@@ -35,7 +35,7 @@
     return dot(narrow, spread_ref[0, u]) + dot(narrow, spread_ref[1, u])
 
 
-def spread_kernel(label_ref, x_ref, start_ref, spread_ref, image_ref, mean_ref, ends_ref, centered):
+def spread_kernel(_, label_ref, x_ref, start_ref, spread_ref, image_ref, mean_ref, ends_ref, centered):
     u = pl.program_id(0)
     width = centered.shape[1]
     ones = jnp.ones((DIRS, UNIT), jnp.bfloat16)
@@ -48,11 +48,11 @@
         high = spread.astype(jnp.bfloat16)
         low = (spread - high.astype(jnp.float32)).astype(jnp.bfloat16)
         for h, part in enumerate((high, low)):
-            spread_ref[h, 0, a : a + BLOCK, a:] = part
+            spread_ref[h, u, a : a + BLOCK, a:] = part
             if a + BLOCK < width:
-                spread_ref[h, 0, a + BLOCK :, a : a + BLOCK] = part[:, BLOCK:].T
+                spread_ref[h, u, a + BLOCK :, a : a + BLOCK] = part[:, BLOCK:].T
     narrow = start_ref[...].astype(jnp.bfloat16)
-    image_ref[u] = apply_unit(narrow, spread_ref, 0)
+    image_ref[u] = apply_unit(narrow, spread_ref, u)
 
     @pl.when(u == pl.num_programs(0) - 1)
     def _():
@@ -83,28 +83,28 @@
     return joined
 
 
-def unit_spread(labels, x, start):
+def unit_spread(me, labels, x, start):
     rows, width = x.shape
     units = rows // UNIT
     return pl.pallas_call(
         spread_kernel,
         grid=(units,),
         in_specs=[
-            *smem(1),
+            *smem(2),
             pl.BlockSpec((UNIT, width), lambda u: (u, 0)),
             pl.BlockSpec((DIRS, width), lambda u: (0, 0)),
         ],
-        out_specs=[pl.BlockSpec((2, 1, width, width), lambda u: (0, u, 0, 0)), *vmem(3)],
+        out_specs=vmem(4),
         out_shape=[
-            pltpu.HBM((2, units, width, width), jnp.bfloat16),
+            pltpu.VMEM((2, units, width, width), jnp.bfloat16),
             jax.ShapeDtypeStruct((units, DIRS, width), jnp.float32),
             jax.ShapeDtypeStruct((units, 1, width), jnp.float32),
             jax.ShapeDtypeStruct((4 * DIRS, width), jnp.float32),
         ],
         scratch_shapes=[pltpu.VMEM((UNIT, width), jnp.bfloat16)],
-        compiler_params=pltpu.CompilerParams(vmem_limit_bytes=26 * MIB),
+        compiler_params=pltpu.CompilerParams(vmem_limit_bytes=18 * MIB),
         name="unit_spread",
-    )(labels, x, start)
+    )(me, labels, x, start)
 
 
 def flags(label_ref):
@@ -181,15 +181,11 @@
     ]
 
 
-def multiply(totals, shift, same, spread_ref, out_ref, ends_ref, copies=()):
+def multiply(totals, shift, same, spread_ref, out_ref, ends_ref):
     units = len(totals)
     basis = orthonormal(totals).astype(jnp.bfloat16)
     narrow = [basis[u * DIRS : (u + 1) * DIRS] for u in range(units)]
-    images = []
-    for u in range(units):
-        if copies:
-            copies[u].wait()
-        images.append(apply_unit(narrow[u], spread_ref, u))
+    images = [apply_unit(narrow[u], spread_ref, u) for u in range(units)]
     merge_units(images, narrow, shift, same, out_ref, ends_ref)
 
 
@@ -232,7 +228,9 @@
         flag(tail == chip_tail),
         chip_head,
         chip_tail,
+        *(jnp.where(value, 1.0, jnp.zeros_like(head)) for value in (even, *upward(me_ref[0]))),
     ]
+    mask_ref[...] = jnp.zeros_like(mask_ref)
     for i, line in enumerate(masks):
         mask_ref[i : i + 1] = line
 
@@ -253,7 +251,7 @@
         chip_kernel,
         in_specs=smem(1) + vmem(3),
         out_specs=vmem(3),
-        out_shape=[part, part, jax.ShapeDtypeStruct((DIRS, width), jnp.float32)],
+        out_shape=[part, part, part],
         compiler_params=pltpu.CompilerParams(vmem_limit_bytes=4 * MIB),
         name="join_chip",
     )(me, own, mate, start)
@@ -293,14 +291,10 @@
 
 
 def first_kernel(
-    label_ref, image_ref, mean_ref, mate_ref, side_ref, other_ref, mask_ref, start_ref, source,
-    out_ref, ends_ref, shift_ref, spread_ref, arrived,
+    label_ref, image_ref, mean_ref, mate_ref, side_ref, other_ref, mask_ref, start_ref, spread_ref,
+    out_ref, ends_ref, shift_ref,
 ):
     units = image_ref.shape[0]
-    copies = []
-    for u in range(units):
-        copies.append(pltpu.make_async_copy(source.at[:, u], spread_ref.at[:, u], arrived.at[u]))
-        copies[u].start()
     same, at_first, at_last = flags(label_ref)
     narrow = start_ref[...].astype(jnp.bfloat16)
     outer = []
@@ -317,21 +311,16 @@
         totals.append(joined[0])
         shift.append(mean_ref[u] - joined[1])
         shift_ref[u] = shift[u]
-    multiply(totals, shift, same, spread_ref, out_ref, ends_ref, copies)
+    multiply(totals, shift, same, spread_ref, out_ref, ends_ref)
 
 
 def first_step(labels, images, means, mate, side, other, masks, start, spread):
     units, _, width = images.shape
     return pl.pallas_call(
         first_kernel,
-        in_specs=smem(1) + vmem(7) + [pl.BlockSpec(memory_space=pl.ANY)],
-        out_specs=vmem(4),
-        out_shape=[
-            *image_shapes(units, width),
-            jax.ShapeDtypeStruct((units, 1, width), jnp.float32),
-            pltpu.VMEM(spread.shape, spread.dtype),
-        ],
-        scratch_shapes=[pltpu.SemaphoreType.DMA((units,))],
+        in_specs=smem(1) + vmem(8),
+        out_specs=vmem(3),
+        out_shape=image_shapes(units, width) + [jax.ShapeDtypeStruct((units, 1, width), jnp.float32)],
         compiler_params=pltpu.CompilerParams(vmem_limit_bytes=8 * MIB),
         name="first_step",
     )(labels, images, means, mate, side, other, masks, start, spread)
@@ -443,7 +432,6 @@
     units = rows // UNIT
     chips = n_dp // 2
     me = lax.axis_index("dp")
-    even = (me & 1) == 0
     labels = cluster_ids[::UNIT]
 
     near = (lambda p: p ^ 1, lambda p: (p + 1) % chips if p % 2 else (p - 1) % chips)
@@ -460,7 +448,7 @@
     def swap(both):
         return halves(lax.ppermute(both, "dp", mates))
 
-    def chip_totals(own, mate, joins):
+    def chip_totals(own, mate, joins, even):
         head = jnp.where(even, own[0] + joins[0] * mate[0], mate[0] + joins[0] * own[0])
         tail = jnp.where(even, mate[1] + joins[1] * own[1], own[1] + joins[1] * mate[1])
         return head, tail
@@ -473,26 +461,25 @@
         return first, last_image
 
     embeddings = pltpu.with_memory_space_constraint(embeddings, pltpu.HBM)
-    spread, raw, means, own = unit_spread(labels, embeddings, start_basis)
-
     place = me.reshape(1)
+    spread, raw, means, own = unit_spread(place, labels, embeddings, start_basis)
+
     mate = lax.ppermute(own, "dp", mates)
     near, far, masks = join_chip(place, own, mate, start_basis)
     near, far = (lax.ppermute(part, "dp", link) for part, link in zip((near, far), links))
     side, origins = join_sides(place, near, far, masks, start_basis)
     other = lax.ppermute(side, "dp", mates)
-    images, ends, shift, spread = first_step(
-        labels, raw, means, mate, side, other, masks, start_basis,
-        pltpu.with_memory_space_constraint(spread, pltpu.HBM),
+    images, ends, shift = first_step(
+        labels, raw, means, mate, side, other, masks, start_basis, spread
     )
     joins = masks[0:1], masks[1:2]
+    even, *ups = (masks[i : i + 1] > 0.5 for i in range(8, 11))
     masks = tuple(masks[i : i + 1] for i in range(2, 6))
     sides = [(origins[i : i + 1], origins[i + 1 : i + 2]) for i in (0, 2)]
-    ups = upward(me)
 
     def exchange(ends, mate=None, beside=lambda: ()):
         mate, own = mate or swap(ends), halves(ends)
-        totals = chip_totals(own, mate, joins)
+        totals = chip_totals(own, mate, joins, even)
         arrived = [
             lax.ppermute(jnp.where(up, totals[1], totals[0]), "dp", link) for link, up in zip(links, ups)
         ]

time: 116 us -> 110 us (0.948)
  Pallas kernels: 50.4 us -> 45 us
    pallas_call x2, Pallas kernels: 27.9 us -> 22.4 us  [the longest x1 18.9 us: unit_spread(): pl.pallas_call(spread_kernel, grid=(units,), in_specs=[*smem(2), pl.Block...]
where the time goes in v6:
time: 110 us
  Pallas kernels  45 us (41%)
  waiting for transfers between devices  34 us (31%)
  starting transfers between devices  28.1 us (26%)
  local copies, waits for them, and re-layouts  1.64 us (1%)
    pallas_call x1, Pallas kernels, unit_spread(): pl.pallas_call(spread_kernel, grid=(units,), in_specs=[*smem(2), pl.Block...  18.9 us
    ppermute x10, waiting for transfers between devices, exchange(): lax.ppermute(jnp.where(up, totals[1], totals[0]), 'dp', link)  18.8 us
    ppermute x9, starting transfers between devices, swap(): return halves(lax.ppermute(both, 'dp', mates))  12.7 us
    pallas_call x3, Pallas kernels, step(): pl.pallas_call(step_kernel, in_specs=smem(1) + vmem(5), out_specs=vmem(2)...  9.9 us
    pallas_call x1, Pallas kernels, project(): pl.pallas_call(project_kernel, in_specs=smem(1) + vmem(5) + [pl.BlockSpec...  8.19 us
    ppermute x9, waiting for transfers between devices, swap(): return halves(lax.ppermute(both, 'dp', mates))  7.17 us
    ppermute x2, starting transfers between devices, per_device(): lax.ppermute(part, 'dp', link)  4.51 us
    ppermute x10, starting transfers between devices, exchange(): lax.ppermute(jnp.where(up, totals[1], totals[0]), 'dp', link)  4.14 us
  transfers between devices with their start and end apart: 27, of which 23 were waited for; matrix products, arithmetic and copies ran while one was open for 0% of the time, Pallas kernels for 7%

profile of v6, /device:TPU:0, one launch (start us, length us, event | category | flops | bytes accessed | tf_op | source)
XLA Modules:
  0.0 110.2 jit_solution(17992071874761102305)
XLA Ops:
  2.2 18.9 %unit_spread.1 = (bf16[2,4,1024,1024]{3,2,1,0:T(8,128)(2,1)S(1)}, f32[4,8,1024]{2,1,0:T(8,128)S(1)}, f32[4,1,1024]{2,1,0:T(1,128)S(1)}, f32[32,1024]{1,0:T(8,128)S(1)}) custom-call(s32[1]{0:T(128)} %bitcast._.me_ref, s32[4]{0:T(128)S(1)} %slice.161.label_ref, bf16[8192,1024]{1,0:T(8,128)(2,1)} %source.1, f32[8,1024]{1,0:T(8,128)S(1)} %copy-done), custom_call_target="tpu_custom_call" | custom-call | tf_op jit(solution)/shard_map/unit_spread/pallas_call | solution.py:89
  21.7 1.0 collective-permute-done.mate_ref
  22.8 2.9 %collective-permute-start.1 = (f32[16,1024]{1,0:T(8,128)S(1)}, f32[16,1024]{1,0:T(8,128)S(1)}, u32[]{:S(2)}, u32[]{:S(2)}) collective-permute-start(f32[16,1024]{1,0:T(8,128)S(1)} %get-tuple-element.37), channel_id=1, source_target_pairs={{0,2},{1,15},{2,0},{3,5},{4,6},{5,3},{6,4},{7,9},{8,10},{9,7},{10,... | collective-permute-start | bytes 196616 | tf_op jit(solution)/shard_map/ppermute | solution.py:469
  25.7 1.6 %collective-permute-start.2 = (f32[16,1024]{1,0:T(8,128)S(1)}, f32[16,1024]{1,0:T(8,128)S(1)}, u32[]{:S(2)}, u32[]{:S(2)}) collective-permute-start(f32[16,1024]{1,0:T(8,128)S(1)} %get-tuple-element.38), channel_id=1, source_target_pairs={{0,4},{1,13},{2,6},{3,15},{4,0},{5,9},{6,2},{7,11},{8,12},{9,5},{1... | collective-permute-start | bytes 196616 | tf_op jit(solution)/shard_map/ppermute | solution.py:469
  27.3 0.9 collective-permute-done.1.near_ref
  28.2 1.7 %collective-permute-done.2.far_ref = f32[16,1024]{1,0:T(8,128)S(1)} collective-permute-done((f32[16,1024]{1,0:T(8,128)S(1)}, f32[16,1024]{1,0:T(8,128)S(1)}, u32[]{:S(2)}, u32[]{:S(2)}) %collective-permute-start.2) | collective-permute-done | bytes 65568 | tf_op jit(solution)/shard_map/ppermute | solution.py:469
  30.1 3.6 %collective-permute-start.3 = (f32[32,1024]{1,0:T(8,128)S(1)}, f32[32,1024]{1,0:T(8,128)S(1)}, u32[]{:S(2)}, u32[]{:S(2)}) collective-permute-start(f32[32,1024]{1,0:T(8,128)S(1)} %get-tuple-element.40.side_ref), channel_id=1, source_target_pairs={{0,1},{1,0},{2,3},{3,2},{4,5},{5,4},{6,7},{7,6},{8,9},{9,8},{10,11... | collective-permute-start | bytes 393224 | tf_op jit(solution)/shard_map/ppermute | solution.py:471
  33.7 1.0 collective-permute-done.3.other_ref
  34.7 3.5 %first_step.1 = (f32[4,8,1024]{2,1,0:T(8,128)S(1)}, f32[16,1024]{1,0:T(8,128)S(1)}, f32[4,1,1024]{2,1,0:T(1,128)S(1)}) custom-call(s32[4]{0:T(128)S(1)} %slice.161.label_ref, f32[4,8,1024]{2,1,0:T(8,128)S(1)} %get-tuple-element.34.image_ref, f32[4,1,1024]{2,1,0:T(1,128)S(1)} %get-tuple-element.35.mean_ref, f32[32,1024]{1,0:T(8,128)S(1)} %collective-permute-done.mate_ref, ...), custom_call_target="tpu_custom_call" | custom-call | tf_op jit(solution)/shard_map/first_step/pallas_call | solution.py:319
  39.7 3.8 %collective-permute-done.5 = f32[8,1024]{1,0:T(8,128)S(1)} collective-permute-done((f32[8,1024]{1,0:T(8,128)S(1)}, f32[8,1024]{1,0:T(8,128)S(1)}, u32[]{:S(2)}, u32[]{:S(2)}) %collective-permute-start.5) | collective-permute-done | bytes 32800 | tf_op jit(solution)/shard_map/ppermute | solution.py:484
  43.6 2.0 %collective-permute-start.7 = (f32[16,1024]{1,0:T(8,128)S(1)}, f32[16,1024]{1,0:T(8,128)S(1)}, u32[]{:S(2)}, u32[]{:S(2)}) collective-permute-start(f32[16,1024]{1,0:T(8,128)S(1)} %pad_maximum_fusion), channel_id=1, source_target_pairs={{0,1},{1,0},{2,3},{3,2},{4,5},{5,4},{6,7},{7,6},{8,9},{9,8},{10,11... | collective-permute-start | bytes 196616 | tf_op jit(solution)/shard_map/ppermute | solution.py:449
  46.6 3.2 %step.3 = (f32[4,8,1024]{2,1,0:T(8,128)S(1)}, f32[16,1024]{1,0:T(8,128)S(1)}) custom-call(s32[4]{0:T(128)S(1)} %slice.161.label_ref, f32[4,8,1024]{2,1,0:T(8,128)S(1)} %get-tuple-element.42.image_ref, f32[8,1024]{1,0:T(8,128)S(1)} %get-tuple-element.88.first_ref, f32[8,1024]{1,0:T(8,128)S(1)} %get-tuple-element.87.last_ref, ...), custom_call_target="tpu_custom_call" | custom-call | tf_op jit(solution)/shard_map/step/pallas_call | solution.py:356
  50.2 0.9 collective-permute-done.8
  52.1 3.0 %collective-permute-done.10 = f32[8,1024]{1,0:T(8,128)S(1)} collective-permute-done((f32[8,1024]{1,0:T(8,128)S(1)}, f32[8,1024]{1,0:T(8,128)S(1)}, u32[]{:S(2)}, u32[]{:S(2)}) %collective-permute-start.10) | collective-permute-done | bytes 32800 | tf_op jit(solution)/shard_map/ppermute | solution.py:484
  55.2 2.3 %collective-permute-start.11 = (f32[16,1024]{1,0:T(8,128)S(1)}, f32[16,1024]{1,0:T(8,128)S(1)}, u32[]{:S(2)}, u32[]{:S(2)}) collective-permute-start(f32[16,1024]{1,0:T(8,128)S(1)} %pad_maximum_fusion.1), channel_id=1, source_target_pairs={{0,1},{1,0},{2,3},{3,2},{4,5},{5,4},{6,7},{7,6},{8,9},{9,8},{10,11... | collective-permute-start | bytes 196616 | tf_op jit(solution)/shard_map/ppermute | solution.py:449
  58.4 3.2 %step.4 = (f32[4,8,1024]{2,1,0:T(8,128)S(1)}, f32[16,1024]{1,0:T(8,128)S(1)}) custom-call(s32[4]{0:T(128)S(1)} %slice.161.label_ref, f32[4,8,1024]{2,1,0:T(8,128)S(1)} %get-tuple-element.48.image_ref, f32[8,1024]{1,0:T(8,128)S(1)} %get-tuple-element.86.first_ref, f32[8,1024]{1,0:T(8,128)S(1)} %get-tuple-element.85.last_ref, ...), custom_call_target="tpu_custom_call" | custom-call | tf_op jit(solution)/shard_map/step/pallas_call | solution.py:356
  63.0 1.6 %collective-permute-start.13 = (f32[8,1024]{1,0:T(8,128)S(1)}, f32[8,1024]{1,0:T(8,128)S(1)}, u32[]{:S(2)}, u32[]{:S(2)}) collective-permute-start(f32[8,1024]{1,0:T(8,128)S(1)} %get-tuple-element.76), channel_id=1, source_target_pairs={{0,2},{1,15},{2,0},{3,5},{4,6},{5,3},{6,4},{7,9},{8,10},{9,7},{10,... | collective-permute-start | bytes 98312 | tf_op jit(solution)/shard_map/ppermute | solution.py:484
  64.6 2.4 %collective-permute-done.13 = f32[8,1024]{1,0:T(8,128)S(1)} collective-permute-done((f32[8,1024]{1,0:T(8,128)S(1)}, f32[8,1024]{1,0:T(8,128)S(1)}, u32[]{:S(2)}, u32[]{:S(2)}) %collective-permute-start.13) | collective-permute-done | bytes 32800 | tf_op jit(solution)/shard_map/ppermute | solution.py:484
  67.0 1.5 %collective-permute-done.14 = f32[8,1024]{1,0:T(8,128)S(1)} collective-permute-done((f32[8,1024]{1,0:T(8,128)S(1)}, f32[8,1024]{1,0:T(8,128)S(1)}, u32[]{:S(2)}, u32[]{:S(2)}) %collective-permute-start.14) | collective-permute-done | bytes 32800 | tf_op jit(solution)/shard_map/ppermute | solution.py:484
  68.6 2.7 %collective-permute-start.15 = (f32[16,1024]{1,0:T(8,128)S(1)}, f32[16,1024]{1,0:T(8,128)S(1)}, u32[]{:S(2)}, u32[]{:S(2)}) collective-permute-start(f32[16,1024]{1,0:T(8,128)S(1)} %pad_maximum_fusion.2), channel_id=1, source_target_pairs={{0,1},{1,0},{2,3},{3,2},{4,5},{5,4},{6,7},{7,6},{8,9},{9,8},{10,11... | collective-permute-start | bytes 196616 | tf_op jit(solution)/shard_map/ppermute | solution.py:449
  72.1 3.4 %step.5 = (f32[4,8,1024]{2,1,0:T(8,128)S(1)}, f32[16,1024]{1,0:T(8,128)S(1)}) custom-call(s32[4]{0:T(128)S(1)} %slice.161.label_ref, f32[4,8,1024]{2,1,0:T(8,128)S(1)} %get-tuple-element.52.image_ref, f32[8,1024]{1,0:T(8,128)S(1)} %get-tuple-element.84.first_ref, f32[8,1024]{1,0:T(8,128)S(1)} %get-tuple-element.83.last_ref, ...), custom_call_target="tpu_custom_call" | custom-call | tf_op jit(solution)/shard_map/step/pallas_call | solution.py:356
  77.1 3.8 %collective-permute-done.17 = f32[8,1024]{1,0:T(8,128)S(1)} collective-permute-done((f32[8,1024]{1,0:T(8,128)S(1)}, f32[8,1024]{1,0:T(8,128)S(1)}, u32[]{:S(2)}, u32[]{:S(2)}) %collective-permute-start.17) | collective-permute-done | bytes 32800 | tf_op jit(solution)/shard_map/ppermute | solution.py:484
  81.0 2.0 %collective-permute-start.19 = (f32[16,1024]{1,0:T(8,128)S(1)}, f32[16,1024]{1,0:T(8,128)S(1)}, u32[]{:S(2)}, u32[]{:S(2)}) collective-permute-start(f32[16,1024]{1,0:T(8,128)S(1)} %pad_maximum_fusion.3), channel_id=1, source_target_pairs={{0,1},{1,0},{2,3},{3,2},{4,5},{5,4},{6,7},{7,6},{8,9},{9,8},{10,11... | collective-permute-start | bytes 196616 | tf_op jit(solution)/shard_map/ppermute | solution.py:449
  84.0 3.3 %step_and_route.1 = (f32[4,8,1024]{2,1,0:T(8,128)S(1)}, f32[80,1024]{1,0:T(8,128)S(1)}, f32[64,1024]{1,0:T(8,128)S(1)}) custom-call(s32[16]{0:T(128)S(1)} %copy-done.1, s32[1]{0:T(128)} %bitcast._.me_ref, s32[4]{0:T(128)S(1)} %slice.161.label_ref, f32[4,8,1024]{2,1,0:T(8,128)S(1)} %get-tuple-element.56.refs_0_, f32[8,1024]{1,0:T(8,128)S(1)} %get-tuple-element.82.refs_1_, ...), custom_call_target="tpu_custom_call" | custom-call | tf_op jit(solution)/shard_map/step_and_route/pallas_call | solution.py:372
  87.7 1.3 %collective-permute-done.20 = f32[80,1024]{1,0:T(8,128)S(1)} collective-permute-done((f32[80,1024]{1,0:T(8,128)S(1)}, f32[80,1024]{1,0:T(8,128)S(1)}, u32[]{:S(2)}, u32[]{:S(2)}) %collective-permute-start.20) | collective-permute-done | bytes 327712 | tf_op jit(solution)/shard_map/ppermute | solution.py:511
  89.9 1.3 %collective-permute-start.21 = (f32[8,1024]{1,0:T(8,128)S(1)}, f32[8,1024]{1,0:T(8,128)S(1)}, u32[]{:S(2)}, u32[]{:S(2)}) collective-permute-start(f32[8,1024]{1,0:T(8,128)S(1)} %get-tuple-element.70), channel_id=1, source_target_pairs={{0,2},{1,15},{2,0},{3,5},{4,6},{5,3},{6,4},{7,9},{8,10},{9,7},{10,... | collective-permute-start | bytes 98312 | tf_op jit(solution)/shard_map/ppermute | solution.py:484
  91.3 4.0 %collective-permute-done.21 = f32[8,1024]{1,0:T(8,128)S(1)} collective-permute-done((f32[8,1024]{1,0:T(8,128)S(1)}, f32[8,1024]{1,0:T(8,128)S(1)}, u32[]{:S(2)}, u32[]{:S(2)}) %collective-permute-start.21) | collective-permute-done | bytes 32800 | tf_op jit(solution)/shard_map/ppermute | solution.py:484
  95.4 2.1 %collective-permute-start.26 = (f32[16,1024]{1,0:T(8,128)S(1)}, f32[16,1024]{1,0:T(8,128)S(1)}, u32[]{:S(2)}, u32[]{:S(2)}) collective-permute-start(f32[16,1024]{1,0:T(8,128)S(1)} %pad_maximum_fusion.4), channel_id=1, source_target_pairs={{0,1},{1,0},{2,3},{3,2},{4,5},{5,4},{6,7},{7,6},{8,9},{9,8},{10,11... | collective-permute-start | bytes 196616 | tf_op jit(solution)/shard_map/ppermute | solution.py:449
  97.5 2.1 %collective-permute-done.24 = f32[2,8,1024]{2,1,0:T(8,128)S(1)} collective-permute-done((f32[2,8,1024]{2,1,0:T(8,128)S(1)}, f32[2,8,1024]{2,1,0:T(8,128)S(1)}, u32[]{:S(2)}, u32[]{:S(2)}) %collective-permute-start.24) | collective-permute-done | bytes 65568 | tf_op jit(solution)/shard_map/ppermute | solution.py:499
  99.7 1.3 %collective-permute-start.25 = (f32[1,8,1024]{2,1,0:T(8,128)S(1)}, f32[1,8,1024]{2,1,0:T(8,128)S(1)}, u32[]{:S(2)}, u32[]{:S(2)}) collective-permute-start(f32[1,8,1024]{2,1,0:T(8,128)S(1)} %get-tuple-element.91), channel_id=1, source_target_pairs={{0,8},{1,9},{2,10},{3,11},{4,12},{5,13},{6,14},{7,15},{8,0},{9,1},... | collective-permute-start | bytes 98312 | tf_op jit(solution)/shard_map/ppermute | solution.py:499
  101.0 8.2 %project.1 = f32[8,8192]{1,0:T(8,128)} custom-call(s32[4]{0:T(128)S(1)} %slice.161.label_ref, f32[4,8,1024]{2,1,0:T(8,128)S(1)} %get-tuple-element.63.image_ref, f32[8,1024]{1,0:T(8,128)S(1)} %get-tuple-element.72.first_ref, f32[8,1024]{1,0:T(8,128)S(1)} %get-tuple-element.71.last_ref, f32[4,1,1024]{2,1,0:T(1,128)S(1)} %get-tuple-element.35.mean_ref, ...), custom_call_target="tpu_custom_call" | custom-call | flops 4294967296 | bytes 16777216 | tf_op jit(solution)/shard_map/project/pallas_call | solution.py:401
  109.2 1.0 finish.1
  (66 shorter events, 13.6 us)
Async XLA Ops:
  1.5 0.8 copy-start
  21.2 1.5 %collective-permute-start = (f32[32,1024]{1,0:T(8,128)S(1)}, f32[32,1024]{1,0:T(8,128)S(1)}, u32[]{:S(2)}, u32[]{:S(2)}) collective-permute-start(f32[32,1024]{1,0:T(8,128)S(1)} %get-tuple-element.36.own_ref), channel_id=1, source_target_pairs={{0,1},{1,0},{2,3},{3,2},{4,5},{5,4},{6,7},{7,6},{8,9},{9,8},{10,11... | collective-permute-start | bytes 393224 | tf_op jit(solution)/shard_map/ppermute | solution.py:467
  22.8 5.5 %collective-permute-start.1 = (f32[16,1024]{1,0:T(8,128)S(1)}, f32[16,1024]{1,0:T(8,128)S(1)}, u32[]{:S(2)}, u32[]{:S(2)}) collective-permute-start(f32[16,1024]{1,0:T(8,128)S(1)} %get-tuple-element.37), channel_id=1, source_target_pairs={{0,2},{1,15},{2,0},{3,5},{4,6},{5,3},{6,4},{7,9},{8,10},{9,7},{10,... | collective-permute-start | bytes 196616 | tf_op jit(solution)/shard_map/ppermute | solution.py:469
  25.7 4.3 %collective-permute-start.2 = (f32[16,1024]{1,0:T(8,128)S(1)}, f32[16,1024]{1,0:T(8,128)S(1)}, u32[]{:S(2)}, u32[]{:S(2)}) collective-permute-start(f32[16,1024]{1,0:T(8,128)S(1)} %get-tuple-element.38), channel_id=1, source_target_pairs={{0,4},{1,13},{2,6},{3,15},{4,0},{5,9},{6,2},{7,11},{8,12},{9,5},{1... | collective-permute-start | bytes 196616 | tf_op jit(solution)/shard_map/ppermute | solution.py:469
  30.1 4.6 %collective-permute-start.3 = (f32[32,1024]{1,0:T(8,128)S(1)}, f32[32,1024]{1,0:T(8,128)S(1)}, u32[]{:S(2)}, u32[]{:S(2)}) collective-permute-start(f32[32,1024]{1,0:T(8,128)S(1)} %get-tuple-element.40.side_ref), channel_id=1, source_target_pairs={{0,1},{1,0},{2,3},{3,2},{4,5},{5,4},{6,7},{7,6},{8,9},{9,8},{10,11... | collective-permute-start | bytes 393224 | tf_op jit(solution)/shard_map/ppermute | solution.py:471
  38.2 1.3 %collective-permute-start.4 = (f32[16,1024]{1,0:T(8,128)S(1)}, f32[16,1024]{1,0:T(8,128)S(1)}, u32[]{:S(2)}, u32[]{:S(2)}) collective-permute-start(f32[16,1024]{1,0:T(8,128)S(1)} %get-tuple-element.44), channel_id=1, source_target_pairs={{0,1},{1,0},{2,3},{3,2},{4,5},{5,4},{6,7},{7,6},{8,9},{9,8},{10,11... | collective-permute-start | bytes 196616 | tf_op jit(solution)/shard_map/ppermute | solution.py:449
  39.5 4.0 %collective-permute-start.5 = (f32[8,1024]{1,0:T(8,128)S(1)}, f32[8,1024]{1,0:T(8,128)S(1)}, u32[]{:S(2)}, u32[]{:S(2)}) collective-permute-start(f32[8,1024]{1,0:T(8,128)S(1)} %get-tuple-element.80), channel_id=1, source_target_pairs={{0,2},{1,15},{2,0},{3,5},{4,6},{5,3},{6,4},{7,9},{8,10},{9,7},{10,... | collective-permute-start | bytes 98312 | tf_op jit(solution)/shard_map/ppermute | solution.py:484
  39.6 4.0 %collective-permute-start.6 = (f32[8,1024]{1,0:T(8,128)S(1)}, f32[8,1024]{1,0:T(8,128)S(1)}, u32[]{:S(2)}, u32[]{:S(2)}) collective-permute-start(f32[8,1024]{1,0:T(8,128)S(1)} %get-tuple-element.79), channel_id=1, source_target_pairs={{0,4},{1,13},{2,6},{3,15},{4,0},{5,9},{6,2},{7,11},{8,12},{9,5},{1... | collective-permute-start | bytes 98312 | tf_op jit(solution)/shard_map/ppermute | solution.py:484
  43.6 2.9 %collective-permute-start.7 = (f32[16,1024]{1,0:T(8,128)S(1)}, f32[16,1024]{1,0:T(8,128)S(1)}, u32[]{:S(2)}, u32[]{:S(2)}) collective-permute-start(f32[16,1024]{1,0:T(8,128)S(1)} %pad_maximum_fusion), channel_id=1, source_target_pairs={{0,1},{1,0},{2,3},{3,2},{4,5},{5,4},{6,7},{7,6},{8,9},{9,8},{10,11... | collective-permute-start | bytes 196616 | tf_op jit(solution)/shard_map/ppermute | solution.py:449
  49.8 1.3 %collective-permute-start.8 = (f32[16,1024]{1,0:T(8,128)S(1)}, f32[16,1024]{1,0:T(8,128)S(1)}, u32[]{:S(2)}, u32[]{:S(2)}) collective-permute-start(f32[16,1024]{1,0:T(8,128)S(1)} %get-tuple-element.49), channel_id=1, source_target_pairs={{0,1},{1,0},{2,3},{3,2},{4,5},{5,4},{6,7},{7,6},{8,9},{9,8},{10,11... | collective-permute-start | bytes 196616 | tf_op jit(solution)/shard_map/ppermute | solution.py:449
  51.1 4.0 %collective-permute-start.10 = (f32[8,1024]{1,0:T(8,128)S(1)}, f32[8,1024]{1,0:T(8,128)S(1)}, u32[]{:S(2)}, u32[]{:S(2)}) collective-permute-start(f32[8,1024]{1,0:T(8,128)S(1)} %get-tuple-element.77), channel_id=1, source_target_pairs={{0,4},{1,13},{2,6},{3,15},{4,0},{5,9},{6,2},{7,11},{8,12},{9,5},{1... | collective-permute-start | bytes 98312 | tf_op jit(solution)/shard_map/ppermute | solution.py:484
  51.2 4.0 %collective-permute-start.9 = (f32[8,1024]{1,0:T(8,128)S(1)}, f32[8,1024]{1,0:T(8,128)S(1)}, u32[]{:S(2)}, u32[]{:S(2)}) collective-permute-start(f32[8,1024]{1,0:T(8,128)S(1)} %get-tuple-element.78), channel_id=1, source_target_pairs={{0,2},{1,15},{2,0},{3,5},{4,6},{5,3},{6,4},{7,9},{8,10},{9,7},{10,... | collective-permute-start | bytes 98312 | tf_op jit(solution)/shard_map/ppermute | solution.py:484
  55.2 3.2 %collective-permute-start.11 = (f32[16,1024]{1,0:T(8,128)S(1)}, f32[16,1024]{1,0:T(8,128)S(1)}, u32[]{:S(2)}, u32[]{:S(2)}) collective-permute-start(f32[16,1024]{1,0:T(8,128)S(1)} %pad_maximum_fusion.1), channel_id=1, source_target_pairs={{0,1},{1,0},{2,3},{3,2},{4,5},{5,4},{6,7},{7,6},{8,9},{9,8},{10,11... | collective-permute-start | bytes 196616 | tf_op jit(solution)/shard_map/ppermute | solution.py:449
  58.4 25.6 %copy-start.1 = (s32[16]{0:T(128)S(1)}, s32[16]{0:T(128)}, u32[]{:S(2)}) copy-start(s32[16]{0:T(128)} %owner_ref.1) | copy-start | bytes 196
  61.7 1.3 %collective-permute-start.12 = (f32[16,1024]{1,0:T(8,128)S(1)}, f32[16,1024]{1,0:T(8,128)S(1)}, u32[]{:S(2)}, u32[]{:S(2)}) collective-permute-start(f32[16,1024]{1,0:T(8,128)S(1)} %get-tuple-element.53), channel_id=1, source_target_pairs={{0,1},{1,0},{2,3},{3,2},{4,5},{5,4},{6,7},{7,6},{8,9},{9,8},{10,11... | collective-permute-start | bytes 196616 | tf_op jit(solution)/shard_map/ppermute | solution.py:449
  63.0 4.0 %collective-permute-start.13 = (f32[8,1024]{1,0:T(8,128)S(1)}, f32[8,1024]{1,0:T(8,128)S(1)}, u32[]{:S(2)}, u32[]{:S(2)}) collective-permute-start(f32[8,1024]{1,0:T(8,128)S(1)} %get-tuple-element.76), channel_id=1, source_target_pairs={{0,2},{1,15},{2,0},{3,5},{4,6},{5,3},{6,4},{7,9},{8,10},{9,7},{10,... | collective-permute-start | bytes 98312 | tf_op jit(solution)/shard_map/ppermute | solution.py:484
  64.6 3.9 %collective-permute-start.14 = (f32[8,1024]{1,0:T(8,128)S(1)}, f32[8,1024]{1,0:T(8,128)S(1)}, u32[]{:S(2)}, u32[]{:S(2)}) collective-permute-start(f32[8,1024]{1,0:T(8,128)S(1)} %get-tuple-element.75), channel_id=1, source_target_pairs={{0,4},{1,13},{2,6},{3,15},{4,0},{5,9},{6,2},{7,11},{8,12},{9,5},{1... | collective-permute-start | bytes 98312 | tf_op jit(solution)/shard_map/ppermute | solution.py:484
  68.6 3.6 %collective-permute-start.15 = (f32[16,1024]{1,0:T(8,128)S(1)}, f32[16,1024]{1,0:T(8,128)S(1)}, u32[]{:S(2)}, u32[]{:S(2)}) collective-permute-start(f32[16,1024]{1,0:T(8,128)S(1)} %pad_maximum_fusion.2), channel_id=1, source_target_pairs={{0,1},{1,0},{2,3},{3,2},{4,5},{5,4},{6,7},{7,6},{8,9},{9,8},{10,11... | collective-permute-start | bytes 196616 | tf_op jit(solution)/shard_map/ppermute | solution.py:449
  75.6 1.3 %collective-permute-start.16 = (f32[16,1024]{1,0:T(8,128)S(1)}, f32[16,1024]{1,0:T(8,128)S(1)}, u32[]{:S(2)}, u32[]{:S(2)}) collective-permute-start(f32[16,1024]{1,0:T(8,128)S(1)} %get-tuple-element.57), channel_id=1, source_target_pairs={{0,1},{1,0},{2,3},{3,2},{4,5},{5,4},{6,7},{7,6},{8,9},{9,8},{10,11... | collective-permute-start | bytes 196616 | tf_op jit(solution)/shard_map/ppermute | solution.py:449
  76.9 4.0 %collective-permute-start.17 = (f32[8,1024]{1,0:T(8,128)S(1)}, f32[8,1024]{1,0:T(8,128)S(1)}, u32[]{:S(2)}, u32[]{:S(2)}) collective-permute-start(f32[8,1024]{1,0:T(8,128)S(1)} %get-tuple-element.74), channel_id=1, source_target_pairs={{0,2},{1,15},{2,0},{3,5},{4,6},{5,3},{6,4},{7,9},{8,10},{9,7},{10,... | collective-permute-start | bytes 98312 | tf_op jit(solution)/shard_map/ppermute | solution.py:484
  77.0 4.0 %collective-permute-start.18 = (f32[8,1024]{1,0:T(8,128)S(1)}, f32[8,1024]{1,0:T(8,128)S(1)}, u32[]{:S(2)}, u32[]{:S(2)}) collective-permute-start(f32[8,1024]{1,0:T(8,128)S(1)} %get-tuple-element.73), channel_id=1, source_target_pairs={{0,4},{1,13},{2,6},{3,15},{4,0},{5,9},{6,2},{7,11},{8,12},{9,5},{1... | collective-permute-start | bytes 98312 | tf_op jit(solution)/shard_map/ppermute | solution.py:484
  81.0 2.9 %collective-permute-start.19 = (f32[16,1024]{1,0:T(8,128)S(1)}, f32[16,1024]{1,0:T(8,128)S(1)}, u32[]{:S(2)}, u32[]{:S(2)}) collective-permute-start(f32[16,1024]{1,0:T(8,128)S(1)} %pad_maximum_fusion.3), channel_id=1, source_target_pairs={{0,1},{1,0},{2,3},{3,2},{4,5},{5,4},{6,7},{7,6},{8,9},{9,8},{10,11... | collective-permute-start | bytes 196616 | tf_op jit(solution)/shard_map/ppermute | solution.py:449
  87.3 1.7 %collective-permute-start.20 = (f32[80,1024]{1,0:T(8,128)S(1)}, f32[80,1024]{1,0:T(8,128)S(1)}, u32[]{:S(2)}, u32[]{:S(2)}) collective-permute-start(f32[80,1024]{1,0:T(8,128)S(1)} %get-tuple-element.61), channel_id=1, source_target_pairs={{0,1},{1,0},{2,3},{3,2},{4,5},{5,4},{6,7},{7,6},{8,9},{9,8},{10,11... | collective-permute-start | bytes 983048 | tf_op jit(solution)/shard_map/ppermute | solution.py:511
  89.1 6.2 %collective-permute-start.23 = (f32[4,8,1024]{2,1,0:T(8,128)S(1)}, f32[4,8,1024]{2,1,0:T(8,128)S(1)}, u32[]{:S(2)}, u32[]{:S(2)}) collective-permute-start(f32[4,8,1024]{2,1,0:T(8,128)S(1)} %slice_select_fusion), channel_id=1, source_target_pairs={{0,2},{1,3},{2,0},{3,1},{4,6},{5,7},{6,4},{7,5},{8,10},{9,11},{10,... | collective-permute-start | bytes 393224 | tf_op jit(solution)/shard_map/ppermute | solution.py:499
  89.9 5.3 %collective-permute-start.21 = (f32[8,1024]{1,0:T(8,128)S(1)}, f32[8,1024]{1,0:T(8,128)S(1)}, u32[]{:S(2)}, u32[]{:S(2)}) collective-permute-start(f32[8,1024]{1,0:T(8,128)S(1)} %get-tuple-element.70), channel_id=1, source_target_pairs={{0,2},{1,15},{2,0},{3,5},{4,6},{5,3},{6,4},{7,9},{8,10},{9,7},{10,... | collective-permute-start | bytes 98312 | tf_op jit(solution)/shard_map/ppermute | solution.py:484
  91.3 4.0 %collective-permute-start.22 = (f32[8,1024]{1,0:T(8,128)S(1)}, f32[8,1024]{1,0:T(8,128)S(1)}, u32[]{:S(2)}, u32[]{:S(2)}) collective-permute-start(f32[8,1024]{1,0:T(8,128)S(1)} %get-tuple-element.69), channel_id=1, source_target_pairs={{0,4},{1,13},{2,6},{3,15},{4,0},{5,9},{6,2},{7,11},{8,12},{9,5},{1... | collective-permute-start | bytes 98312 | tf_op jit(solution)/shard_map/ppermute | solution.py:484
  95.3 4.3 %collective-permute-start.24 = (f32[2,8,1024]{2,1,0:T(8,128)S(1)}, f32[2,8,1024]{2,1,0:T(8,128)S(1)}, u32[]{:S(2)}, u32[]{:S(2)}) collective-permute-start(f32[2,8,1024]{2,1,0:T(8,128)S(1)} %slice_select_fusion.1), channel_id=1, source_target_pairs={{0,4},{1,5},{2,6},{3,7},{4,0},{5,1},{6,2},{7,3},{8,12},{9,13},{10,... | collective-permute-start | bytes 196616 | tf_op jit(solution)/shard_map/ppermute | solution.py:499
  95.4 5.5 %collective-permute-start.26 = (f32[16,1024]{1,0:T(8,128)S(1)}, f32[16,1024]{1,0:T(8,128)S(1)}, u32[]{:S(2)}, u32[]{:S(2)}) collective-permute-start(f32[16,1024]{1,0:T(8,128)S(1)} %pad_maximum_fusion.4), channel_id=1, source_target_pairs={{0,1},{1,0},{2,3},{3,2},{4,5},{5,4},{6,7},{7,6},{8,9},{9,8},{10,11... | collective-permute-start | bytes 196616 | tf_op jit(solution)/shard_map/ppermute | solution.py:449
  99.7 9.5 %collective-permute-start.25 = (f32[1,8,1024]{2,1,0:T(8,128)S(1)}, f32[1,8,1024]{2,1,0:T(8,128)S(1)}, u32[]{:S(2)}, u32[]{:S(2)}) collective-permute-start(f32[1,8,1024]{2,1,0:T(8,128)S(1)} %get-tuple-element.91), channel_id=1, source_target_pairs={{0,8},{1,9},{2,10},{3,11},{4,12},{5,13},{6,14},{7,15},{8,0},{9,1},... | collective-permute-start | bytes 98312 | tf_op jit(solution)/shard_map/ppermute | solution.py:499

commit v7 on v6

--- a/solution.py
+++ b/solution.py
@@ -22,27 +22,38 @@
     )
 
 
-def fetch(source, target, arrived, first, size):
-    copies = []
-    for i in range(target.shape[0] // size):
-        part = source.at[pl.ds(first + i * size, size)]
-        copies.append(pltpu.make_async_copy(part, target.at[pl.ds(i * size, size)], arrived.at[i]))
-        copies[-1].start()
-    return copies
-
-
 def apply_unit(narrow, spread_ref, u):
     return dot(narrow, spread_ref[0, u]) + dot(narrow, spread_ref[1, u])
 
 
-def spread_kernel(_, label_ref, x_ref, start_ref, spread_ref, image_ref, mean_ref, ends_ref, centered):
+def spread_kernel(
+    _, label_ref, source, start_ref, spread_ref, image_ref, mean_ref, ends_ref, x_ref, centered, arrived
+):
     u = pl.program_id(0)
     width = centered.shape[1]
+
+    def copy(v):
+        part = pl.ds(pl.multiple_of(v * UNIT, UNIT), UNIT)
+        return pltpu.make_async_copy(source.at[part], x_ref.at[part], arrived.at[v])
+
+    @pl.when(u == 0)
+    def _():
+        copy(0).start()
+
+    def rows(a, size):
+        return x_ref[pl.ds(pl.multiple_of(u * UNIT + a, BLOCK), size)]
+
+    copy(u).wait()
+
+    @pl.when(u + 1 < pl.num_programs(0))
+    def _():
+        copy(u + 1).start()
+
     ones = jnp.ones((DIRS, UNIT), jnp.bfloat16)
-    mean = dot(ones, x_ref[...])[:1] * (1 / UNIT)
+    mean = dot(ones, rows(0, UNIT))[:1] * (1 / UNIT)
     mean_ref[u] = mean
     for a in range(0, UNIT, BLOCK):
-        centered[a : a + BLOCK] = (x_ref[a : a + BLOCK].astype(jnp.float32) - mean).astype(jnp.bfloat16)
+        centered[a : a + BLOCK] = (rows(a, BLOCK).astype(jnp.float32) - mean).astype(jnp.bfloat16)
     for a in range(0, width, BLOCK):
         spread = dot(centered[:, a : a + BLOCK], centered[:, a:], ((0,), (0,)))
         high = spread.astype(jnp.bfloat16)
@@ -91,18 +102,19 @@
         grid=(units,),
         in_specs=[
             *smem(2),
-            pl.BlockSpec((UNIT, width), lambda u: (u, 0)),
+            pl.BlockSpec(memory_space=pl.ANY),
             pl.BlockSpec((DIRS, width), lambda u: (0, 0)),
         ],
-        out_specs=vmem(4),
+        out_specs=vmem(5),
         out_shape=[
             pltpu.VMEM((2, units, width, width), jnp.bfloat16),
             jax.ShapeDtypeStruct((units, DIRS, width), jnp.float32),
             jax.ShapeDtypeStruct((units, 1, width), jnp.float32),
             jax.ShapeDtypeStruct((4 * DIRS, width), jnp.float32),
+            pltpu.VMEM((rows, width), x.dtype),
         ],
-        scratch_shapes=[pltpu.VMEM((UNIT, width), jnp.bfloat16)],
-        compiler_params=pltpu.CompilerParams(vmem_limit_bytes=18 * MIB),
+        scratch_shapes=[pltpu.VMEM((UNIT, width), jnp.bfloat16), pltpu.SemaphoreType.DMA((units,))],
+        compiler_params=pltpu.CompilerParams(vmem_limit_bytes=12 * MIB),
         name="unit_spread",
     )(me, labels, x, start)
 
@@ -229,6 +241,7 @@
         chip_head,
         chip_tail,
         *(jnp.where(value, 1.0, jnp.zeros_like(head)) for value in (even, *upward(me_ref[0]))),
+        *(jnp.where(((me_ref[0] >> b) & 1) == 1, 1.0, jnp.zeros_like(head)) for b in range(1, 6)),
     ]
     mask_ref[...] = jnp.zeros_like(mask_ref)
     for i, line in enumerate(masks):
@@ -379,20 +392,16 @@
     )(owners, me, labels, images, first, last_image, shift, spread)
 
 
-def project_kernel(
-    label_ref, image_ref, first_ref, last_ref, mean_ref, shift_ref, source, out_ref, x_ref, arrived
-):
-    copies = fetch(source, x_ref, arrived, 0, PART)
+def project_kernel(label_ref, image_ref, first_ref, last_ref, mean_ref, shift_ref, x_ref, out_ref):
     _, at_first, at_last = flags(label_ref)
     totals = whole_images(at_first, at_last, image_ref, first_ref, last_ref)
     narrow = orthonormal(totals).astype(jnp.bfloat16)
-    for i, copy in enumerate(copies):
-        u = i * PART // UNIT
+    for start in range(0, x_ref.shape[0], PART):
+        u = start // UNIT
         chosen = narrow[u * DIRS : (u + 1) * DIRS]
         mean = mean_ref[u] - shift_ref[u]
         offset = jnp.sum(chosen.astype(jnp.float32) * mean, axis=1, keepdims=True)
-        copy.wait()
-        rows = slice(i * PART, (i + 1) * PART)
+        rows = slice(start, start + PART)
         out_ref[:, rows] = dot(chosen, x_ref[rows], ((1,), (1,))) - offset
 
 
@@ -400,11 +409,10 @@
     rows, width = x.shape
     return pl.pallas_call(
         project_kernel,
-        in_specs=smem(1) + vmem(5) + [pl.BlockSpec(memory_space=pl.ANY)],
+        in_specs=smem(1) + vmem(6),
         out_specs=vmem(1)[0],
         out_shape=jax.ShapeDtypeStruct((DIRS, rows), jnp.float32),
-        scratch_shapes=[pltpu.VMEM(x.shape, x.dtype), pltpu.SemaphoreType.DMA((rows // PART,))],
-        compiler_params=pltpu.CompilerParams(vmem_limit_bytes=24 * MIB),
+        compiler_params=pltpu.CompilerParams(vmem_limit_bytes=8 * MIB),
         cost_estimate=pl.CostEstimate(
             flops=2 * rows * width * 256, bytes_accessed=2 * rows * width, transcendentals=0
         ),
@@ -462,7 +470,7 @@
 
     embeddings = pltpu.with_memory_space_constraint(embeddings, pltpu.HBM)
     place = me.reshape(1)
-    spread, raw, means, own = unit_spread(place, labels, embeddings, start_basis)
+    spread, raw, means, own, rows_here = unit_spread(place, labels, embeddings, start_basis)
 
     mate = lax.ppermute(own, "dp", mates)
     near, far, masks = join_chip(place, own, mate, start_basis)
@@ -474,6 +482,7 @@
     )
     joins = masks[0:1], masks[1:2]
     even, *ups = (masks[i : i + 1] > 0.5 for i in range(8, 11))
+    bits = {1 << b: masks[10 + b : 11 + b] > 0.5 for b in range(1, 6)}
     masks = tuple(masks[i : i + 1] for i in range(2, 6))
     sides = [(origins[i : i + 1], origins[i + 1 : i + 2]) for i in (0, 2)]
 
@@ -492,7 +501,7 @@
 
     def halve(tiles, bit):
         low, high = tiles[0::2], tiles[1::2]
-        set_here = (me & bit) != 0
+        set_here = bits[bit]
         return jnp.where(set_here, high, low), jnp.where(set_here, low, high)
 
     def route(sent, bit):
@@ -519,7 +528,7 @@
         bit *= 2
     kept, sent = halve(kept, bit)
     got = route(sent, bit)
-    projections = project(labels, images, first, last_image, means, shift, embeddings)
+    projections = project(labels, images, first, last_image, means, shift, rows_here)
     return finish(kept, got), projections
 
 

time: 110 us -> 109 us (level)
  starting transfers between devices: 28.1 us -> 25.6 us
  waiting for transfers between devices: 34 us -> 35.9 us
  Pallas kernels: 45 us -> 43.8 us
    pallas_call x1, Pallas kernels: 8.19 us -> 6.03 us  [project(): pl.pallas_call(project_kernel, in_specs=smem(1) + vmem(6), out_specs=vmem...]
    ppermute x3, starting transfers between devices: 2.17 us -> 0.36 us  [route(): return lax.ppermute(sent, 'dp', [(i, i ^ bit) for i in range(n_dp)])]
    ppermute x3, waiting for transfers between devices: 2.13 us -> 3.52 us  [route(): return lax.ppermute(sent, 'dp', [(i, i ^ bit) for i in range(n_dp)])]
  transfers between devices with their start and end apart: 27 -> 27, of which waited for: 23 -> 22; matrix products, arithmetic and copies ran while one was open for 0% -> 0% of each run, Pallas kernels for 7% -> 6%
where the time goes in v7:
time: 109 us; the launch traced here: 108 us
  Pallas kernels  43.8 us (40%)
  waiting for transfers between devices  35.9 us (33%)
  starting transfers between devices  25.6 us (23%)
  local copies, waits for them, and re-layouts  1.64 us (2%)
    pallas_call x1, Pallas kernels, unit_spread(): pl.pallas_call(spread_kernel, grid=(units,), in_specs=[*smem(2), pl.Block...  19.9 us
    ppermute x10, waiting for transfers between devices, exchange(): lax.ppermute(jnp.where(up, totals[1], totals[0]), 'dp', link)  19.3 us
    ppermute x9, starting transfers between devices, swap(): return halves(lax.ppermute(both, 'dp', mates))  12.9 us
    pallas_call x3, Pallas kernels, step(): pl.pallas_call(step_kernel, in_specs=smem(1) + vmem(5), out_specs=vmem(2)...  9.9 us
    ppermute x9, waiting for transfers between devices, swap(): return halves(lax.ppermute(both, 'dp', mates))  7.13 us
    pallas_call x1, Pallas kernels, project(): pl.pallas_call(project_kernel, in_specs=smem(1) + vmem(6), out_specs=vmem...  6.03 us
    ppermute x2, starting transfers between devices, per_device(): lax.ppermute(part, 'dp', link)  4.52 us
    ppermute x1, starting transfers between devices, per_device(): other = lax.ppermute(side, 'dp', mates)  3.62 us
  transfers between devices with their start and end apart: 27, of which 22 were waited for; matrix products, arithmetic and copies ran while one was open for 0% of the time, Pallas kernels for 6%

profile of v7, /device:TPU:0, one launch (start us, length us, event | category | flops | bytes accessed | tf_op | source)
XLA Modules:
  0.0 108.3 jit_solution(1747357562294554012)
XLA Ops:
  2.2 19.9 %unit_spread.1 = (bf16[2,4,1024,1024]{3,2,1,0:T(8,128)(2,1)S(1)}, f32[4,8,1024]{2,1,0:T(8,128)S(1)}, f32[4,1,1024]{2,1,0:T(1,128)S(1)}, f32[32,1024]{1,0:T(8,128)S(1)}, bf16[8192,1024]{1,0:T(8,128)(2,1)S(1)}) custom-call(s32[1]{0:T(128)} %bitcast._.me_ref, s32[4]{0:T(128)S(1)} %slice.170.label_ref, bf16[8192,1024]{1,0:T(8,128)(2,1)} %source.1, ...), custom_call_target="tpu_custom_call" | custom-call | tf_op jit(solution)/shard_map/unit_spread/pallas_call | solution.py:100
  22.6 1.0 collective-permute-done.mate_ref
  23.7 2.9 %collective-permute-start.1 = (f32[16,1024]{1,0:T(8,128)S(1)}, f32[16,1024]{1,0:T(8,128)S(1)}, u32[]{:S(2)}, u32[]{:S(2)}) collective-permute-start(f32[16,1024]{1,0:T(8,128)S(1)} %get-tuple-element.39), channel_id=1, source_target_pairs={{0,2},{1,15},{2,0},{3,5},{4,6},{5,3},{6,4},{7,9},{8,10},{9,7},{10,... | collective-permute-start | bytes 196616 | tf_op jit(solution)/shard_map/ppermute | solution.py:477
  26.7 1.6 %collective-permute-start.2 = (f32[16,1024]{1,0:T(8,128)S(1)}, f32[16,1024]{1,0:T(8,128)S(1)}, u32[]{:S(2)}, u32[]{:S(2)}) collective-permute-start(f32[16,1024]{1,0:T(8,128)S(1)} %get-tuple-element.40), channel_id=1, source_target_pairs={{0,4},{1,13},{2,6},{3,15},{4,0},{5,9},{6,2},{7,11},{8,12},{9,5},{1... | collective-permute-start | bytes 196616 | tf_op jit(solution)/shard_map/ppermute | solution.py:477
  28.2 0.9 collective-permute-done.1.near_ref
  29.2 1.7 %collective-permute-done.2.far_ref = f32[16,1024]{1,0:T(8,128)S(1)} collective-permute-done((f32[16,1024]{1,0:T(8,128)S(1)}, f32[16,1024]{1,0:T(8,128)S(1)}, u32[]{:S(2)}, u32[]{:S(2)}) %collective-permute-start.2) | collective-permute-done | bytes 65568 | tf_op jit(solution)/shard_map/ppermute | solution.py:477
  31.0 3.6 %collective-permute-start.3 = (f32[32,1024]{1,0:T(8,128)S(1)}, f32[32,1024]{1,0:T(8,128)S(1)}, u32[]{:S(2)}, u32[]{:S(2)}) collective-permute-start(f32[32,1024]{1,0:T(8,128)S(1)} %get-tuple-element.41.side_ref), channel_id=1, source_target_pairs={{0,1},{1,0},{2,3},{3,2},{4,5},{5,4},{6,7},{7,6},{8,9},{9,8},{10,11... | collective-permute-start | bytes 393224 | tf_op jit(solution)/shard_map/ppermute | solution.py:479
  34.7 1.0 collective-permute-done.3.other_ref
  35.6 3.5 %first_step.1 = (f32[4,8,1024]{2,1,0:T(8,128)S(1)}, f32[16,1024]{1,0:T(8,128)S(1)}, f32[4,1,1024]{2,1,0:T(1,128)S(1)}) custom-call(s32[4]{0:T(128)S(1)} %slice.170.label_ref, f32[4,8,1024]{2,1,0:T(8,128)S(1)} %get-tuple-element.37.image_ref, f32[4,1,1024]{2,1,0:T(1,128)S(1)} %get-tuple-element.38.mean_ref, f32[32,1024]{1,0:T(8,128)S(1)} %collective-permute-done.mate_ref, ...), custom_call_target="tpu_custom_call" | custom-call | tf_op jit(solution)/shard_map/first_step/pallas_call | solution.py:332
  40.7 3.8 %collective-permute-done.6 = f32[8,1024]{1,0:T(8,128)S(1)} collective-permute-done((f32[8,1024]{1,0:T(8,128)S(1)}, f32[8,1024]{1,0:T(8,128)S(1)}, u32[]{:S(2)}, u32[]{:S(2)}) %collective-permute-start.6) | collective-permute-done | bytes 32800 | tf_op jit(solution)/shard_map/ppermute | solution.py:493
  44.6 3.2 %collective-permute-start.7 = (f32[16,1024]{1,0:T(8,128)S(1)}, f32[16,1024]{1,0:T(8,128)S(1)}, u32[]{:S(2)}, u32[]{:S(2)}) collective-permute-start(f32[16,1024]{1,0:T(8,128)S(1)} %pad_maximum_fusion), channel_id=1, source_target_pairs={{0,1},{1,0},{2,3},{3,2},{4,5},{5,4},{6,7},{7,6},{8,9},{9,8},{10,11... | collective-permute-start | bytes 196616 | tf_op jit(solution)/shard_map/ppermute | solution.py:457
  47.8 0.9 collective-permute-done.7
  48.7 3.2 %step.3 = (f32[4,8,1024]{2,1,0:T(8,128)S(1)}, f32[16,1024]{1,0:T(8,128)S(1)}) custom-call(s32[4]{0:T(128)S(1)} %slice.170.label_ref, f32[4,8,1024]{2,1,0:T(8,128)S(1)} %get-tuple-element.43.image_ref, f32[8,1024]{1,0:T(8,128)S(1)} %get-tuple-element.93.first_ref, f32[8,1024]{1,0:T(8,128)S(1)} %get-tuple-element.92.last_ref, ...), custom_call_target="tpu_custom_call" | custom-call | tf_op jit(solution)/shard_map/step/pallas_call | solution.py:369
  52.4 0.9 collective-permute-done.8
  53.5 3.9 %collective-permute-done.10 = f32[8,1024]{1,0:T(8,128)S(1)} collective-permute-done((f32[8,1024]{1,0:T(8,128)S(1)}, f32[8,1024]{1,0:T(8,128)S(1)}, u32[]{:S(2)}, u32[]{:S(2)}) %collective-permute-start.10) | collective-permute-done | bytes 32800 | tf_op jit(solution)/shard_map/ppermute | solution.py:493
  57.4 2.0 %collective-permute-start.11 = (f32[16,1024]{1,0:T(8,128)S(1)}, f32[16,1024]{1,0:T(8,128)S(1)}, u32[]{:S(2)}, u32[]{:S(2)}) collective-permute-start(f32[16,1024]{1,0:T(8,128)S(1)} %pad_maximum_fusion.1), channel_id=1, source_target_pairs={{0,1},{1,0},{2,3},{3,2},{4,5},{5,4},{6,7},{7,6},{8,9},{9,8},{10,11... | collective-permute-start | bytes 196616 | tf_op jit(solution)/shard_map/ppermute | solution.py:457
  60.3 3.2 %step.4 = (f32[4,8,1024]{2,1,0:T(8,128)S(1)}, f32[16,1024]{1,0:T(8,128)S(1)}) custom-call(s32[4]{0:T(128)S(1)} %slice.170.label_ref, f32[4,8,1024]{2,1,0:T(8,128)S(1)} %get-tuple-element.49.image_ref, f32[8,1024]{1,0:T(8,128)S(1)} %get-tuple-element.91.first_ref, f32[8,1024]{1,0:T(8,128)S(1)} %get-tuple-element.90.last_ref, ...), custom_call_target="tpu_custom_call" | custom-call | tf_op jit(solution)/shard_map/step/pallas_call | solution.py:369
  65.3 3.6 %collective-permute-done.14 = f32[8,1024]{1,0:T(8,128)S(1)} collective-permute-done((f32[8,1024]{1,0:T(8,128)S(1)}, f32[8,1024]{1,0:T(8,128)S(1)}, u32[]{:S(2)}, u32[]{:S(2)}) %collective-permute-start.14) | collective-permute-done | bytes 32800 | tf_op jit(solution)/shard_map/ppermute | solution.py:493
  69.3 3.0 %collective-permute-start.15 = (f32[16,1024]{1,0:T(8,128)S(1)}, f32[16,1024]{1,0:T(8,128)S(1)}, u32[]{:S(2)}, u32[]{:S(2)}) collective-permute-start(f32[16,1024]{1,0:T(8,128)S(1)} %pad_maximum_fusion.2), channel_id=1, source_target_pairs={{0,1},{1,0},{2,3},{3,2},{4,5},{5,4},{6,7},{7,6},{8,9},{9,8},{10,11... | collective-permute-start | bytes 196616 | tf_op jit(solution)/shard_map/ppermute | solution.py:457
  73.2 3.4 %step.5 = (f32[4,8,1024]{2,1,0:T(8,128)S(1)}, f32[16,1024]{1,0:T(8,128)S(1)}) custom-call(s32[4]{0:T(128)S(1)} %slice.170.label_ref, f32[4,8,1024]{2,1,0:T(8,128)S(1)} %get-tuple-element.53.image_ref, f32[8,1024]{1,0:T(8,128)S(1)} %get-tuple-element.89.first_ref, f32[8,1024]{1,0:T(8,128)S(1)} %get-tuple-element.88.last_ref, ...), custom_call_target="tpu_custom_call" | custom-call | tf_op jit(solution)/shard_map/step/pallas_call | solution.py:369
  77.0 0.9 collective-permute-done.16
  78.1 4.0 %collective-permute-done.18 = f32[8,1024]{1,0:T(8,128)S(1)} collective-permute-done((f32[8,1024]{1,0:T(8,128)S(1)}, f32[8,1024]{1,0:T(8,128)S(1)}, u32[]{:S(2)}, u32[]{:S(2)}) %collective-permute-start.18) | collective-permute-done | bytes 32800 | tf_op jit(solution)/shard_map/ppermute | solution.py:493
  82.1 1.9 %collective-permute-start.19 = (f32[16,1024]{1,0:T(8,128)S(1)}, f32[16,1024]{1,0:T(8,128)S(1)}, u32[]{:S(2)}, u32[]{:S(2)}) collective-permute-start(f32[16,1024]{1,0:T(8,128)S(1)} %pad_maximum_fusion.3), channel_id=1, source_target_pairs={{0,1},{1,0},{2,3},{3,2},{4,5},{5,4},{6,7},{7,6},{8,9},{9,8},{10,11... | collective-permute-start | bytes 196616 | tf_op jit(solution)/shard_map/ppermute | solution.py:457
  85.0 3.3 %step_and_route.1 = (f32[4,8,1024]{2,1,0:T(8,128)S(1)}, f32[80,1024]{1,0:T(8,128)S(1)}, f32[64,1024]{1,0:T(8,128)S(1)}) custom-call(s32[16]{0:T(128)S(1)} %copy-done.1, s32[1]{0:T(128)} %bitcast._.me_ref, s32[4]{0:T(128)S(1)} %slice.170.label_ref, f32[4,8,1024]{2,1,0:T(8,128)S(1)} %get-tuple-element.57.refs_0_, f32[8,1024]{1,0:T(8,128)S(1)} %get-tuple-element.87.refs_1_, ...), custom_call_target="tpu_custom_call" | custom-call | tf_op jit(solution)/shard_map/step_and_route/pallas_call | solution.py:385
  88.8 1.3 %collective-permute-done.20 = f32[80,1024]{1,0:T(8,128)S(1)} collective-permute-done((f32[80,1024]{1,0:T(8,128)S(1)}, f32[80,1024]{1,0:T(8,128)S(1)}, u32[]{:S(2)}, u32[]{:S(2)}) %collective-permute-start.20) | collective-permute-done | bytes 327712 | tf_op jit(solution)/shard_map/ppermute | solution.py:520
  90.6 2.0 %collective-permute-start.21 = (f32[8,1024]{1,0:T(8,128)S(1)}, f32[8,1024]{1,0:T(8,128)S(1)}, u32[]{:S(2)}, u32[]{:S(2)}) collective-permute-start(f32[8,1024]{1,0:T(8,128)S(1)} %get-tuple-element.75), channel_id=1, source_target_pairs={{0,2},{1,15},{2,0},{3,5},{4,6},{5,3},{6,4},{7,9},{8,10},{9,7},{10,... | collective-permute-start | bytes 98312 | tf_op jit(solution)/shard_map/ppermute | solution.py:493
  92.6 1.6 %collective-permute-done.22 = f32[8,1024]{1,0:T(8,128)S(1)} collective-permute-done((f32[8,1024]{1,0:T(8,128)S(1)}, f32[8,1024]{1,0:T(8,128)S(1)}, u32[]{:S(2)}, u32[]{:S(2)}) %collective-permute-start.22) | collective-permute-done | bytes 32800 | tf_op jit(solution)/shard_map/ppermute | solution.py:493
  94.2 2.1 %collective-permute-done.21 = f32[8,1024]{1,0:T(8,128)S(1)} collective-permute-done((f32[8,1024]{1,0:T(8,128)S(1)}, f32[8,1024]{1,0:T(8,128)S(1)}, u32[]{:S(2)}, u32[]{:S(2)}) %collective-permute-start.21) | collective-permute-done | bytes 32800 | tf_op jit(solution)/shard_map/ppermute | solution.py:493
  96.6 1.1 collective-permute-start.26
  97.7 3.5 %collective-permute-done.24 = f32[2,8,1024]{2,1,0:T(8,128)S(1)} collective-permute-done((f32[2,8,1024]{2,1,0:T(8,128)S(1)}, f32[2,8,1024]{2,1,0:T(8,128)S(1)}, u32[]{:S(2)}, u32[]{:S(2)}) %collective-permute-start.24) | collective-permute-done | bytes 65568 | tf_op jit(solution)/shard_map/ppermute | solution.py:508
  101.3 6.0 %project.1 = f32[8,8192]{1,0:T(8,128)} custom-call(s32[4]{0:T(128)S(1)} %slice.170.label_ref, f32[4,8,1024]{2,1,0:T(8,128)S(1)} %get-tuple-element.64.image_ref, f32[8,1024]{1,0:T(8,128)S(1)} %get-tuple-element.77.first_ref, f32[8,1024]{1,0:T(8,128)S(1)} %get-tuple-element.76.last_ref, f32[4,1,1024]{2,1,0:T(1,128)S(1)} %get-tuple-element.38.mean_ref, ...), custom_call_target="tpu_custom_call" | custom-call | flops 4294967296 | bytes 16777216 | tf_op jit(solution)/shard_map/project/pallas_call | solution.py:410
  107.4 1.0 finish.1
  (66 shorter events, 11.5 us)
Async XLA Ops:
  1.5 0.8 copy-start
  22.1 1.5 %collective-permute-start = (f32[32,1024]{1,0:T(8,128)S(1)}, f32[32,1024]{1,0:T(8,128)S(1)}, u32[]{:S(2)}, u32[]{:S(2)}) collective-permute-start(f32[32,1024]{1,0:T(8,128)S(1)} %get-tuple-element.35.own_ref), channel_id=1, source_target_pairs={{0,1},{1,0},{2,3},{3,2},{4,5},{5,4},{6,7},{7,6},{8,9},{9,8},{10,11... | collective-permute-start | bytes 393224 | tf_op jit(solution)/shard_map/ppermute | solution.py:475
  23.7 5.5 %collective-permute-start.1 = (f32[16,1024]{1,0:T(8,128)S(1)}, f32[16,1024]{1,0:T(8,128)S(1)}, u32[]{:S(2)}, u32[]{:S(2)}) collective-permute-start(f32[16,1024]{1,0:T(8,128)S(1)} %get-tuple-element.39), channel_id=1, source_target_pairs={{0,2},{1,15},{2,0},{3,5},{4,6},{5,3},{6,4},{7,9},{8,10},{9,7},{10,... | collective-permute-start | bytes 196616 | tf_op jit(solution)/shard_map/ppermute | solution.py:477
  26.7 4.3 %collective-permute-start.2 = (f32[16,1024]{1,0:T(8,128)S(1)}, f32[16,1024]{1,0:T(8,128)S(1)}, u32[]{:S(2)}, u32[]{:S(2)}) collective-permute-start(f32[16,1024]{1,0:T(8,128)S(1)} %get-tuple-element.40), channel_id=1, source_target_pairs={{0,4},{1,13},{2,6},{3,15},{4,0},{5,9},{6,2},{7,11},{8,12},{9,5},{1... | collective-permute-start | bytes 196616 | tf_op jit(solution)/shard_map/ppermute | solution.py:477
  31.0 4.6 %collective-permute-start.3 = (f32[32,1024]{1,0:T(8,128)S(1)}, f32[32,1024]{1,0:T(8,128)S(1)}, u32[]{:S(2)}, u32[]{:S(2)}) collective-permute-start(f32[32,1024]{1,0:T(8,128)S(1)} %get-tuple-element.41.side_ref), channel_id=1, source_target_pairs={{0,1},{1,0},{2,3},{3,2},{4,5},{5,4},{6,7},{7,6},{8,9},{9,8},{10,11... | collective-permute-start | bytes 393224 | tf_op jit(solution)/shard_map/ppermute | solution.py:479
  39.1 1.3 %collective-permute-start.4 = (f32[16,1024]{1,0:T(8,128)S(1)}, f32[16,1024]{1,0:T(8,128)S(1)}, u32[]{:S(2)}, u32[]{:S(2)}) collective-permute-start(f32[16,1024]{1,0:T(8,128)S(1)} %get-tuple-element.45), channel_id=1, source_target_pairs={{0,1},{1,0},{2,3},{3,2},{4,5},{5,4},{6,7},{7,6},{8,9},{9,8},{10,11... | collective-permute-start | bytes 196616 | tf_op jit(solution)/shard_map/ppermute | solution.py:457
  40.5 4.0 %collective-permute-start.6 = (f32[8,1024]{1,0:T(8,128)S(1)}, f32[8,1024]{1,0:T(8,128)S(1)}, u32[]{:S(2)}, u32[]{:S(2)}) collective-permute-start(f32[8,1024]{1,0:T(8,128)S(1)} %get-tuple-element.84), channel_id=1, source_target_pairs={{0,4},{1,13},{2,6},{3,15},{4,0},{5,9},{6,2},{7,11},{8,12},{9,5},{1... | collective-permute-start | bytes 98312 | tf_op jit(solution)/shard_map/ppermute | solution.py:493
  40.6 4.0 %collective-permute-start.5 = (f32[8,1024]{1,0:T(8,128)S(1)}, f32[8,1024]{1,0:T(8,128)S(1)}, u32[]{:S(2)}, u32[]{:S(2)}) collective-permute-start(f32[8,1024]{1,0:T(8,128)S(1)} %get-tuple-element.85), channel_id=1, source_target_pairs={{0,2},{1,15},{2,0},{3,5},{4,6},{5,3},{6,4},{7,9},{8,10},{9,7},{10,... | collective-permute-start | bytes 98312 | tf_op jit(solution)/shard_map/ppermute | solution.py:493
  44.6 4.1 %collective-permute-start.7 = (f32[16,1024]{1,0:T(8,128)S(1)}, f32[16,1024]{1,0:T(8,128)S(1)}, u32[]{:S(2)}, u32[]{:S(2)}) collective-permute-start(f32[16,1024]{1,0:T(8,128)S(1)} %pad_maximum_fusion), channel_id=1, source_target_pairs={{0,1},{1,0},{2,3},{3,2},{4,5},{5,4},{6,7},{7,6},{8,9},{9,8},{10,11... | collective-permute-start | bytes 196616 | tf_op jit(solution)/shard_map/ppermute | solution.py:457
  51.9 1.3 %collective-permute-start.8 = (f32[16,1024]{1,0:T(8,128)S(1)}, f32[16,1024]{1,0:T(8,128)S(1)}, u32[]{:S(2)}, u32[]{:S(2)}) collective-permute-start(f32[16,1024]{1,0:T(8,128)S(1)} %get-tuple-element.50), channel_id=1, source_target_pairs={{0,1},{1,0},{2,3},{3,2},{4,5},{5,4},{6,7},{7,6},{8,9},{9,8},{10,11... | collective-permute-start | bytes 196616 | tf_op jit(solution)/shard_map/ppermute | solution.py:457
  53.3 4.1 %collective-permute-start.10 = (f32[8,1024]{1,0:T(8,128)S(1)}, f32[8,1024]{1,0:T(8,128)S(1)}, u32[]{:S(2)}, u32[]{:S(2)}) collective-permute-start(f32[8,1024]{1,0:T(8,128)S(1)} %get-tuple-element.82), channel_id=1, source_target_pairs={{0,4},{1,13},{2,6},{3,15},{4,0},{5,9},{6,2},{7,11},{8,12},{9,5},{1... | collective-permute-start | bytes 98312 | tf_op jit(solution)/shard_map/ppermute | solution.py:493
  53.4 4.0 %collective-permute-start.9 = (f32[8,1024]{1,0:T(8,128)S(1)}, f32[8,1024]{1,0:T(8,128)S(1)}, u32[]{:S(2)}, u32[]{:S(2)}) collective-permute-start(f32[8,1024]{1,0:T(8,128)S(1)} %get-tuple-element.83), channel_id=1, source_target_pairs={{0,2},{1,15},{2,0},{3,5},{4,6},{5,3},{6,4},{7,9},{8,10},{9,7},{10,... | collective-permute-start | bytes 98312 | tf_op jit(solution)/shard_map/ppermute | solution.py:493
  57.4 2.9 %collective-permute-start.11 = (f32[16,1024]{1,0:T(8,128)S(1)}, f32[16,1024]{1,0:T(8,128)S(1)}, u32[]{:S(2)}, u32[]{:S(2)}) collective-permute-start(f32[16,1024]{1,0:T(8,128)S(1)} %pad_maximum_fusion.1), channel_id=1, source_target_pairs={{0,1},{1,0},{2,3},{3,2},{4,5},{5,4},{6,7},{7,6},{8,9},{9,8},{10,11... | collective-permute-start | bytes 196616 | tf_op jit(solution)/shard_map/ppermute | solution.py:457
  60.3 24.7 %copy-start.1 = (s32[16]{0:T(128)S(1)}, s32[16]{0:T(128)}, u32[]{:S(2)}) copy-start(s32[16]{0:T(128)} %owner_ref.1) | copy-start | bytes 196
  63.6 1.3 %collective-permute-start.12 = (f32[16,1024]{1,0:T(8,128)S(1)}, f32[16,1024]{1,0:T(8,128)S(1)}, u32[]{:S(2)}, u32[]{:S(2)}) collective-permute-start(f32[16,1024]{1,0:T(8,128)S(1)} %get-tuple-element.54), channel_id=1, source_target_pairs={{0,1},{1,0},{2,3},{3,2},{4,5},{5,4},{6,7},{7,6},{8,9},{9,8},{10,11... | collective-permute-start | bytes 196616 | tf_op jit(solution)/shard_map/ppermute | solution.py:457
  64.9 4.0 %collective-permute-start.14 = (f32[8,1024]{1,0:T(8,128)S(1)}, f32[8,1024]{1,0:T(8,128)S(1)}, u32[]{:S(2)}, u32[]{:S(2)}) collective-permute-start(f32[8,1024]{1,0:T(8,128)S(1)} %get-tuple-element.80), channel_id=1, source_target_pairs={{0,4},{1,13},{2,6},{3,15},{4,0},{5,9},{6,2},{7,11},{8,12},{9,5},{1... | collective-permute-start | bytes 98312 | tf_op jit(solution)/shard_map/ppermute | solution.py:493
  65.3 3.9 %collective-permute-start.13 = (f32[8,1024]{1,0:T(8,128)S(1)}, f32[8,1024]{1,0:T(8,128)S(1)}, u32[]{:S(2)}, u32[]{:S(2)}) collective-permute-start(f32[8,1024]{1,0:T(8,128)S(1)} %get-tuple-element.81), channel_id=1, source_target_pairs={{0,2},{1,15},{2,0},{3,5},{4,6},{5,3},{6,4},{7,9},{8,10},{9,7},{10,... | collective-permute-start | bytes 98312 | tf_op jit(solution)/shard_map/ppermute | solution.py:493
  69.3 3.9 %collective-permute-start.15 = (f32[16,1024]{1,0:T(8,128)S(1)}, f32[16,1024]{1,0:T(8,128)S(1)}, u32[]{:S(2)}, u32[]{:S(2)}) collective-permute-start(f32[16,1024]{1,0:T(8,128)S(1)} %pad_maximum_fusion.2), channel_id=1, source_target_pairs={{0,1},{1,0},{2,3},{3,2},{4,5},{5,4},{6,7},{7,6},{8,9},{9,8},{10,11... | collective-permute-start | bytes 196616 | tf_op jit(solution)/shard_map/ppermute | solution.py:457
  76.6 1.3 %collective-permute-start.16 = (f32[16,1024]{1,0:T(8,128)S(1)}, f32[16,1024]{1,0:T(8,128)S(1)}, u32[]{:S(2)}, u32[]{:S(2)}) collective-permute-start(f32[16,1024]{1,0:T(8,128)S(1)} %get-tuple-element.58), channel_id=1, source_target_pairs={{0,1},{1,0},{2,3},{3,2},{4,5},{5,4},{6,7},{7,6},{8,9},{9,8},{10,11... | collective-permute-start | bytes 196616 | tf_op jit(solution)/shard_map/ppermute | solution.py:457
  78.0 4.1 %collective-permute-start.18 = (f32[8,1024]{1,0:T(8,128)S(1)}, f32[8,1024]{1,0:T(8,128)S(1)}, u32[]{:S(2)}, u32[]{:S(2)}) collective-permute-start(f32[8,1024]{1,0:T(8,128)S(1)} %get-tuple-element.78), channel_id=1, source_target_pairs={{0,4},{1,13},{2,6},{3,15},{4,0},{5,9},{6,2},{7,11},{8,12},{9,5},{1... | collective-permute-start | bytes 98312 | tf_op jit(solution)/shard_map/ppermute | solution.py:493
  78.0 4.1 %collective-permute-start.17 = (f32[8,1024]{1,0:T(8,128)S(1)}, f32[8,1024]{1,0:T(8,128)S(1)}, u32[]{:S(2)}, u32[]{:S(2)}) collective-permute-start(f32[8,1024]{1,0:T(8,128)S(1)} %get-tuple-element.79), channel_id=1, source_target_pairs={{0,2},{1,15},{2,0},{3,5},{4,6},{5,3},{6,4},{7,9},{8,10},{9,7},{10,... | collective-permute-start | bytes 98312 | tf_op jit(solution)/shard_map/ppermute | solution.py:493
  82.1 2.8 %collective-permute-start.19 = (f32[16,1024]{1,0:T(8,128)S(1)}, f32[16,1024]{1,0:T(8,128)S(1)}, u32[]{:S(2)}, u32[]{:S(2)}) collective-permute-start(f32[16,1024]{1,0:T(8,128)S(1)} %pad_maximum_fusion.3), channel_id=1, source_target_pairs={{0,1},{1,0},{2,3},{3,2},{4,5},{5,4},{6,7},{7,6},{8,9},{9,8},{10,11... | collective-permute-start | bytes 196616 | tf_op jit(solution)/shard_map/ppermute | solution.py:457
  88.3 1.7 %collective-permute-start.20 = (f32[80,1024]{1,0:T(8,128)S(1)}, f32[80,1024]{1,0:T(8,128)S(1)}, u32[]{:S(2)}, u32[]{:S(2)}) collective-permute-start(f32[80,1024]{1,0:T(8,128)S(1)} %get-tuple-element.62), channel_id=1, source_target_pairs={{0,1},{1,0},{2,3},{3,2},{4,5},{5,4},{6,7},{7,6},{8,9},{9,8},{10,11... | collective-permute-start | bytes 983048 | tf_op jit(solution)/shard_map/ppermute | solution.py:520
  90.1 6.2 %collective-permute-start.23 = (f32[4,8,1024]{2,1,0:T(8,128)S(1)}, f32[4,8,1024]{2,1,0:T(8,128)S(1)}, u32[]{:S(2)}, u32[]{:S(2)}) collective-permute-start(f32[4,8,1024]{2,1,0:T(8,128)S(1)} %slice_select_fusion), channel_id=1, source_target_pairs={{0,2},{1,3},{2,0},{3,1},{4,6},{5,7},{6,4},{7,5},{8,10},{9,11},{10,... | collective-permute-start | bytes 393224 | tf_op jit(solution)/shard_map/ppermute | solution.py:508
  90.2 4.0 %collective-permute-start.22 = (f32[8,1024]{1,0:T(8,128)S(1)}, f32[8,1024]{1,0:T(8,128)S(1)}, u32[]{:S(2)}, u32[]{:S(2)}) collective-permute-start(f32[8,1024]{1,0:T(8,128)S(1)} %get-tuple-element.74), channel_id=1, source_target_pairs={{0,4},{1,13},{2,6},{3,15},{4,0},{5,9},{6,2},{7,11},{8,12},{9,5},{1... | collective-permute-start | bytes 98312 | tf_op jit(solution)/shard_map/ppermute | solution.py:493
  90.6 5.7 %collective-permute-start.21 = (f32[8,1024]{1,0:T(8,128)S(1)}, f32[8,1024]{1,0:T(8,128)S(1)}, u32[]{:S(2)}, u32[]{:S(2)}) collective-permute-start(f32[8,1024]{1,0:T(8,128)S(1)} %get-tuple-element.75), channel_id=1, source_target_pairs={{0,2},{1,15},{2,0},{3,5},{4,6},{5,3},{6,4},{7,9},{8,10},{9,7},{10,... | collective-permute-start | bytes 98312 | tf_op jit(solution)/shard_map/ppermute | solution.py:493
  96.3 4.8 %collective-permute-start.24 = (f32[2,8,1024]{2,1,0:T(8,128)S(1)}, f32[2,8,1024]{2,1,0:T(8,128)S(1)}, u32[]{:S(2)}, u32[]{:S(2)}) collective-permute-start(f32[2,8,1024]{2,1,0:T(8,128)S(1)} %slice_select_fusion.1), channel_id=1, source_target_pairs={{0,4},{1,5},{2,6},{3,7},{4,0},{5,1},{6,2},{7,3},{8,12},{9,13},{10,... | collective-permute-start | bytes 196616 | tf_op jit(solution)/shard_map/ppermute | solution.py:508
  96.6 4.7 %collective-permute-start.26 = (f32[16,1024]{1,0:T(8,128)S(1)}, f32[16,1024]{1,0:T(8,128)S(1)}, u32[]{:S(2)}, u32[]{:S(2)}) collective-permute-start(f32[16,1024]{1,0:T(8,128)S(1)} %pad_maximum_fusion.4), channel_id=1, source_target_pairs={{0,1},{1,0},{2,3},{3,2},{4,5},{5,4},{6,7},{7,6},{8,9},{9,8},{10,11... | collective-permute-start | bytes 196616 | tf_op jit(solution)/shard_map/ppermute | solution.py:457
  101.2 6.2 %collective-permute-start.25 = (f32[1,8,1024]{2,1,0:T(8,128)S(1)}, f32[1,8,1024]{2,1,0:T(8,128)S(1)}, u32[]{:S(2)}, u32[]{:S(2)}) collective-permute-start(f32[1,8,1024]{2,1,0:T(8,128)S(1)} %get-tuple-element.94), channel_id=1, source_target_pairs={{0,8},{1,9},{2,10},{3,11},{4,12},{5,13},{6,14},{7,15},{8,0},{9,1},... | collective-permute-start | bytes 98312 | tf_op jit(solution)/shard_map/ppermute | solution.py:508

commit v8 on v7

--- a/solution.py
+++ b/solution.py
@@ -470,7 +470,9 @@
 
     embeddings = pltpu.with_memory_space_constraint(embeddings, pltpu.HBM)
     place = me.reshape(1)
-    spread, raw, means, own, rows_here = unit_spread(place, labels, embeddings, start_basis)
+    spread, raw, means, own, rows_here = unit_spread(
+        place, labels, embeddings, pltpu.with_memory_space_constraint(start_basis, pltpu.HBM)
+    )
 
     mate = lax.ppermute(own, "dp", mates)
     near, far, masks = join_chip(place, own, mate, start_basis)

time: 109 us -> 108 us (level)
  no operation moved by 1% of the time
where the time goes in v8:
time: 108 us
  Pallas kernels  44 us (41%)
  waiting for transfers between devices  35.9 us (33%)
  starting transfers between devices  25.6 us (24%)
    pallas_call x1, Pallas kernels, unit_spread(): pl.pallas_call(spread_kernel, grid=(units,), in_specs=[*smem(2), pl.Block...  20.1 us
    ppermute x10, waiting for transfers between devices, exchange(): lax.ppermute(jnp.where(up, totals[1], totals[0]), 'dp', link)  19.3 us
    ppermute x9, starting transfers between devices, swap(): return halves(lax.ppermute(both, 'dp', mates))  12.9 us
    pallas_call x3, Pallas kernels, step(): pl.pallas_call(step_kernel, in_specs=smem(1) + vmem(5), out_specs=vmem(2)...  9.9 us
    ppermute x9, waiting for transfers between devices, swap(): return halves(lax.ppermute(both, 'dp', mates))  7.13 us
    pallas_call x1, Pallas kernels, project(): pl.pallas_call(project_kernel, in_specs=smem(1) + vmem(6), out_specs=vmem...  6.04 us
    ppermute x2, starting transfers between devices, per_device(): lax.ppermute(part, 'dp', link)  4.51 us
    ppermute x1, starting transfers between devices, per_device(): other = lax.ppermute(side, 'dp', mates)  3.62 us
  transfers between devices with their start and end apart: 27, of which 22 were waited for; matrix products, arithmetic and copies ran while one was open for 0% of the time, Pallas kernels for 6%

profile of v8, /device:TPU:0, one launch (start us, length us, event | category | flops | bytes accessed | tf_op | source)
XLA Modules:
  0.0 107.8 jit_solution(4528868760565538625)
XLA Ops:
  1.5 20.1 %unit_spread.1 = (bf16[2,4,1024,1024]{3,2,1,0:T(8,128)(2,1)S(1)}, f32[4,8,1024]{2,1,0:T(8,128)S(1)}, f32[4,1,1024]{2,1,0:T(1,128)S(1)}, f32[32,1024]{1,0:T(8,128)S(1)}, bf16[8192,1024]{1,0:T(8,128)(2,1)S(1)}) custom-call(s32[1]{0:T(128)} %bitcast._.me_ref, s32[4]{0:T(128)S(1)} %slice.170.label_ref, bf16[8192,1024]{1,0:T(8,128)(2,1)} %source.1, ...), custom_call_target="tpu_custom_call" | custom-call | tf_op jit(solution)/shard_map/unit_spread/pallas_call | solution.py:100
  22.1 1.0 collective-permute-done.mate_ref
  23.2 2.9 %collective-permute-start.1 = (f32[16,1024]{1,0:T(8,128)S(1)}, f32[16,1024]{1,0:T(8,128)S(1)}, u32[]{:S(2)}, u32[]{:S(2)}) collective-permute-start(f32[16,1024]{1,0:T(8,128)S(1)} %get-tuple-element.39), channel_id=1, source_target_pairs={{0,2},{1,15},{2,0},{3,5},{4,6},{5,3},{6,4},{7,9},{8,10},{9,7},{10,... | collective-permute-start | bytes 196616 | tf_op jit(solution)/shard_map/ppermute | solution.py:479
  26.1 1.6 %collective-permute-start.2 = (f32[16,1024]{1,0:T(8,128)S(1)}, f32[16,1024]{1,0:T(8,128)S(1)}, u32[]{:S(2)}, u32[]{:S(2)}) collective-permute-start(f32[16,1024]{1,0:T(8,128)S(1)} %get-tuple-element.40), channel_id=1, source_target_pairs={{0,4},{1,13},{2,6},{3,15},{4,0},{5,9},{6,2},{7,11},{8,12},{9,5},{1... | collective-permute-start | bytes 196616 | tf_op jit(solution)/shard_map/ppermute | solution.py:479
  27.7 0.9 collective-permute-done.1.near_ref
  28.7 1.7 %collective-permute-done.2.far_ref = f32[16,1024]{1,0:T(8,128)S(1)} collective-permute-done((f32[16,1024]{1,0:T(8,128)S(1)}, f32[16,1024]{1,0:T(8,128)S(1)}, u32[]{:S(2)}, u32[]{:S(2)}) %collective-permute-start.2) | collective-permute-done | bytes 65568 | tf_op jit(solution)/shard_map/ppermute | solution.py:479
  30.5 3.6 %collective-permute-start.3 = (f32[32,1024]{1,0:T(8,128)S(1)}, f32[32,1024]{1,0:T(8,128)S(1)}, u32[]{:S(2)}, u32[]{:S(2)}) collective-permute-start(f32[32,1024]{1,0:T(8,128)S(1)} %get-tuple-element.41.side_ref), channel_id=1, source_target_pairs={{0,1},{1,0},{2,3},{3,2},{4,5},{5,4},{6,7},{7,6},{8,9},{9,8},{10,11... | collective-permute-start | bytes 393224 | tf_op jit(solution)/shard_map/ppermute | solution.py:481
  34.2 1.0 collective-permute-done.3.other_ref
  35.1 3.5 %first_step.1 = (f32[4,8,1024]{2,1,0:T(8,128)S(1)}, f32[16,1024]{1,0:T(8,128)S(1)}, f32[4,1,1024]{2,1,0:T(1,128)S(1)}) custom-call(s32[4]{0:T(128)S(1)} %slice.170.label_ref, f32[4,8,1024]{2,1,0:T(8,128)S(1)} %get-tuple-element.37.image_ref, f32[4,1,1024]{2,1,0:T(1,128)S(1)} %get-tuple-element.38.mean_ref, f32[32,1024]{1,0:T(8,128)S(1)} %collective-permute-done.mate_ref, ...), custom_call_target="tpu_custom_call" | custom-call | tf_op jit(solution)/shard_map/first_step/pallas_call | solution.py:332
  40.1 3.8 %collective-permute-done.6 = f32[8,1024]{1,0:T(8,128)S(1)} collective-permute-done((f32[8,1024]{1,0:T(8,128)S(1)}, f32[8,1024]{1,0:T(8,128)S(1)}, u32[]{:S(2)}, u32[]{:S(2)}) %collective-permute-start.6) | collective-permute-done | bytes 32800 | tf_op jit(solution)/shard_map/ppermute | solution.py:495
  44.1 3.2 %collective-permute-start.7 = (f32[16,1024]{1,0:T(8,128)S(1)}, f32[16,1024]{1,0:T(8,128)S(1)}, u32[]{:S(2)}, u32[]{:S(2)}) collective-permute-start(f32[16,1024]{1,0:T(8,128)S(1)} %pad_maximum_fusion), channel_id=1, source_target_pairs={{0,1},{1,0},{2,3},{3,2},{4,5},{5,4},{6,7},{7,6},{8,9},{9,8},{10,11... | collective-permute-start | bytes 196616 | tf_op jit(solution)/shard_map/ppermute | solution.py:457
  48.2 3.2 %step.3 = (f32[4,8,1024]{2,1,0:T(8,128)S(1)}, f32[16,1024]{1,0:T(8,128)S(1)}) custom-call(s32[4]{0:T(128)S(1)} %slice.170.label_ref, f32[4,8,1024]{2,1,0:T(8,128)S(1)} %get-tuple-element.43.image_ref, f32[8,1024]{1,0:T(8,128)S(1)} %get-tuple-element.93.first_ref, f32[8,1024]{1,0:T(8,128)S(1)} %get-tuple-element.92.last_ref, ...), custom_call_target="tpu_custom_call" | custom-call | tf_op jit(solution)/shard_map/step/pallas_call | solution.py:369
  51.8 0.9 collective-permute-done.8
  52.9 3.9 %collective-permute-done.10 = f32[8,1024]{1,0:T(8,128)S(1)} collective-permute-done((f32[8,1024]{1,0:T(8,128)S(1)}, f32[8,1024]{1,0:T(8,128)S(1)}, u32[]{:S(2)}, u32[]{:S(2)}) %collective-permute-start.10) | collective-permute-done | bytes 32800 | tf_op jit(solution)/shard_map/ppermute | solution.py:495
  56.9 2.0 %collective-permute-start.11 = (f32[16,1024]{1,0:T(8,128)S(1)}, f32[16,1024]{1,0:T(8,128)S(1)}, u32[]{:S(2)}, u32[]{:S(2)}) collective-permute-start(f32[16,1024]{1,0:T(8,128)S(1)} %pad_maximum_fusion.1), channel_id=1, source_target_pairs={{0,1},{1,0},{2,3},{3,2},{4,5},{5,4},{6,7},{7,6},{8,9},{9,8},{10,11... | collective-permute-start | bytes 196616 | tf_op jit(solution)/shard_map/ppermute | solution.py:457
  58.9 0.9 collective-permute-done.11
  59.8 3.2 %step.4 = (f32[4,8,1024]{2,1,0:T(8,128)S(1)}, f32[16,1024]{1,0:T(8,128)S(1)}) custom-call(s32[4]{0:T(128)S(1)} %slice.170.label_ref, f32[4,8,1024]{2,1,0:T(8,128)S(1)} %get-tuple-element.49.image_ref, f32[8,1024]{1,0:T(8,128)S(1)} %get-tuple-element.91.first_ref, f32[8,1024]{1,0:T(8,128)S(1)} %get-tuple-element.90.last_ref, ...), custom_call_target="tpu_custom_call" | custom-call | tf_op jit(solution)/shard_map/step/pallas_call | solution.py:369
  63.5 0.9 collective-permute-done.12
  64.8 3.6 %collective-permute-done.14 = f32[8,1024]{1,0:T(8,128)S(1)} collective-permute-done((f32[8,1024]{1,0:T(8,128)S(1)}, f32[8,1024]{1,0:T(8,128)S(1)}, u32[]{:S(2)}, u32[]{:S(2)}) %collective-permute-start.14) | collective-permute-done | bytes 32800 | tf_op jit(solution)/shard_map/ppermute | solution.py:495
  68.8 3.0 %collective-permute-start.15 = (f32[16,1024]{1,0:T(8,128)S(1)}, f32[16,1024]{1,0:T(8,128)S(1)}, u32[]{:S(2)}, u32[]{:S(2)}) collective-permute-start(f32[16,1024]{1,0:T(8,128)S(1)} %pad_maximum_fusion.2), channel_id=1, source_target_pairs={{0,1},{1,0},{2,3},{3,2},{4,5},{5,4},{6,7},{7,6},{8,9},{9,8},{10,11... | collective-permute-start | bytes 196616 | tf_op jit(solution)/shard_map/ppermute | solution.py:457
  72.6 3.4 %step.5 = (f32[4,8,1024]{2,1,0:T(8,128)S(1)}, f32[16,1024]{1,0:T(8,128)S(1)}) custom-call(s32[4]{0:T(128)S(1)} %slice.170.label_ref, f32[4,8,1024]{2,1,0:T(8,128)S(1)} %get-tuple-element.53.image_ref, f32[8,1024]{1,0:T(8,128)S(1)} %get-tuple-element.89.first_ref, f32[8,1024]{1,0:T(8,128)S(1)} %get-tuple-element.88.last_ref, ...), custom_call_target="tpu_custom_call" | custom-call | tf_op jit(solution)/shard_map/step/pallas_call | solution.py:369
  77.6 4.0 %collective-permute-done.18 = f32[8,1024]{1,0:T(8,128)S(1)} collective-permute-done((f32[8,1024]{1,0:T(8,128)S(1)}, f32[8,1024]{1,0:T(8,128)S(1)}, u32[]{:S(2)}, u32[]{:S(2)}) %collective-permute-start.18) | collective-permute-done | bytes 32800 | tf_op jit(solution)/shard_map/ppermute | solution.py:495
  81.6 1.9 %collective-permute-start.19 = (f32[16,1024]{1,0:T(8,128)S(1)}, f32[16,1024]{1,0:T(8,128)S(1)}, u32[]{:S(2)}, u32[]{:S(2)}) collective-permute-start(f32[16,1024]{1,0:T(8,128)S(1)} %pad_maximum_fusion.3), channel_id=1, source_target_pairs={{0,1},{1,0},{2,3},{3,2},{4,5},{5,4},{6,7},{7,6},{8,9},{9,8},{10,11... | collective-permute-start | bytes 196616 | tf_op jit(solution)/shard_map/ppermute | solution.py:457
  84.5 3.3 %step_and_route.1 = (f32[4,8,1024]{2,1,0:T(8,128)S(1)}, f32[80,1024]{1,0:T(8,128)S(1)}, f32[64,1024]{1,0:T(8,128)S(1)}) custom-call(s32[16]{0:T(128)S(1)} %copy-done.1, s32[1]{0:T(128)} %bitcast._.me_ref, s32[4]{0:T(128)S(1)} %slice.170.label_ref, f32[4,8,1024]{2,1,0:T(8,128)S(1)} %get-tuple-element.57.refs_0_, f32[8,1024]{1,0:T(8,128)S(1)} %get-tuple-element.87.refs_1_, ...), custom_call_target="tpu_custom_call" | custom-call | tf_op jit(solution)/shard_map/step_and_route/pallas_call | solution.py:385
  88.2 1.3 %collective-permute-done.20 = f32[80,1024]{1,0:T(8,128)S(1)} collective-permute-done((f32[80,1024]{1,0:T(8,128)S(1)}, f32[80,1024]{1,0:T(8,128)S(1)}, u32[]{:S(2)}, u32[]{:S(2)}) %collective-permute-start.20) | collective-permute-done | bytes 327712 | tf_op jit(solution)/shard_map/ppermute | solution.py:522
  90.1 2.0 %collective-permute-start.21 = (f32[8,1024]{1,0:T(8,128)S(1)}, f32[8,1024]{1,0:T(8,128)S(1)}, u32[]{:S(2)}, u32[]{:S(2)}) collective-permute-start(f32[8,1024]{1,0:T(8,128)S(1)} %get-tuple-element.75), channel_id=1, source_target_pairs={{0,2},{1,15},{2,0},{3,5},{4,6},{5,3},{6,4},{7,9},{8,10},{9,7},{10,... | collective-permute-start | bytes 98312 | tf_op jit(solution)/shard_map/ppermute | solution.py:495
  92.1 1.6 %collective-permute-done.22 = f32[8,1024]{1,0:T(8,128)S(1)} collective-permute-done((f32[8,1024]{1,0:T(8,128)S(1)}, f32[8,1024]{1,0:T(8,128)S(1)}, u32[]{:S(2)}, u32[]{:S(2)}) %collective-permute-start.22) | collective-permute-done | bytes 32800 | tf_op jit(solution)/shard_map/ppermute | solution.py:495
  93.7 2.1 %collective-permute-done.21 = f32[8,1024]{1,0:T(8,128)S(1)} collective-permute-done((f32[8,1024]{1,0:T(8,128)S(1)}, f32[8,1024]{1,0:T(8,128)S(1)}, u32[]{:S(2)}, u32[]{:S(2)}) %collective-permute-start.21) | collective-permute-done | bytes 32800 | tf_op jit(solution)/shard_map/ppermute | solution.py:495
  96.0 1.1 %collective-permute-start.26 = (f32[16,1024]{1,0:T(8,128)S(1)}, f32[16,1024]{1,0:T(8,128)S(1)}, u32[]{:S(2)}, u32[]{:S(2)}) collective-permute-start(f32[16,1024]{1,0:T(8,128)S(1)} %pad_maximum_fusion.4), channel_id=1, source_target_pairs={{0,1},{1,0},{2,3},{3,2},{4,5},{5,4},{6,7},{7,6},{8,9},{9,8},{10,11... | collective-permute-start | bytes 196616 | tf_op jit(solution)/shard_map/ppermute | solution.py:457
  97.1 3.5 %collective-permute-done.24 = f32[2,8,1024]{2,1,0:T(8,128)S(1)} collective-permute-done((f32[2,8,1024]{2,1,0:T(8,128)S(1)}, f32[2,8,1024]{2,1,0:T(8,128)S(1)}, u32[]{:S(2)}, u32[]{:S(2)}) %collective-permute-start.24) | collective-permute-done | bytes 65568 | tf_op jit(solution)/shard_map/ppermute | solution.py:510
  100.8 6.0 %project.1 = f32[8,8192]{1,0:T(8,128)} custom-call(s32[4]{0:T(128)S(1)} %slice.170.label_ref, f32[4,8,1024]{2,1,0:T(8,128)S(1)} %get-tuple-element.64.image_ref, f32[8,1024]{1,0:T(8,128)S(1)} %get-tuple-element.77.first_ref, f32[8,1024]{1,0:T(8,128)S(1)} %get-tuple-element.76.last_ref, f32[4,1,1024]{2,1,0:T(1,128)S(1)} %get-tuple-element.38.mean_ref, ...), custom_call_target="tpu_custom_call" | custom-call | flops 4294967296 | bytes 16777216 | tf_op jit(solution)/shard_map/project/pallas_call | solution.py:410
  106.8 1.0 finish.1
  (66 shorter events, 10.7 us)
Async XLA Ops:
  0.6 22.5 %copy-start = (f32[8,1024]{1,0:T(8,128)S(1)}, f32[8,1024]{1,0:T(8,128)}, u32[]{:S(2)}) copy-start(f32[8,1024]{1,0:T(8,128)} %start_ref.7) | copy-start | bytes 98308
  21.6 1.5 %collective-permute-start = (f32[32,1024]{1,0:T(8,128)S(1)}, f32[32,1024]{1,0:T(8,128)S(1)}, u32[]{:S(2)}, u32[]{:S(2)}) collective-permute-start(f32[32,1024]{1,0:T(8,128)S(1)} %get-tuple-element.35.own_ref), channel_id=1, source_target_pairs={{0,1},{1,0},{2,3},{3,2},{4,5},{5,4},{6,7},{7,6},{8,9},{9,8},{10,11... | collective-permute-start | bytes 393224 | tf_op jit(solution)/shard_map/ppermute | solution.py:477
  23.2 5.5 %collective-permute-start.1 = (f32[16,1024]{1,0:T(8,128)S(1)}, f32[16,1024]{1,0:T(8,128)S(1)}, u32[]{:S(2)}, u32[]{:S(2)}) collective-permute-start(f32[16,1024]{1,0:T(8,128)S(1)} %get-tuple-element.39), channel_id=1, source_target_pairs={{0,2},{1,15},{2,0},{3,5},{4,6},{5,3},{6,4},{7,9},{8,10},{9,7},{10,... | collective-permute-start | bytes 196616 | tf_op jit(solution)/shard_map/ppermute | solution.py:479
  26.1 4.3 %collective-permute-start.2 = (f32[16,1024]{1,0:T(8,128)S(1)}, f32[16,1024]{1,0:T(8,128)S(1)}, u32[]{:S(2)}, u32[]{:S(2)}) collective-permute-start(f32[16,1024]{1,0:T(8,128)S(1)} %get-tuple-element.40), channel_id=1, source_target_pairs={{0,4},{1,13},{2,6},{3,15},{4,0},{5,9},{6,2},{7,11},{8,12},{9,5},{1... | collective-permute-start | bytes 196616 | tf_op jit(solution)/shard_map/ppermute | solution.py:479
  30.5 4.6 %collective-permute-start.3 = (f32[32,1024]{1,0:T(8,128)S(1)}, f32[32,1024]{1,0:T(8,128)S(1)}, u32[]{:S(2)}, u32[]{:S(2)}) collective-permute-start(f32[32,1024]{1,0:T(8,128)S(1)} %get-tuple-element.41.side_ref), channel_id=1, source_target_pairs={{0,1},{1,0},{2,3},{3,2},{4,5},{5,4},{6,7},{7,6},{8,9},{9,8},{10,11... | collective-permute-start | bytes 393224 | tf_op jit(solution)/shard_map/ppermute | solution.py:481
  38.6 1.3 %collective-permute-start.4 = (f32[16,1024]{1,0:T(8,128)S(1)}, f32[16,1024]{1,0:T(8,128)S(1)}, u32[]{:S(2)}, u32[]{:S(2)}) collective-permute-start(f32[16,1024]{1,0:T(8,128)S(1)} %get-tuple-element.45), channel_id=1, source_target_pairs={{0,1},{1,0},{2,3},{3,2},{4,5},{5,4},{6,7},{7,6},{8,9},{9,8},{10,11... | collective-permute-start | bytes 196616 | tf_op jit(solution)/shard_map/ppermute | solution.py:457
  40.0 4.0 %collective-permute-start.6 = (f32[8,1024]{1,0:T(8,128)S(1)}, f32[8,1024]{1,0:T(8,128)S(1)}, u32[]{:S(2)}, u32[]{:S(2)}) collective-permute-start(f32[8,1024]{1,0:T(8,128)S(1)} %get-tuple-element.84), channel_id=1, source_target_pairs={{0,4},{1,13},{2,6},{3,15},{4,0},{5,9},{6,2},{7,11},{8,12},{9,5},{1... | collective-permute-start | bytes 98312 | tf_op jit(solution)/shard_map/ppermute | solution.py:495
  40.0 4.0 %collective-permute-start.5 = (f32[8,1024]{1,0:T(8,128)S(1)}, f32[8,1024]{1,0:T(8,128)S(1)}, u32[]{:S(2)}, u32[]{:S(2)}) collective-permute-start(f32[8,1024]{1,0:T(8,128)S(1)} %get-tuple-element.85), channel_id=1, source_target_pairs={{0,2},{1,15},{2,0},{3,5},{4,6},{5,3},{6,4},{7,9},{8,10},{9,7},{10,... | collective-permute-start | bytes 98312 | tf_op jit(solution)/shard_map/ppermute | solution.py:495
  44.1 4.1 %collective-permute-start.7 = (f32[16,1024]{1,0:T(8,128)S(1)}, f32[16,1024]{1,0:T(8,128)S(1)}, u32[]{:S(2)}, u32[]{:S(2)}) collective-permute-start(f32[16,1024]{1,0:T(8,128)S(1)} %pad_maximum_fusion), channel_id=1, source_target_pairs={{0,1},{1,0},{2,3},{3,2},{4,5},{5,4},{6,7},{7,6},{8,9},{9,8},{10,11... | collective-permute-start | bytes 196616 | tf_op jit(solution)/shard_map/ppermute | solution.py:457
  51.4 1.3 %collective-permute-start.8 = (f32[16,1024]{1,0:T(8,128)S(1)}, f32[16,1024]{1,0:T(8,128)S(1)}, u32[]{:S(2)}, u32[]{:S(2)}) collective-permute-start(f32[16,1024]{1,0:T(8,128)S(1)} %get-tuple-element.50), channel_id=1, source_target_pairs={{0,1},{1,0},{2,3},{3,2},{4,5},{5,4},{6,7},{7,6},{8,9},{9,8},{10,11... | collective-permute-start | bytes 196616 | tf_op jit(solution)/shard_map/ppermute | solution.py:457
  52.8 4.1 %collective-permute-start.10 = (f32[8,1024]{1,0:T(8,128)S(1)}, f32[8,1024]{1,0:T(8,128)S(1)}, u32[]{:S(2)}, u32[]{:S(2)}) collective-permute-start(f32[8,1024]{1,0:T(8,128)S(1)} %get-tuple-element.82), channel_id=1, source_target_pairs={{0,4},{1,13},{2,6},{3,15},{4,0},{5,9},{6,2},{7,11},{8,12},{9,5},{1... | collective-permute-start | bytes 98312 | tf_op jit(solution)/shard_map/ppermute | solution.py:495
  52.9 4.0 %collective-permute-start.9 = (f32[8,1024]{1,0:T(8,128)S(1)}, f32[8,1024]{1,0:T(8,128)S(1)}, u32[]{:S(2)}, u32[]{:S(2)}) collective-permute-start(f32[8,1024]{1,0:T(8,128)S(1)} %get-tuple-element.83), channel_id=1, source_target_pairs={{0,2},{1,15},{2,0},{3,5},{4,6},{5,3},{6,4},{7,9},{8,10},{9,7},{10,... | collective-permute-start | bytes 98312 | tf_op jit(solution)/shard_map/ppermute | solution.py:495
  56.9 2.9 %collective-permute-start.11 = (f32[16,1024]{1,0:T(8,128)S(1)}, f32[16,1024]{1,0:T(8,128)S(1)}, u32[]{:S(2)}, u32[]{:S(2)}) collective-permute-start(f32[16,1024]{1,0:T(8,128)S(1)} %pad_maximum_fusion.1), channel_id=1, source_target_pairs={{0,1},{1,0},{2,3},{3,2},{4,5},{5,4},{6,7},{7,6},{8,9},{9,8},{10,11... | collective-permute-start | bytes 196616 | tf_op jit(solution)/shard_map/ppermute | solution.py:457
  59.8 24.7 %copy-start.1 = (s32[16]{0:T(128)S(1)}, s32[16]{0:T(128)}, u32[]{:S(2)}) copy-start(s32[16]{0:T(128)} %owner_ref.1) | copy-start | bytes 196
  63.1 1.3 %collective-permute-start.12 = (f32[16,1024]{1,0:T(8,128)S(1)}, f32[16,1024]{1,0:T(8,128)S(1)}, u32[]{:S(2)}, u32[]{:S(2)}) collective-permute-start(f32[16,1024]{1,0:T(8,128)S(1)} %get-tuple-element.54), channel_id=1, source_target_pairs={{0,1},{1,0},{2,3},{3,2},{4,5},{5,4},{6,7},{7,6},{8,9},{9,8},{10,11... | collective-permute-start | bytes 196616 | tf_op jit(solution)/shard_map/ppermute | solution.py:457
  64.4 4.0 %collective-permute-start.14 = (f32[8,1024]{1,0:T(8,128)S(1)}, f32[8,1024]{1,0:T(8,128)S(1)}, u32[]{:S(2)}, u32[]{:S(2)}) collective-permute-start(f32[8,1024]{1,0:T(8,128)S(1)} %get-tuple-element.80), channel_id=1, source_target_pairs={{0,4},{1,13},{2,6},{3,15},{4,0},{5,9},{6,2},{7,11},{8,12},{9,5},{1... | collective-permute-start | bytes 98312 | tf_op jit(solution)/shard_map/ppermute | solution.py:495
  64.8 3.9 %collective-permute-start.13 = (f32[8,1024]{1,0:T(8,128)S(1)}, f32[8,1024]{1,0:T(8,128)S(1)}, u32[]{:S(2)}, u32[]{:S(2)}) collective-permute-start(f32[8,1024]{1,0:T(8,128)S(1)} %get-tuple-element.81), channel_id=1, source_target_pairs={{0,2},{1,15},{2,0},{3,5},{4,6},{5,3},{6,4},{7,9},{8,10},{9,7},{10,... | collective-permute-start | bytes 98312 | tf_op jit(solution)/shard_map/ppermute | solution.py:495
  68.8 3.9 %collective-permute-start.15 = (f32[16,1024]{1,0:T(8,128)S(1)}, f32[16,1024]{1,0:T(8,128)S(1)}, u32[]{:S(2)}, u32[]{:S(2)}) collective-permute-start(f32[16,1024]{1,0:T(8,128)S(1)} %pad_maximum_fusion.2), channel_id=1, source_target_pairs={{0,1},{1,0},{2,3},{3,2},{4,5},{5,4},{6,7},{7,6},{8,9},{9,8},{10,11... | collective-permute-start | bytes 196616 | tf_op jit(solution)/shard_map/ppermute | solution.py:457
  76.1 1.3 %collective-permute-start.16 = (f32[16,1024]{1,0:T(8,128)S(1)}, f32[16,1024]{1,0:T(8,128)S(1)}, u32[]{:S(2)}, u32[]{:S(2)}) collective-permute-start(f32[16,1024]{1,0:T(8,128)S(1)} %get-tuple-element.58), channel_id=1, source_target_pairs={{0,1},{1,0},{2,3},{3,2},{4,5},{5,4},{6,7},{7,6},{8,9},{9,8},{10,11... | collective-permute-start | bytes 196616 | tf_op jit(solution)/shard_map/ppermute | solution.py:457
  77.4 4.1 %collective-permute-start.18 = (f32[8,1024]{1,0:T(8,128)S(1)}, f32[8,1024]{1,0:T(8,128)S(1)}, u32[]{:S(2)}, u32[]{:S(2)}) collective-permute-start(f32[8,1024]{1,0:T(8,128)S(1)} %get-tuple-element.78), channel_id=1, source_target_pairs={{0,4},{1,13},{2,6},{3,15},{4,0},{5,9},{6,2},{7,11},{8,12},{9,5},{1... | collective-permute-start | bytes 98312 | tf_op jit(solution)/shard_map/ppermute | solution.py:495
  77.5 4.1 %collective-permute-start.17 = (f32[8,1024]{1,0:T(8,128)S(1)}, f32[8,1024]{1,0:T(8,128)S(1)}, u32[]{:S(2)}, u32[]{:S(2)}) collective-permute-start(f32[8,1024]{1,0:T(8,128)S(1)} %get-tuple-element.79), channel_id=1, source_target_pairs={{0,2},{1,15},{2,0},{3,5},{4,6},{5,3},{6,4},{7,9},{8,10},{9,7},{10,... | collective-permute-start | bytes 98312 | tf_op jit(solution)/shard_map/ppermute | solution.py:495
  81.6 2.8 %collective-permute-start.19 = (f32[16,1024]{1,0:T(8,128)S(1)}, f32[16,1024]{1,0:T(8,128)S(1)}, u32[]{:S(2)}, u32[]{:S(2)}) collective-permute-start(f32[16,1024]{1,0:T(8,128)S(1)} %pad_maximum_fusion.3), channel_id=1, source_target_pairs={{0,1},{1,0},{2,3},{3,2},{4,5},{5,4},{6,7},{7,6},{8,9},{9,8},{10,11... | collective-permute-start | bytes 196616 | tf_op jit(solution)/shard_map/ppermute | solution.py:457
  87.8 1.7 %collective-permute-start.20 = (f32[80,1024]{1,0:T(8,128)S(1)}, f32[80,1024]{1,0:T(8,128)S(1)}, u32[]{:S(2)}, u32[]{:S(2)}) collective-permute-start(f32[80,1024]{1,0:T(8,128)S(1)} %get-tuple-element.62), channel_id=1, source_target_pairs={{0,1},{1,0},{2,3},{3,2},{4,5},{5,4},{6,7},{7,6},{8,9},{9,8},{10,11... | collective-permute-start | bytes 983048 | tf_op jit(solution)/shard_map/ppermute | solution.py:522
  89.6 6.2 %collective-permute-start.23 = (f32[4,8,1024]{2,1,0:T(8,128)S(1)}, f32[4,8,1024]{2,1,0:T(8,128)S(1)}, u32[]{:S(2)}, u32[]{:S(2)}) collective-permute-start(f32[4,8,1024]{2,1,0:T(8,128)S(1)} %slice_select_fusion), channel_id=1, source_target_pairs={{0,2},{1,3},{2,0},{3,1},{4,6},{5,7},{6,4},{7,5},{8,10},{9,11},{10,... | collective-permute-start | bytes 393224 | tf_op jit(solution)/shard_map/ppermute | solution.py:510
  89.7 4.0 %collective-permute-start.22 = (f32[8,1024]{1,0:T(8,128)S(1)}, f32[8,1024]{1,0:T(8,128)S(1)}, u32[]{:S(2)}, u32[]{:S(2)}) collective-permute-start(f32[8,1024]{1,0:T(8,128)S(1)} %get-tuple-element.74), channel_id=1, source_target_pairs={{0,4},{1,13},{2,6},{3,15},{4,0},{5,9},{6,2},{7,11},{8,12},{9,5},{1... | collective-permute-start | bytes 98312 | tf_op jit(solution)/shard_map/ppermute | solution.py:495
  90.1 5.6 %collective-permute-start.21 = (f32[8,1024]{1,0:T(8,128)S(1)}, f32[8,1024]{1,0:T(8,128)S(1)}, u32[]{:S(2)}, u32[]{:S(2)}) collective-permute-start(f32[8,1024]{1,0:T(8,128)S(1)} %get-tuple-element.75), channel_id=1, source_target_pairs={{0,2},{1,15},{2,0},{3,5},{4,6},{5,3},{6,4},{7,9},{8,10},{9,7},{10,... | collective-permute-start | bytes 98312 | tf_op jit(solution)/shard_map/ppermute | solution.py:495
  95.8 4.8 %collective-permute-start.24 = (f32[2,8,1024]{2,1,0:T(8,128)S(1)}, f32[2,8,1024]{2,1,0:T(8,128)S(1)}, u32[]{:S(2)}, u32[]{:S(2)}) collective-permute-start(f32[2,8,1024]{2,1,0:T(8,128)S(1)} %slice_select_fusion.1), channel_id=1, source_target_pairs={{0,4},{1,5},{2,6},{3,7},{4,0},{5,1},{6,2},{7,3},{8,12},{9,13},{10,... | collective-permute-start | bytes 196616 | tf_op jit(solution)/shard_map/ppermute | solution.py:510
  96.0 4.7 %collective-permute-start.26 = (f32[16,1024]{1,0:T(8,128)S(1)}, f32[16,1024]{1,0:T(8,128)S(1)}, u32[]{:S(2)}, u32[]{:S(2)}) collective-permute-start(f32[16,1024]{1,0:T(8,128)S(1)} %pad_maximum_fusion.4), channel_id=1, source_target_pairs={{0,1},{1,0},{2,3},{3,2},{4,5},{5,4},{6,7},{7,6},{8,9},{9,8},{10,11... | collective-permute-start | bytes 196616 | tf_op jit(solution)/shard_map/ppermute | solution.py:457
  100.7 6.2 %collective-permute-start.25 = (f32[1,8,1024]{2,1,0:T(8,128)S(1)}, f32[1,8,1024]{2,1,0:T(8,128)S(1)}, u32[]{:S(2)}, u32[]{:S(2)}) collective-permute-start(f32[1,8,1024]{2,1,0:T(8,128)S(1)} %get-tuple-element.94), channel_id=1, source_target_pairs={{0,8},{1,9},{2,10},{3,11},{4,12},{5,13},{6,14},{7,15},{8,0},{9,1},... | collective-permute-start | bytes 98312 | tf_op jit(solution)/shard_map/ppermute | solution.py:510
